TPU v7x, 32 devices: a whole 2x2x4 slice. The times are simulated.
32 devices in a mesh: dp: 8 (over z, x), tensor: 4 (over y, core).
Axes of the slice: x: 2, y: 2, z: 4, core: 2. Of those that a mesh axis runs over, the one named last changes fastest.
Arguments:
- latents: bfloat16 [16, 1024, 1408], P('dp', 'tensor'), may hold values from -6 to 6
- skip_input: bfloat16 [16, 1024, 1408], P('dp', 'tensor'), may hold values from -6 to 6
- text_states: bfloat16 [16, 333, 1024], P('dp'), may hold values from -6 to 6
- timesteps: int32 [16], P('dp'), may hold values from 0 to 999
- patch_order: int32 [1024], replicated, may hold values from 0 to 1023, each once
- out_grad: float32 [16, 1024, 1408], P('dp', 'tensor'), may hold values from -6 to 6
- head_inputs: float32 [1408, 4, 1408], P('dp', None, 'tensor'), may hold values from -0.15625 to 0.15625
- first_head_inputs: float32 [1408, 4, 1408], P('dp', None, 'tensor'), may hold values from -24 to 24
- second_head_inputs: float32 [1408, 4, 1408], P('dp', None, 'tensor'), may hold values from 163.84 to 655.36
- text_inputs: float32 [1024, 2, 1408], P('dp', None, 'tensor'), may hold values from -0.1875 to 0.1875
- first_text_inputs: float32 [1024, 2, 1408], P('dp', None, 'tensor'), may hold values from -24 to 24
- second_text_inputs: float32 [1024, 2, 1408], P('dp', None, 'tensor'), may hold values from 163.84 to 655.36
- head_outputs: float32 [2, 1408, 1408], P(None, 'tensor', 'dp'), may hold values from -1.25 to 1.25
- first_head_outputs: float32 [2, 1408, 1408], P(None, 'tensor', 'dp'), may hold values from -24 to 24
- second_head_outputs: float32 [2, 1408, 1408], P(None, 'tensor', 'dp'), may hold values from 2.56 to 10.24
- mlp_inner: float32 [1408, 6144], P('dp', 'tensor'), may hold values from -0.15625 to 0.15625
- first_mlp_inner: float32 [1408, 6144], P('dp', 'tensor'), may hold values from -24 to 24
- second_mlp_inner: float32 [1408, 6144], P('dp', 'tensor'), may hold values from 3.2768 to 13.1072
- mlp_outer: float32 [6144, 1408], P('tensor', 'dp'), may hold values from -0.078125 to 0.078125
- first_mlp_outer: float32 [6144, 1408], P('tensor', 'dp'), may hold values from -24 to 24
- second_mlp_outer: float32 [6144, 1408], P('tensor', 'dp'), may hold values from 10.24 to 40.96
- skip_linear: float32 [2816, 1408], P('dp'), may hold values from -0.109375 to 0.109375
- first_skip_linear: float32 [2816, 1408], P('dp'), may hold values from -24 to 24
- second_skip_linear: float32 [2816, 1408], P('dp'), may hold values from 163.84 to 655.36
- shift_linear: float32 [1408, 1408], P('dp'), may hold values from -0.15625 to 0.15625
- first_shift_linear: float32 [1408, 1408], P('dp'), may hold values from -24 to 24
- second_shift_linear: float32 [1408, 1408], P('dp'), may hold values from 163.84 to 655.36
- row_gains: float32 [5, 1408], replicated, may hold values from 0.5 to 1.5
- first_row_gains: float32 [5, 1408], replicated, may hold values from -24 to 24
- second_row_gains: float32 [5, 1408], replicated, may hold values from 163.84 to 655.36
- head_gains: float32 [4, 88], replicated, may hold values from 0.25 to 1.75
- first_head_gains: float32 [4, 88], replicated, may hold values from -96 to 96
- second_head_gains: float32 [4, 88], replicated, may hold values from 2621.44 to 10485.76
Outputs:
- block_out: float32 [16, 1024, 1408], P('dp', 'tensor')
- grad_latents: float32 [16, 1024, 1408], P('dp', 'tensor')
- grad_skip_input: float32 [16, 1024, 1408], P('dp', 'tensor')
- grad_head_inputs: float32 [1408, 4, 1408], P('dp', None, 'tensor')
- next_first_head_inputs: float32 [1408, 4, 1408], P('dp', None, 'tensor')
- next_second_head_inputs: float32 [1408, 4, 1408], P('dp', None, 'tensor')
- new_head_inputs: float32 [1408, 4, 1408], P('dp', None, 'tensor')
- grad_text_inputs: float32 [1024, 2, 1408], P('dp', None, 'tensor')
- next_first_text_inputs: float32 [1024, 2, 1408], P('dp', None, 'tensor')
- next_second_text_inputs: float32 [1024, 2, 1408], P('dp', None, 'tensor')
- new_text_inputs: float32 [1024, 2, 1408], P('dp', None, 'tensor')
- grad_head_outputs: float32 [2, 1408, 1408], P(None, 'tensor', 'dp')
- next_first_head_outputs: float32 [2, 1408, 1408], P(None, 'tensor', 'dp')
- next_second_head_outputs: float32 [2, 1408, 1408], P(None, 'tensor', 'dp')
- new_head_outputs: float32 [2, 1408, 1408], P(None, 'tensor', 'dp')
- grad_mlp_inner: float32 [1408, 6144], P('dp', 'tensor')
- next_first_mlp_inner: float32 [1408, 6144], P('dp', 'tensor')
- next_second_mlp_inner: float32 [1408, 6144], P('dp', 'tensor')
- new_mlp_inner: float32 [1408, 6144], P('dp', 'tensor')
- grad_mlp_outer: float32 [6144, 1408], P('tensor', 'dp')
- next_first_mlp_outer: float32 [6144, 1408], P('tensor', 'dp')
- next_second_mlp_outer: float32 [6144, 1408], P('tensor', 'dp')
- new_mlp_outer: float32 [6144, 1408], P('tensor', 'dp')
- grad_skip_linear: float32 [2816, 1408], P('dp')
- next_first_skip_linear: float32 [2816, 1408], P('dp')
- next_second_skip_linear: float32 [2816, 1408], P('dp')
- new_skip_linear: float32 [2816, 1408], P('dp')
- grad_shift_linear: float32 [1408, 1408], P('dp')
- next_first_shift_linear: float32 [1408, 1408], P('dp')
- next_second_shift_linear: float32 [1408, 1408], P('dp')
- new_shift_linear: float32 [1408, 1408], P('dp')
- grad_row_gains: float32 [5, 1408], replicated
- next_first_row_gains: float32 [5, 1408], replicated
- next_second_row_gains: float32 [5, 1408], replicated
- new_row_gains: float32 [5, 1408], replicated
- grad_head_gains: float32 [4, 88], replicated
- next_first_head_gains: float32 [4, 88], replicated
- next_second_head_gains: float32 [4, 88], replicated
- new_head_gains: float32 [4, 88], replicated
- weight_norms: float32 [12], replicated
- ratio_norms: float32 [12], replicated
Inputs may be any that keep to these rules, and one draw needn't show every extreme that they name: `patch_order`: each of the 1024 grid cells once; cell c lies at row c // 32, column c % 32.
All inputs are finite; a program needn't handle non-finite values.
Results may differ from a plain program's by a relative error of at most 0.018.
Values may be sent and summed in bfloat16 or wider, within the bound.
No kernel may reach another device: no remote copies, remote signals or barrier semaphores. Data moves between devices by JAX's collectives and lax.ppermute only.
A program may use at most 320 MiB of HBM per device.

v0:
```python
from functools import partial
import math

import jax
import jax.numpy as jnp
from jax import lax
from jax.sharding import PartitionSpec as P

D = 1408
HD = 88
GRID = 32


norm_eps = 1e-06
beta_one = 0.9
beta_two = 0.999
adam_eps = 1e-06
decay_rate = 0.01
learn_rate = 0.3
step_count = 10.0


def matmul(left, right):
    return jnp.dot(left, right, preferred_element_type=jnp.float32)


def matmul_tn(left, right):
    return lax.dot_general(
        left, right, (((0,), (0,)), ((), ())), preferred_element_type=jnp.float32
    )


def matmul_nt(left, right):
    return lax.dot_general(
        left, right, (((1,), (1,)), ((), ())), preferred_element_type=jnp.float32
    )


def norm_rows(values, factor):
    center = values - jnp.mean(values, axis=-1, keepdims=True)
    spread = jnp.mean(center * center, axis=-1, keepdims=True)
    return center * lax.rsqrt(spread + norm_eps) * factor


def rotate_pairs(values, cosines, sines):
    layout = values.shape
    paired = values.reshape(layout[:-1] + (layout[-1] // 2, 2))
    turned = jnp.stack([-paired[..., 1], paired[..., 0]], -1).reshape(layout)
    return values * cosines + turned * sines


def rotary_tables(patch_order):
    grid_row = (patch_order // GRID).astype(jnp.float32)
    grid_col = (patch_order % GRID).astype(jnp.float32)
    quarter = HD // 4
    spacing = 10000.0 ** (-jnp.arange(quarter).astype(jnp.float32) / quarter)
    row_angle = jnp.repeat(grid_row[:, None] * spacing[None, :], 2, axis=1)
    col_angle = jnp.repeat(grid_col[:, None] * spacing[None, :], 2, axis=1)
    angles = jnp.concatenate([row_angle, col_angle], 1)
    return (jnp.cos(angles)[:, None, :], jnp.sin(angles)[:, None, :])


def time_embed(timesteps):
    half_width = D // 2
    spacing = jnp.exp(-math.log(10000.0) * jnp.arange(half_width).astype(jnp.float32) / half_width)
    angles = timesteps.astype(jnp.float32)[:, None] * spacing[None, :]
    return jnp.concatenate([jnp.cos(angles), jnp.sin(angles)], -1)


def rope_heads(pre, factor, cosines, sines):
    return rotate_pairs(norm_rows(pre.reshape(pre.shape[0], -1, HD), factor), cosines, sines)


def plain_heads(pre, factor):
    return norm_rows(pre.reshape(pre.shape[0], -1, HD), factor)


def gelu_tanh(values):
    return jax.nn.gelu(values, approximate=True)


def attend(query, keys, values):
    factor = HD ** (-0.5)
    scores = jnp.einsum("qhd,khd->hqk", query, keys, preferred_element_type=jnp.float32) * factor
    highest = jnp.max(scores, axis=-1, keepdims=True)
    raised = jnp.exp(scores - highest)
    summed = jnp.sum(raised, axis=-1, keepdims=True)
    chances = raised / summed
    log_total = highest + jnp.log(summed)
    mixed = jnp.einsum(
        "hqk,khd->qhd", chances.astype(jnp.bfloat16), values, preferred_element_type=jnp.float32
    )
    return (mixed.astype(jnp.bfloat16), log_total)


def attend_back(query, keys, values, log_total, mixed_grad):
    factor = HD ** (-0.5)
    scores = jnp.einsum("qhd,khd->hqk", query, keys, preferred_element_type=jnp.float32) * factor
    chances = jnp.exp(scores - log_total)
    chance_grad = jnp.einsum("qhd,khd->hqk", mixed_grad, values, preferred_element_type=jnp.float32)
    centre = jnp.sum(chance_grad * chances, axis=-1, keepdims=True)
    score_grad = (chances * (chance_grad - centre)).astype(jnp.bfloat16)
    query_grad = (
        jnp.einsum("hqk,khd->qhd", score_grad, keys, preferred_element_type=jnp.float32) * factor
    )
    keys_grad = (
        jnp.einsum("hqk,qhd->khd", score_grad, query, preferred_element_type=jnp.float32) * factor
    )
    values_grad = jnp.einsum(
        "hqk,qhd->khd", chances.astype(jnp.bfloat16), mixed_grad, preferred_element_type=jnp.float32
    )
    return (query_grad, keys_grad, values_grad)


def project(local_rows, matrix):
    gathered = lax.all_gather(local_rows, "tensor", axis=0, tiled=True)
    return (gathered, matmul(gathered, matrix))


def weight_grad(kept_rows, grad):
    return matmul_tn(kept_rows, grad)


def rows_times(left, right):
    return matmul(left, right)


def rows_times_t(left, right):
    return matmul_nt(left, right)


def sum_tokens(left, right):
    return lax.psum_scatter(rows_times(left, right), "tensor", scatter_dimension=0, tiled=True)


def sum_grads(left, right):
    return lax.psum_scatter(rows_times_t(left, right), "tensor", scatter_dimension=0, tiled=True)


def gather_grads(local_rows):
    return lax.all_gather(local_rows, "tensor", axis=0, tiled=True)


def fetch_weights(head_mats, text_mats, out_mats, inner_mat, outer_mat, skip_mat, shift_mat):
    return tuple(
        (
            lax.all_gather(head_mats, "dp", axis=0, tiled=True),
            lax.all_gather(text_mats, "dp", axis=0, tiled=True),
            lax.all_gather(out_mats, "dp", axis=2, tiled=True),
            lax.all_gather(inner_mat, "dp", axis=0, tiled=True),
            lax.all_gather(outer_mat, "dp", axis=1, tiled=True),
            lax.all_gather(skip_mat, "dp", axis=0, tiled=True),
            lax.all_gather(shift_mat, "dp", axis=0, tiled=True),
        )
    )


def lamb_parts(master, first, second, grad):
    next_first = beta_one * first + (1.0 - beta_one) * grad
    next_second = beta_two * second + (1.0 - beta_two) * grad * grad
    ratio = (
        next_first
        / (1.0 - beta_one**step_count)
        / (jnp.sqrt(next_second / (1.0 - beta_two**step_count)) + adam_eps)
        + decay_rate * master
    )
    return (next_first, next_second, ratio)


def group_squares(values, axes):
    return jnp.sum(values * values, axis=axes).reshape(-1)


def row_renew(master, ratio):
    weight_norm = jnp.sqrt(jnp.sum(master * master, axis=1, keepdims=True))
    ratio_norm = jnp.sqrt(jnp.sum(ratio * ratio, axis=1, keepdims=True))
    return master - learn_rate * (weight_norm / ratio_norm) * ratio


def body(
    latents,
    skip_input,
    text_states,
    timesteps,
    patch_order,
    out_grad,
    head_inputs,
    first_head_inputs,
    second_head_inputs,
    text_inputs,
    first_text_inputs,
    second_text_inputs,
    head_outputs,
    first_head_outputs,
    second_head_outputs,
    mlp_inner,
    first_mlp_inner,
    second_mlp_inner,
    mlp_outer,
    first_mlp_outer,
    second_mlp_outer,
    skip_linear,
    first_skip_linear,
    second_skip_linear,
    shift_linear,
    first_shift_linear,
    second_shift_linear,
    row_gains,
    first_row_gains,
    second_row_gains,
    head_gains,
    first_head_gains,
    second_head_gains,
):
    cosines, sines = rotary_tables(patch_order)
    conditions = time_embed(timesteps)
    dp_count = lax.axis_size("dp")
    width = latents.shape[2]
    head_cols = head_inputs.shape[2]
    text_width = text_inputs.shape[0] * dp_count
    hidden_cols = mlp_inner.shape[1]
    low_head = head_inputs.astype(jnp.bfloat16)
    low_text = text_inputs.astype(jnp.bfloat16)
    low_out = head_outputs.astype(jnp.bfloat16)
    low_inner = mlp_inner.astype(jnp.bfloat16)
    low_outer = mlp_outer.astype(jnp.bfloat16)
    low_skip = skip_linear.astype(jnp.bfloat16)
    low_shift = shift_linear.astype(jnp.bfloat16)
    fetched = fetch_weights(low_head, low_text, low_out, low_inner, low_outer, low_skip, low_shift)

    def micro_step(totals, items):
        latent, skip_part, text_part, cond, shift_row, cotangent = items
        head_mats, text_mats, out_mats, inner_mat, outer_mat, skip_mat, shift_mat = fetched
        local_rows = latent.shape[0]
        total_rows = local_rows * lax.axis_size("tensor")
        text_rows = text_part.shape[0]
        joined = jnp.concatenate([latent, skip_part], -1).astype(jnp.float32)
        skip_gain = row_gains[0:2].reshape(-1)
        normed, normed_back = jax.vjp(norm_rows, joined, skip_gain)
        normed16 = normed.astype(jnp.bfloat16)
        hidden = matmul(normed16, skip_mat)
        silu16 = jax.nn.silu(cond).astype(jnp.bfloat16)
        shift = matmul(silu16[None, :], shift_mat)
        first_norm, first_back = jax.vjp(norm_rows, hidden, row_gains[2])
        attn16 = (first_norm + shift).astype(jnp.bfloat16)
        self_cols = head_mats[:, 0:3, :].reshape(width, 3 * head_cols)
        attn_kept, self_pre = project(attn16, self_cols)
        query, query_back = jax.vjp(
            partial(rope_heads, cosines=cosines, sines=sines),
            self_pre[:, :head_cols],
            head_gains[0],
        )
        keys, keys_back = jax.vjp(
            partial(rope_heads, cosines=cosines, sines=sines),
            self_pre[:, head_cols : 2 * head_cols],
            head_gains[1],
        )
        query16 = query.astype(jnp.bfloat16)
        keys16 = keys.astype(jnp.bfloat16)
        values16 = self_pre[:, 2 * head_cols :].reshape(total_rows, -1, HD).astype(jnp.bfloat16)
        self_out16, self_lse = attend(query16, keys16, values16)
        self_flat = self_out16.reshape(total_rows, head_cols)
        after_self = hidden + sum_tokens(self_flat, out_mats[0])
        third_norm, third_back = jax.vjp(norm_rows, after_self, row_gains[3])
        cross16 = third_norm.astype(jnp.bfloat16)
        cross_mat = head_mats[:, 3, :]
        cross_kept, cross_pre = project(cross16, cross_mat)
        cross_query, cross_query_back = jax.vjp(
            partial(rope_heads, cosines=cosines, sines=sines), cross_pre, head_gains[2]
        )
        text_pre = matmul(text_part, text_mats.reshape(text_width, 2 * head_cols))
        text_keys, text_keys_back = jax.vjp(plain_heads, text_pre[:, :head_cols], head_gains[3])
        cross_query16 = cross_query.astype(jnp.bfloat16)
        text_keys16 = text_keys.astype(jnp.bfloat16)
        text_values16 = text_pre[:, head_cols:].reshape(text_rows, -1, HD).astype(jnp.bfloat16)
        cross_out16, cross_lse = attend(cross_query16, text_keys16, text_values16)
        cross_flat = cross_out16.reshape(total_rows, head_cols)
        after_cross = after_self + sum_tokens(cross_flat, out_mats[1])
        second_norm, second_back = jax.vjp(norm_rows, after_cross, row_gains[4])
        mlp16 = second_norm.astype(jnp.bfloat16)
        mlp_kept, inner = project(mlp16, inner_mat)
        activated, gelu_back = jax.vjp(gelu_tanh, inner)
        activated16 = activated.astype(jnp.bfloat16)
        block_out = after_cross + sum_tokens(activated16, outer_mat)
        mlp_full_grad = gather_grads(cotangent.astype(jnp.bfloat16))
        outer_grad = matmul_tn(activated16, mlp_full_grad)
        (inner_grad,) = gelu_back(matmul_nt(mlp_full_grad, outer_mat))
        inner_grad16 = inner_grad.astype(jnp.bfloat16)
        inner_wgrad = weight_grad(mlp_kept, inner_grad16)
        mlp_in_grad = sum_grads(inner_grad16, inner_mat)
        cross_res_grad, fifth_gain_grad = second_back(mlp_in_grad)
        after_cross_grad = cotangent + cross_res_grad
        cross_full_grad = gather_grads(after_cross_grad.astype(jnp.bfloat16))
        cross_out_wgrad = matmul_tn(cross_flat, cross_full_grad)
        cross_mixed_grad = (
            matmul_nt(cross_full_grad, out_mats[1]).astype(jnp.bfloat16).reshape(total_rows, -1, HD)
        )
        cq_grad, ck_grad, cv_grad = attend_back(
            cross_query16, text_keys16, text_values16, cross_lse, cross_mixed_grad
        )
        cq_pre_grad, cq_gain_grad = cross_query_back(cq_grad)
        ck_pre_grad, ck_gain_grad = text_keys_back(ck_grad)
        text_grad16 = jnp.concatenate(
            [ck_pre_grad, cv_grad.reshape(text_rows, head_cols)], 1
        ).astype(jnp.bfloat16)
        text_wgrad = matmul_tn(text_part, text_grad16).reshape(text_width, 2, head_cols)
        cq_pre16 = cq_pre_grad.astype(jnp.bfloat16)
        cross_q_wgrad = weight_grad(cross_kept, cq_pre16)
        cross_in_grad = sum_grads(cq_pre16, cross_mat)
        self_res_grad, fourth_gain_grad = third_back(cross_in_grad)
        after_self_grad = after_cross_grad + self_res_grad
        self_full_grad = gather_grads(after_self_grad.astype(jnp.bfloat16))
        self_out_wgrad = matmul_tn(self_flat, self_full_grad)
        self_mixed_grad = (
            matmul_nt(self_full_grad, out_mats[0]).astype(jnp.bfloat16).reshape(total_rows, -1, HD)
        )
        sq_grad, sk_grad, sv_grad = attend_back(
            query16, keys16, values16, self_lse, self_mixed_grad
        )
        sq_pre_grad, sq_gain_grad = query_back(sq_grad)
        sk_pre_grad, sk_gain_grad = keys_back(sk_grad)
        self_pre16 = jnp.concatenate(
            [sq_pre_grad, sk_pre_grad, sv_grad.reshape(total_rows, head_cols)], 1
        ).astype(jnp.bfloat16)
        self_wgrad = weight_grad(attn_kept, self_pre16).reshape(width, 3, head_cols)
        attn_grad = sum_grads(self_pre16, self_cols)
        hidden_norm_grad, third_gain_grad = first_back(attn_grad)
        shift_grad = jnp.sum(attn_grad, axis=0)
        hidden_grad16 = (after_self_grad + hidden_norm_grad).astype(jnp.bfloat16)
        skip_wgrad = matmul_tn(normed16, hidden_grad16)
        joined_grad, skip_gain_grad = normed_back(matmul_nt(hidden_grad16, skip_mat))
        row_grad = jnp.stack(
            [
                skip_gain_grad[:width],
                skip_gain_grad[width:],
                third_gain_grad,
                fourth_gain_grad,
                fifth_gain_grad,
            ]
        )
        head_grad = jnp.stack([sq_gain_grad, sk_gain_grad, cq_gain_grad, ck_gain_grad])
        head_in_wgrad = jnp.concatenate([self_wgrad, cross_q_wgrad[:, None, :]], 1)
        out_wgrad = jnp.stack([self_out_wgrad, cross_out_wgrad])
        increments = (head_in_wgrad, text_wgrad, out_wgrad, inner_wgrad, outer_grad, skip_wgrad)
        increments = increments + (silu16.astype(jnp.float32)[:, None] * shift_grad[None, :],)
        increments = increments + (row_grad, head_grad)
        totals = tuple((left + right for left, right in zip(totals, increments)))
        return (totals, (block_out, joined_grad[:, :width], joined_grad[:, width:], shift_grad))

    zero_totals = (
        jnp.zeros((width, 4, head_cols), jnp.float32),
        jnp.zeros((text_width, 2, head_cols), jnp.float32),
        jnp.zeros((2, head_cols, width), jnp.float32),
        jnp.zeros((width, hidden_cols), jnp.float32),
        jnp.zeros((hidden_cols, width), jnp.float32),
        jnp.zeros((2 * width, width), jnp.float32),
    )
    zero_totals = zero_totals + (jnp.zeros((width, width), jnp.float32),)
    zero_totals = zero_totals + (
        jnp.zeros((5, width), jnp.float32),
        jnp.zeros((4, HD), jnp.float32),
    )
    totals, (block_out, grad_latents, grad_skip_input, shift_grads) = lax.scan(
        micro_step,
        zero_totals,
        (latents, skip_input, text_states, conditions, conditions, out_grad),
    )
    row_sum = totals[-2]
    head_sum = totals[-1]
    head_in_grad, text_in_grad, head_out_grad, mlp_in_grad, mlp_out_grad, skip_part, shift_part = (
        lax.psum_scatter(totals[0], "dp", scatter_dimension=0, tiled=True),
        lax.psum_scatter(totals[1], "dp", scatter_dimension=0, tiled=True),
        lax.psum_scatter(totals[2], "dp", scatter_dimension=2, tiled=True),
        lax.psum_scatter(totals[3], "dp", scatter_dimension=0, tiled=True),
        lax.psum_scatter(totals[4], "dp", scatter_dimension=1, tiled=True),
        lax.psum_scatter(totals[5], "dp", scatter_dimension=0, tiled=True),
        lax.psum_scatter(totals[6], "dp", scatter_dimension=0, tiled=True),
    )
    skip_mat_grad, shift_mat_grad = lax.psum((skip_part, shift_part), "tensor")
    head_in_first, head_in_second, head_in_ratio = lamb_parts(
        head_inputs, first_head_inputs, second_head_inputs, head_in_grad
    )
    text_in_first, text_in_second, text_in_ratio = lamb_parts(
        text_inputs, first_text_inputs, second_text_inputs, text_in_grad
    )
    head_out_first, head_out_second, head_out_ratio = lamb_parts(
        head_outputs, first_head_outputs, second_head_outputs, head_out_grad
    )
    mlp_in_first, mlp_in_second, mlp_in_ratio = lamb_parts(
        mlp_inner, first_mlp_inner, second_mlp_inner, mlp_in_grad
    )
    mlp_out_first, mlp_out_second, mlp_out_ratio = lamb_parts(
        mlp_outer, first_mlp_outer, second_mlp_outer, mlp_out_grad
    )
    skip_mat_first, skip_mat_second, skip_mat_ratio = lamb_parts(
        skip_linear, first_skip_linear, second_skip_linear, skip_mat_grad
    )
    shift_mat_first, shift_mat_second, shift_mat_ratio = lamb_parts(
        shift_linear, first_shift_linear, second_shift_linear, shift_mat_grad
    )
    weight_squares = jnp.concatenate(
        [
            group_squares(head_inputs, (0, 2)),
            group_squares(text_inputs, (0, 2)),
            group_squares(head_outputs, (1, 2)),
            group_squares(mlp_inner, (0, 1)),
            group_squares(mlp_outer, (0, 1)),
            group_squares(skip_linear, (0, 1)),
            group_squares(shift_linear, (0, 1)),
        ]
    )
    ratio_squares = jnp.concatenate(
        [
            group_squares(head_in_ratio, (0, 2)),
            group_squares(text_in_ratio, (0, 2)),
            group_squares(head_out_ratio, (1, 2)),
            group_squares(mlp_in_ratio, (0, 1)),
            group_squares(mlp_out_ratio, (0, 1)),
            group_squares(skip_mat_ratio, (0, 1)),
            group_squares(shift_mat_ratio, (0, 1)),
        ]
    )
    weight_squares, ratio_squares, row_gain_grad, head_gain_grad = lax.psum(
        (weight_squares, ratio_squares, row_sum, head_sum), ("dp", "tensor")
    )
    correction = jnp.concatenate(
        [jnp.ones((10,), jnp.float32), jnp.full((2,), 1.0 / lax.axis_size("tensor"), jnp.float32)]
    )
    weight_norms = jnp.sqrt(weight_squares * correction)
    ratio_norms = jnp.sqrt(ratio_squares * correction)
    trust = weight_norms / ratio_norms
    head_in_new = head_inputs - learn_rate * trust[0:4][None, :, None] * head_in_ratio
    text_in_new = text_inputs - learn_rate * trust[4:6][None, :, None] * text_in_ratio
    head_out_new = head_outputs - learn_rate * trust[6:8][:, None, None] * head_out_ratio
    mlp_in_new = mlp_inner - learn_rate * trust[8] * mlp_in_ratio
    mlp_out_new = mlp_outer - learn_rate * trust[9] * mlp_out_ratio
    skip_mat_new = skip_linear - learn_rate * trust[10] * skip_mat_ratio
    shift_mat_new = shift_linear - learn_rate * trust[11] * shift_mat_ratio
    row_gain_first, row_gain_second, row_gain_ratio = lamb_parts(
        row_gains, first_row_gains, second_row_gains, row_gain_grad
    )
    head_gain_first, head_gain_second, head_gain_ratio = lamb_parts(
        head_gains, first_head_gains, second_head_gains, head_gain_grad
    )
    row_gain_new = row_renew(row_gains, row_gain_ratio)
    head_gain_new = row_renew(head_gains, head_gain_ratio)
    return (
        block_out,
        grad_latents,
        grad_skip_input,
        head_in_grad,
        head_in_first,
        head_in_second,
        head_in_new,
        text_in_grad,
        text_in_first,
        text_in_second,
        text_in_new,
        head_out_grad,
        head_out_first,
        head_out_second,
        head_out_new,
        mlp_in_grad,
        mlp_in_first,
        mlp_in_second,
        mlp_in_new,
        mlp_out_grad,
        mlp_out_first,
        mlp_out_second,
        mlp_out_new,
        skip_mat_grad,
        skip_mat_first,
        skip_mat_second,
        skip_mat_new,
        shift_mat_grad,
        shift_mat_first,
        shift_mat_second,
        shift_mat_new,
        row_gain_grad,
        row_gain_first,
        row_gain_second,
        row_gain_new,
        head_gain_grad,
        head_gain_first,
        head_gain_second,
        head_gain_new,
        weight_norms,
        ratio_norms,
    )


def solution(mesh):
    return jax.shard_map(
        body,
        mesh=mesh,
        in_specs=(
            P("dp", "tensor", None),
            P("dp", "tensor", None),
            P("dp", None, None),
            P("dp"),
            P(),
            P("dp", "tensor", None),
            P("dp", None, "tensor"),
            P("dp", None, "tensor"),
            P("dp", None, "tensor"),
            P("dp", None, "tensor"),
            P("dp", None, "tensor"),
            P("dp", None, "tensor"),
            P(None, "tensor", "dp"),
            P(None, "tensor", "dp"),
            P(None, "tensor", "dp"),
            P("dp", "tensor"),
            P("dp", "tensor"),
            P("dp", "tensor"),
            P("tensor", "dp"),
            P("tensor", "dp"),
            P("tensor", "dp"),
            P("dp", None),
            P("dp", None),
            P("dp", None),
            P("dp", None),
            P("dp", None),
            P("dp", None),
            P(),
            P(),
            P(),
            P(),
            P(),
            P(),
        ),
        out_specs=(
            P("dp", "tensor", None),
            P("dp", "tensor", None),
            P("dp", "tensor", None),
            P("dp", None, "tensor"),
            P("dp", None, "tensor"),
            P("dp", None, "tensor"),
            P("dp", None, "tensor"),
            P("dp", None, "tensor"),
            P("dp", None, "tensor"),
            P("dp", None, "tensor"),
            P("dp", None, "tensor"),
            P(None, "tensor", "dp"),
            P(None, "tensor", "dp"),
            P(None, "tensor", "dp"),
            P(None, "tensor", "dp"),
            P("dp", "tensor"),
            P("dp", "tensor"),
            P("dp", "tensor"),
            P("dp", "tensor"),
            P("tensor", "dp"),
            P("tensor", "dp"),
            P("tensor", "dp"),
            P("tensor", "dp"),
            P("dp", None),
            P("dp", None),
            P("dp", None),
            P("dp", None),
            P("dp", None),
            P("dp", None),
            P("dp", None),
            P("dp", None),
            P(),
            P(),
            P(),
            P(),
            P(),
            P(),
            P(),
            P(),
            P(),
            P(),
        ),
        check_vma=False,
    )
```

profile of v0, /device:TPU:0, one launch (start us, length us, event | category | flops | bytes accessed | tf_op | source)
XLA Modules:
  0.0 3316.5 jit_solution(8359241189672621077)
XLA Ops:
  22.0 41.6 %all-gather.22.cloned.1.call-done = bf16[2,352,1408]{1,0,2:T(2,128)(2,1)} async-done(((bf16[2,352,176]{1,0,2:T(2,128)(2,1)}), bf16[2,352,1408]{1,0,2:T(2,128)(2,1)}) %all-gather.22.cloned.1.call-update) | async-done | bytes 1982480 | tf_op jit(solution)/shard_map/all_gather | solution.py:149
  70.2 69.6 %all-gather.18.cloned.1.call-done = bf16[1408,4,352]{2,1,0:T(4,128)(2,1)} async-done(((bf16[176,4,352]{2,1,0:T(4,128)(2,1)}), bf16[1408,4,352]{2,1,0:T(4,128)(2,1)}) %all-gather.18.cloned.1.call-update) | async-done | bytes 3964944 | tf_op jit(solution)/shard_map/all_gather | solution.py:147
  139.8 8.1 copy.111
  147.9 68.0 %all-gather.20.cloned.1.call-done = bf16[1536,1408]{0,1:T(8,128)(2,1)} async-done(((bf16[1536,176]{0,1:T(8,128)(2,1)}), bf16[1536,1408]{0,1:T(8,128)(2,1)}) %all-gather.20.cloned.1.call-update) | async-done | bytes 4325392 | tf_op jit(solution)/shard_map/all_gather | solution.py:151
  222.3 38.1 %all-gather.24.cloned.1.call-done = bf16[1024,2,352]{0,2,1:T(8,128)(2,1)} async-done(((bf16[128,2,352]{0,2,1:T(8,128)(2,1)}), bf16[1024,2,352]{0,2,1:T(8,128)(2,1)}) %all-gather.24.cloned.1.call-update) | async-done | bytes 1441808 | tf_op jit(solution)/shard_map/all_gather | solution.py:148
  260.4 71.5 %all-gather.16.cloned.1.call-done = bf16[1408,1408]{1,0:T(8,128)(2,1)} async-done(((bf16[176,1408]{1,0:T(8,128)(2,1)}), bf16[1408,1408]{1,0:T(8,128)(2,1)}) %all-gather.16.cloned.1.call-update) | async-done | bytes 3964944 | tf_op jit(solution)/shard_map/all_gather | solution.py:153
  331.9 76.0 %all-gather.26.cloned.1.call-done = bf16[1408,1536]{1,0:T(8,128)(2,1)} async-done(((bf16[176,1536]{1,0:T(8,128)(2,1)}), bf16[1408,1536]{1,0:T(8,128)(2,1)}) %all-gather.26.cloned.1.call-update) | async-done | bytes 4325392 | tf_op jit(solution)/shard_map/all_gather | solution.py:150
  408.0 120.2 %all-gather.14.cloned.1.call-done = bf16[2816,1408]{1,0:T(8,128)(2,1)} async-done(((bf16[352,1408]{1,0:T(8,128)(2,1)}), bf16[2816,1408]{1,0:T(8,128)(2,1)}) %all-gather.14.cloned.1.call-update) | async-done | bytes 7929872 | tf_op jit(solution)/shard_map/all_gather | solution.py:152
  528.2 1451.9 %while.35 = (s32[]{:T(128)}, f32[1408,4,352]{0,2,1:T(8,128)}, f32[1024,2,352]{0,2,1:T(8,128)}, f32[2,352,1408]{2,1,0:T(8,128)}, f32[1408,1536]{1,0:T(8,128)}, /*...) while((s32[]{:T(128)}, f32[1408,4,352]{0,2,1:T(8,128)}, ...), condition=%wide.region_54.55_spmd.clone, body=%wide.region_0.54_spmd.clone.sunk | while | flops 58117910528 | bytes 1525128832 | solution.py:363
  545.3 20.2 all-gather.28.cloned.1.call-done
  598.4 8.2 multiply_reduce_fusion.63
  606.6 8.6 fusion.368
  628.4 55.0 %reduce-scatter.25.cloned.1.call-done = f32[256,1408]{1,0:T(8,128)} async-done(((f32[1024,1408]{1,0:T(8,128)}), f32[256,1408]{1,0:T(8,128)}) %reduce-scatter.25.cloned.1.call-update) | async-done | bytes 1441808 | tf_op jit(solution)/shard_map/while/body/eval_jaxpr/reduce_scatter | solution.py:133
  692.4 21.2 all-gather.30.cloned.1.call-done
  745.2 52.6 %reduce-scatter.27.cloned.1.call-done = f32[256,1408]{1,0:T(8,128)} async-done(((f32[1024,1408]{1,0:T(8,128)}), f32[256,1408]{1,0:T(8,128)}) %reduce-scatter.27.cloned.1.call-update) | async-done | bytes 1441808 | tf_op jit(solution)/shard_map/while/body/eval_jaxpr/reduce_scatter | solution.py:133
  801.7 25.2 all-gather.32.cloned.1.call-done
  826.9 9.8 fusion.378
  836.7 19.4 all-gather.34.cloned.1.call-done
  856.1 13.2 fusion.383
  870.9 9.1 fusion.384
  880.1 55.0 %reduce-scatter.29.cloned.1.call-done = f32[256,1408]{1,0:T(8,128)} async-done(((f32[1024,1408]{1,0:T(8,128)}), f32[256,1408]{1,0:T(8,128)}) %reduce-scatter.29.cloned.1.call-update) | async-done | bytes 1441808 | tf_op jit(solution)/shard_map/while/body/eval_jaxpr/reduce_scatter | solution.py:137
  943.1 25.2 all-gather.36.cloned.1.call-done
  999.8 55.0 %reduce-scatter.31.cloned.1.call-done = f32[256,1408]{1,0:T(8,128)} async-done(((f32[1024,1408]{1,0:T(8,128)}), f32[256,1408]{1,0:T(8,128)}) %reduce-scatter.31.cloned.1.call-update) | async-done | bytes 1441808 | tf_op jit(solution)/shard_map/while/body/eval_jaxpr/reduce_scatter | solution.py:137
  1060.1 10.3 fusion.403
  1071.1 16.1 all-gather.38.cloned.1.call-done
  1090.7 16.5 multiply_reduce_fusion.74
  1109.5 8.6 multiply_convert_fusion.22
  1146.8 9.1 fusion.391
  1164.7 9.4 convolution_add_fusion.4
  1174.1 13.0 convolution_add_fusion.5
  1261.5 22.1 all-gather.28.cloned.1.call-done
  1316.2 8.2 multiply_reduce_fusion.63
  1324.4 8.6 fusion.368
  1333.0 8.3 fusion.369
  1346.5 55.0 %reduce-scatter.25.cloned.1.call-done = f32[256,1408]{1,0:T(8,128)} async-done(((f32[1024,1408]{1,0:T(8,128)}), f32[256,1408]{1,0:T(8,128)}) %reduce-scatter.25.cloned.1.call-update) | async-done | bytes 1441808 | tf_op jit(solution)/shard_map/while/body/eval_jaxpr/reduce_scatter | solution.py:133
  1410.5 21.2 all-gather.30.cloned.1.call-done
  1463.3 52.6 %reduce-scatter.27.cloned.1.call-done = f32[256,1408]{1,0:T(8,128)} async-done(((f32[1024,1408]{1,0:T(8,128)}), f32[256,1408]{1,0:T(8,128)}) %reduce-scatter.27.cloned.1.call-update) | async-done | bytes 1441808 | tf_op jit(solution)/shard_map/while/body/eval_jaxpr/reduce_scatter | solution.py:133
  1519.7 25.3 all-gather.32.cloned.1.call-done
  1545.0 9.6 fusion.378
  1554.6 19.6 all-gather.34.cloned.1.call-done
  1574.2 13.2 fusion.383
  1589.0 9.1 fusion.384
  1598.2 55.0 %reduce-scatter.29.cloned.1.call-done = f32[256,1408]{1,0:T(8,128)} async-done(((f32[1024,1408]{1,0:T(8,128)}), f32[256,1408]{1,0:T(8,128)}) %reduce-scatter.29.cloned.1.call-update) | async-done | bytes 1441808 | tf_op jit(solution)/shard_map/while/body/eval_jaxpr/reduce_scatter | solution.py:137
  1661.2 25.2 all-gather.36.cloned.1.call-done
  1718.2 55.0 %reduce-scatter.31.cloned.1.call-done = f32[256,1408]{1,0:T(8,128)} async-done(((f32[1024,1408]{1,0:T(8,128)}), f32[256,1408]{1,0:T(8,128)}) %reduce-scatter.31.cloned.1.call-update) | async-done | bytes 1441808 | tf_op jit(solution)/shard_map/while/body/eval_jaxpr/reduce_scatter | solution.py:137
  1778.4 10.3 fusion.403
  1789.5 16.1 all-gather.38.cloned.1.call-done
  1809.0 16.3 multiply_reduce_fusion.74
  1827.8 8.6 multiply_convert_fusion.22
  1865.3 9.1 fusion.391
  1883.2 10.7 convolution_add_fusion.4
  1894.0 14.1 convolution_add_fusion.5
  1953.3 10.3 select_add_fusion.9
  1987.7 10.9 copy.115
  1999.2 9.2 copy.117
  2010.3 47.4 %reduce-scatter.13.cloned.1.call-done = f32[128,2,352]{0,2,1:T(8,128)} async-done(((f32[1024,2,352]{0,2,1:T(8,128)}), f32[128,2,352]{0,2,1:T(8,128)}) %reduce-scatter.13.cloned.1.call-update) | async-done | bytes 360464 | tf_op jit(solution)/shard_map/reduce_scatter | solution.py:372
  2059.8 142.0 %reduce-scatter.23.cloned.1.call-done = f32[176,1408]{1,0:T(8,128)} async-done(((f32[1408,1408]{1,0:T(8,128)}), f32[176,1408]{1,0:T(8,128)}) %reduce-scatter.23.cloned.1.call-update) | async-done | bytes 991248 | tf_op jit(solution)/shard_map/reduce_scatter | solution.py:377
  2201.8 270.7 %reduce-scatter.21.cloned.1.call-done = f32[352,1408]{1,0:T(8,128)} async-done(((f32[2816,1408]{1,0:T(8,128)}), f32[352,1408]{1,0:T(8,128)}) %reduce-scatter.21.cloned.1.call-update) | async-done | bytes 1982480 | tf_op jit(solution)/shard_map/reduce_scatter | solution.py:376
  2472.6 93.1 %reduce-scatter.15.cloned.1.call-done = f32[2,352,176]{1,2,0:T(8,128)} async-done(((f32[2,352,1408]{1,2,0:T(8,128)}), f32[2,352,176]{1,2,0:T(8,128)}) %reduce-scatter.15.cloned.1.call-update) | async-done | bytes 495632 | tf_op jit(solution)/shard_map/reduce_scatter | solution.py:373
  2568.4 277.9 %all-reduce.12.cloned.1.call-done = f32[1408,4,352]{2,1,0:T(4,128)} async-done(((f32[1408,4,352]{2,1,0:T(4,128)}), f32[1408,4,352]{2,1,0:T(4,128)}) %all-reduce.12.cloned.1.call-update) | async-done | bytes 7929872
  2851.5 151.4 %reduce-scatter.17.cloned.1.call-done = f32[176,1536]{1,0:T(8,128)} async-done(((f32[1408,1536]{1,0:T(8,128)}), f32[176,1536]{1,0:T(8,128)}) %reduce-scatter.17.cloned.1.call-update) | async-done | bytes 1081360 | tf_op jit(solution)/shard_map/reduce_scatter | solution.py:374
  3007.9 152.2 %reduce-scatter.19.cloned.1.call-done = f32[1536,176]{0,1:T(8,128)} async-done(((f32[1536,1408]{0,1:T(8,128)}), f32[1536,176]{0,1:T(8,128)}) %reduce-scatter.19.cloned.1.call-update) | async-done | bytes 1081360 | tf_op jit(solution)/shard_map/reduce_scatter | solution.py:375
  3164.8 62.6 %all-reduce.14.cloned.1.call-done = (f32[352,1408]{1,0:T(8,128)}, f32[176,1408]{1,0:T(8,128)}) async-done(((f32[352,1408]{1,0:T(8,128)}, f32[176,1408]{1,0:T(8,128)}), (f32[352,1408]{1,0:T(8,128)}, f32[176,1408]{1,0:T(8,128)})) %all-reduce.14.cloned.1.call-update) | async-done | bytes 2973712 | tf_op jit(solution)/shard_map/psum | solution.py:379
  3243.6 40.5 %all-reduce.7 = (f32[12]{0:T(128)S(1)}, f32[12]{0:T(128)S(1)}, f32[5,1408]{1,0:T(8,128)}, f32[4,88]{1,0:T(4,128)S(1)}) all-reduce(f32[12]{0:T(128)S(1)} %concatenate.60, f32[12]{0:T(128)S(1)} %concatenate.61, f32[5,1408]{1,0:T(8,128)S(1)} %copy-done.121, f32[4,88]{1,0:T(4,128)S(1)} %copy-done.168), channel_id=1, replica_groups=mesh['dp'=8,'tensor'=4] {'dp','tensor'}, use_global_device_ids=true, to_apply=%region_63.64 | all-reduce | flops 7416 | bytes 59328 | tf_op jit(solution)/shard_map/psum | solution.py:423
  (1162 shorter events, 591.3 us)
Async XLA Ops:
  7.2 56.3 %all-gather.22.cloned.1.call-start = ((), (), s32[]{:S(2)}) async-start(), calls=%async_computation.16 | async-start | bytes 2433024 | tf_op jit(solution)/shard_map/all_gather | solution.py:149
  9.5 130.3 %all-gather.18.cloned.1.call-start = ((), (), s32[]{:S(2)}) async-start(), calls=%async_computation.14 | async-start | bytes 4866048 | tf_op jit(solution)/shard_map/all_gather | solution.py:147
  11.5 204.4 %all-gather.20.cloned.1.call-start = ((), (), s32[]{:S(2)}) async-start(), calls=%async_computation.15 | async-start | bytes 4866048 | tf_op jit(solution)/shard_map/all_gather | solution.py:151
  12.5 248.0 %all-gather.24.cloned.1.call-start = ((), (), s32[]{:S(2)}) async-start(), calls=%async_computation.17 | async-start | bytes 1622016 | tf_op jit(solution)/shard_map/all_gather | solution.py:148
  13.2 318.7 %all-gather.16.cloned.1.call-start = ((), (), s32[]{:S(2)}) async-start(), calls=%async_computation.13 | async-start | bytes 4460544 | tf_op jit(solution)/shard_map/all_gather | solution.py:153
  14.2 393.8 %all-gather.26.cloned.1.call-start = ((), (), s32[]{:S(2)}) async-start(), calls=%async_computation.18 | async-start | bytes 4866048 | tf_op jit(solution)/shard_map/all_gather | solution.py:150
  15.1 513.0 %all-gather.14.cloned.1.call-start = ((), (), s32[]{:S(2)}) async-start(), calls=%async_computation.12 | async-start | bytes 8921088 | tf_op jit(solution)/shard_map/all_gather | solution.py:152
  147.9 380.3 %copy-start.127 = (f32[5,1408]{1,0:T(8,128)S(1)}, f32[5,1408]{1,0:T(8,128)}, u32[]{:S(2)}) copy-start(f32[5,1408]{1,0:T(8,128)} %param.62) | copy-start | bytes 84484
  528.5 66.9 %copy-start.41 = (f32[1024,1,88]{0,2,1:T(8,128)}, f32[1024,1,88]{0,2,1:T(8,128)S(1)}, u32[]{:S(2)}) copy-start(f32[1024,1,88]{0,2,1:T(8,128)S(1)} %get-tuple-element.1239) | copy-start | bytes 1081348 | tf_op jit(solution)/shard_map/while
  528.5 37.0 %all-gather.28.cloned.1.call-start = ((), (), s32[]{:S(2)}) async-start(), calls=%async_computation.27 | async-start | bytes 3604480 | tf_op jit(solution)/shard_map/while/body/eval_jaxpr/all_gather | solution.py:116
  540.1 143.2 %reduce-scatter.25.cloned.1.call-start = ((), (), s32[]{:S(2)}) async-start(), calls=%async_computation.28 | async-start | bytes 7208960 | tf_op jit(solution)/shard_map/while/body/eval_jaxpr/reduce_scatter | solution.py:133
  541.4 54.0 %copy-start.151 = (f32[88]{0:T(128)}, f32[88]{0:T(128)S(1)}, u32[]{:S(2)}) copy-start(f32[88]{0:T(128)S(1)} %get-tuple-element.1075) | copy-start | bytes 1060 | tf_op jit(solution)/shard_map/while
  541.4 54.0 %copy-start.153 = (f32[88]{0:T(128)}, f32[88]{0:T(128)S(1)}, u32[]{:S(2)}) copy-start(f32[88]{0:T(128)S(1)} %get-tuple-element.1080) | copy-start | bytes 1060 | tf_op jit(solution)/shard_map/while
  541.4 189.4 %copy-start.140 = (f32[88]{0:T(128)}, f32[88]{0:T(128)S(1)}, u32[]{:S(2)}) copy-start(f32[88]{0:T(128)S(1)} %get-tuple-element.1089) | copy-start | bytes 1060 | tf_op jit(solution)/shard_map/while
  541.4 191.4 %copy-start.164 = (f32[88]{0:T(128)}, f32[88]{0:T(128)S(1)}, u32[]{:S(2)}) copy-start(f32[88]{0:T(128)S(1)} %get-tuple-element.1093) | copy-start | bytes 1060 | tf_op jit(solution)/shard_map/while
  628.3 55.0 %copy-start.10 = (f32[256,1408]{1,0:T(8,128)S(1)}, f32[256,1408]{1,0:T(8,128)}, u32[]{:S(2)}) copy-start(f32[256,1408]{1,0:T(8,128)} %copy-done.9) | copy-start | bytes 4325380 | tf_op jit(solution)/shard_map/while
  628.3 85.3 %all-gather.30.cloned.1.call-start = ((), (), s32[]{:S(2)}) async-start(), calls=%async_computation.29 | async-start | bytes 3604480 | tf_op jit(solution)/shard_map/while/body/eval_jaxpr/all_gather | solution.py:116
  686.5 111.4 %reduce-scatter.27.cloned.1.call-start = ((), (), s32[]{:S(2)}) async-start(), calls=%async_computation.31 | async-start | bytes 7208960 | tf_op jit(solution)/shard_map/while/body/eval_jaxpr/reduce_scatter | solution.py:133
  742.8 84.1 %all-gather.32.cloned.1.call-start = ((), (), s32[]{:S(2)}) async-start(), calls=%async_computation.30 | async-start | bytes 3604480 | tf_op jit(solution)/shard_map/while/body/eval_jaxpr/all_gather | solution.py:141
  745.2 110.9 %all-gather.34.cloned.1.call-start = ((), (), s32[]{:S(2)}) async-start(), calls=%async_computation.32 | async-start | bytes 3604480 | tf_op jit(solution)/shard_map/while/body/eval_jaxpr/all_gather | solution.py:116
  799.4 138.3 %copy-start.5 = (f32[256,1408]{1,0:T(8,128)}, f32[256,1408]{1,0:T(8,128)S(1)}, u32[]{:S(2)}) copy-start(f32[256,1408]{1,0:T(8,128)S(1)} %get-tuple-element.1096) | copy-start | bytes 4325380 | tf_op jit(solution)/shard_map/while
  801.6 133.5 %reduce-scatter.29.cloned.1.call-start = ((), (), s32[]{:S(2)}) async-start(), calls=%async_computation.33 | async-start | bytes 7208960 | tf_op jit(solution)/shard_map/while/body/eval_jaxpr/reduce_scatter | solution.py:137
  880.1 88.3 %all-gather.36.cloned.1.call-start = ((), (), s32[]{:S(2)}) async-start(), calls=%async_computation.34 | async-start | bytes 3604480 | tf_op jit(solution)/shard_map/while/body/eval_jaxpr/all_gather | solution.py:141
  941.1 113.7 %reduce-scatter.31.cloned.1.call-start = ((), (), s32[]{:S(2)}) async-start(), calls=%async_computation.35 | async-start | bytes 7208960 | tf_op jit(solution)/shard_map/while/body/eval_jaxpr/reduce_scatter | solution.py:137
  999.7 55.1 %copy-start.138 = (f32[256]{0:T(256)S(1)}, f32[256]{0:T(256)}, u32[]{:S(2)}) copy-start(f32[256]{0:T(256)} %copy-done.137) | copy-start | bytes 3076 | tf_op jit(solution)/shard_map/while
  999.7 55.1 %copy-start.146 = (f32[256]{0:T(256)S(1)}, f32[256]{0:T(256)}, u32[]{:S(2)}) copy-start(f32[256]{0:T(256)} %copy-done.145) | copy-start | bytes 3076 | tf_op jit(solution)/shard_map/while
  999.8 57.5 %copy-start.160 = (f32[256]{0:T(256)S(1)}, f32[256]{0:T(256)}, u32[]{:S(2)}) copy-start(f32[256]{0:T(256)} %copy-done.159) | copy-start | bytes 3076 | tf_op jit(solution)/shard_map/while
  999.8 87.5 %all-gather.38.cloned.1.call-start = ((), (), s32[]{:S(2)}) async-start(), calls=%async_computation.36 | async-start | bytes 3604480 | tf_op jit(solution)/shard_map/while/body/eval_jaxpr/all_gather | solution.py:141
  1060.0 127.1 %reduce-scatter.35.cloned.1.call-start = ((), (), s32[]{:S(2)}) async-start(), calls=%async_computation.38 | async-start | bytes 7208960 | tf_op jit(solution)/shard_map/while/body/eval_jaxpr/reduce_scatter | solution.py:133
  1070.4 147.6 %reduce-scatter.33.cloned.1.call-start = ((), (), s32[]{:S(2)}) async-start(), calls=%async_computation.37 | async-start | bytes 7208960 | tf_op jit(solution)/shard_map/while/body/eval_jaxpr/reduce_scatter | solution.py:137
  1244.8 68.4 %copy-start.41 = (f32[1024,1,88]{0,2,1:T(8,128)}, f32[1024,1,88]{0,2,1:T(8,128)S(1)}, u32[]{:S(2)}) copy-start(f32[1024,1,88]{0,2,1:T(8,128)S(1)} %get-tuple-element.1239) | copy-start | bytes 1081348 | tf_op jit(solution)/shard_map/while
  1244.8 38.8 %all-gather.28.cloned.1.call-start = ((), (), s32[]{:S(2)}) async-start(), calls=%async_computation.27 | async-start | bytes 3604480 | tf_op jit(solution)/shard_map/while/body/eval_jaxpr/all_gather | solution.py:116
  1256.4 145.0 %reduce-scatter.25.cloned.1.call-start = ((), (), s32[]{:S(2)}) async-start(), calls=%async_computation.28 | async-start | bytes 7208960 | tf_op jit(solution)/shard_map/while/body/eval_jaxpr/reduce_scatter | solution.py:133
  1257.6 55.6 %copy-start.151 = (f32[88]{0:T(128)}, f32[88]{0:T(128)S(1)}, u32[]{:S(2)}) copy-start(f32[88]{0:T(128)S(1)} %get-tuple-element.1075) | copy-start | bytes 1060 | tf_op jit(solution)/shard_map/while
  1257.6 55.6 %copy-start.153 = (f32[88]{0:T(128)}, f32[88]{0:T(128)S(1)}, u32[]{:S(2)}) copy-start(f32[88]{0:T(128)S(1)} %get-tuple-element.1080) | copy-start | bytes 1060 | tf_op jit(solution)/shard_map/while
  1257.6 191.3 %copy-start.140 = (f32[88]{0:T(128)}, f32[88]{0:T(128)S(1)}, u32[]{:S(2)}) copy-start(f32[88]{0:T(128)S(1)} %get-tuple-element.1089) | copy-start | bytes 1060 | tf_op jit(solution)/shard_map/while
  1257.6 193.3 %copy-start.164 = (f32[88]{0:T(128)}, f32[88]{0:T(128)S(1)}, u32[]{:S(2)}) copy-start(f32[88]{0:T(128)S(1)} %get-tuple-element.1093) | copy-start | bytes 1060 | tf_op jit(solution)/shard_map/while
  1346.4 55.0 %copy-start.10 = (f32[256,1408]{1,0:T(8,128)S(1)}, f32[256,1408]{1,0:T(8,128)}, u32[]{:S(2)}) copy-start(f32[256,1408]{1,0:T(8,128)} %copy-done.9) | copy-start | bytes 4325380 | tf_op jit(solution)/shard_map/while
  1346.4 85.3 %all-gather.30.cloned.1.call-start = ((), (), s32[]{:S(2)}) async-start(), calls=%async_computation.29 | async-start | bytes 3604480 | tf_op jit(solution)/shard_map/while/body/eval_jaxpr/all_gather | solution.py:116
  1404.6 111.3 %reduce-scatter.27.cloned.1.call-start = ((), (), s32[]{:S(2)}) async-start(), calls=%async_computation.31 | async-start | bytes 7208960 | tf_op jit(solution)/shard_map/while/body/eval_jaxpr/reduce_scatter | solution.py:133
  1460.9 84.1 %all-gather.32.cloned.1.call-start = ((), (), s32[]{:S(2)}) async-start(), calls=%async_computation.30 | async-start | bytes 3604480 | tf_op jit(solution)/shard_map/while/body/eval_jaxpr/all_gather | solution.py:141
  1463.2 110.9 %all-gather.34.cloned.1.call-start = ((), (), s32[]{:S(2)}) async-start(), calls=%async_computation.32 | async-start | bytes 3604480 | tf_op jit(solution)/shard_map/while/body/eval_jaxpr/all_gather | solution.py:116
  1517.4 138.3 %copy-start.5 = (f32[256,1408]{1,0:T(8,128)}, f32[256,1408]{1,0:T(8,128)S(1)}, u32[]{:S(2)}) copy-start(f32[256,1408]{1,0:T(8,128)S(1)} %get-tuple-element.1096) | copy-start | bytes 4325380 | tf_op jit(solution)/shard_map/while
  1519.7 133.5 %reduce-scatter.29.cloned.1.call-start = ((), (), s32[]{:S(2)}) async-start(), calls=%async_computation.33 | async-start | bytes 7208960 | tf_op jit(solution)/shard_map/while/body/eval_jaxpr/reduce_scatter | solution.py:137
  1598.1 88.3 %all-gather.36.cloned.1.call-start = ((), (), s32[]{:S(2)}) async-start(), calls=%async_computation.34 | async-start | bytes 3604480 | tf_op jit(solution)/shard_map/while/body/eval_jaxpr/all_gather | solution.py:141
  1659.2 114.0 %reduce-scatter.31.cloned.1.call-start = ((), (), s32[]{:S(2)}) async-start(), calls=%async_computation.35 | async-start | bytes 7208960 | tf_op jit(solution)/shard_map/while/body/eval_jaxpr/reduce_scatter | solution.py:137
  1718.1 55.1 %copy-start.138 = (f32[256]{0:T(256)S(1)}, f32[256]{0:T(256)}, u32[]{:S(2)}) copy-start(f32[256]{0:T(256)} %copy-done.137) | copy-start | bytes 3076 | tf_op jit(solution)/shard_map/while
  1718.1 55.1 %copy-start.146 = (f32[256]{0:T(256)S(1)}, f32[256]{0:T(256)}, u32[]{:S(2)}) copy-start(f32[256]{0:T(256)} %copy-done.145) | copy-start | bytes 3076 | tf_op jit(solution)/shard_map/while
  1718.1 57.5 %copy-start.160 = (f32[256]{0:T(256)S(1)}, f32[256]{0:T(256)}, u32[]{:S(2)}) copy-start(f32[256]{0:T(256)} %copy-done.159) | copy-start | bytes 3076 | tf_op jit(solution)/shard_map/while
  1718.1 87.5 %all-gather.38.cloned.1.call-start = ((), (), s32[]{:S(2)}) async-start(), calls=%async_computation.36 | async-start | bytes 3604480 | tf_op jit(solution)/shard_map/while/body/eval_jaxpr/all_gather | solution.py:141
  1778.4 129.8 %reduce-scatter.35.cloned.1.call-start = ((), (), s32[]{:S(2)}) async-start(), calls=%async_computation.38 | async-start | bytes 7208960 | tf_op jit(solution)/shard_map/while/body/eval_jaxpr/reduce_scatter | solution.py:133
  1788.8 150.9 %reduce-scatter.33.cloned.1.call-start = ((), (), s32[]{:S(2)}) async-start(), calls=%async_computation.37 | async-start | bytes 7208960 | tf_op jit(solution)/shard_map/while/body/eval_jaxpr/reduce_scatter | solution.py:137
  1980.1 77.6 %reduce-scatter.13.cloned.1.call-start = ((), (), s32[]{:S(2)}) async-start(), calls=%async_computation.19 | async-start | bytes 3244032 | tf_op jit(solution)/shard_map/reduce_scatter | solution.py:372
  1980.8 221.0 %reduce-scatter.23.cloned.1.call-start = ((), (), s32[]{:S(2)}) async-start(), calls=%async_computation.24 | async-start | bytes 8921088 | tf_op jit(solution)/shard_map/reduce_scatter | solution.py:377
  1981.4 491.1 %reduce-scatter.21.cloned.1.call-start = ((), (), s32[]{:S(2)}) async-start(), calls=%async_computation.23 | async-start | bytes 17842176 | tf_op jit(solution)/shard_map/reduce_scatter | solution.py:376
  1982.1 583.5 %reduce-scatter.15.cloned.1.call-start = ((), (), s32[]{:S(2)}) async-start(), calls=%async_computation.20 | async-start | bytes 4866048 | tf_op jit(solution)/shard_map/reduce_scatter | solution.py:373
  1987.7 858.6 %all-reduce.12.cloned.1.call-start = ((), (), s32[]{:S(2)}) async-start(), calls=%async_computation.25 | async-start | bytes 17301504
  1998.6 1004.3 %reduce-scatter.17.cloned.1.call-start = ((), (), s32[]{:S(2)}) async-start(), calls=%async_computation.21 | async-start | bytes 9732096 | tf_op jit(solution)/shard_map/reduce_scatter | solution.py:374
  1999.2 1160.9 %reduce-scatter.19.cloned.1.call-start = ((), (), s32[]{:S(2)}) async-start(), calls=%async_computation.22 | async-start | bytes 9732096 | tf_op jit(solution)/shard_map/reduce_scatter | solution.py:375
  2008.5 1218.9 %all-reduce.14.cloned.1.call-start = ((), (), s32[]{:S(2)}) async-start(), calls=%async_computation.26 | async-start | bytes 5947392 | tf_op jit(solution)/shard_map/psum | solution.py:379
  2472.5 93.1 %copy-start.95 = (f32[2,352,176]{1,2,0:T(8,128)S(1)}, f32[2,352,176]{1,2,0:T(8,128)}, u32[]{:S(2)}) copy-start(f32[2,352,176]{1,2,0:T(8,128)} %param.47) | copy-start | bytes 1486852
  2472.5 373.8 %copy-start.83 = (f32[176,4,352]{2,1,0:T(4,128)S(1)}, f32[176,4,352]{2,1,0:T(4,128)}, u32[]{:S(2)}) copy-start(f32[176,4,352]{2,1,0:T(4,128)} %param.41) | copy-start | bytes 2973700
  2472.5 373.7 %copy-start.129 = (f32[176,4,352]{2,1,0:T(4,128)S(1)}, f32[176,4,352]{2,1,0:T(4,128)}, u32[]{:S(2)}) copy-start(f32[176,4,352]{2,1,0:T(4,128)} %param.43) | copy-start | bytes 2973700
  2851.5 308.6 %copy-start.85 = (f32[1536,176]{0,1:T(8,128)S(1)}, f32[1536,176]{0,1:T(8,128)}, u32[]{:S(2)}) copy-start(f32[1536,176]{0,1:T(8,128)} %param.53) | copy-start | bytes 3244036
  (316 other events, 1837.9 us)
Sparse Core Ops, SparseCore 0:
  10.8 52.6 all-gather.21
  66.3 73.5 all-gather.17
  142.6 73.2 all-gather.19
  218.3 42.0 all-gather.23
  263.0 68.8 all-gather.15
  334.6 73.3 all-gather.25
  410.7 117.4 all-gather.13
  540.2 25.2 all-gather.27
  628.5 54.8 reduce-scatter.24
  686.6 27.0 all-gather.29
  742.9 54.8 reduce-scatter.26
  799.8 27.0 all-gather.31
  829.0 27.0 all-gather.33
  880.2 54.8 reduce-scatter.28
  941.2 27.0 all-gather.35
  999.9 54.8 reduce-scatter.30
  1060.1 27.0 all-gather.37
  1089.6 54.8 reduce-scatter.34
  1163.0 55.0 reduce-scatter.32
  1256.6 27.0 all-gather.27
  1346.6 54.8 reduce-scatter.24
  1404.7 27.0 all-gather.29
  1461.0 54.8 reduce-scatter.26
  1517.8 27.0 all-gather.31
  1547.1 27.0 all-gather.33
  1598.2 54.8 reduce-scatter.28
  1659.3 27.0 all-gather.35
  1718.2 54.8 reduce-scatter.30
  1778.5 27.0 all-gather.37
  1808.0 54.8 reduce-scatter.34
  1881.5 55.0 reduce-scatter.32
  1985.0 72.5 reduce-scatter.12
  2061.2 140.5 reduce-scatter.22
  2205.7 266.7 reduce-scatter.20
  2476.7 88.8 reduce-scatter.14
  2569.8 276.4 all-reduce.11
  2850.3 152.5 reduce-scatter.16
  3007.5 152.5 reduce-scatter.18
  3162.4 64.9 all-reduce.13
where the time goes:
time: 3320 us
  waiting for transfers between devices  2380 us (72%)
  matrix products  394 us (12%)
  other arithmetic  260 us (8%)
  local copies, waits for them, and re-layouts  210 us (6%)
  blocking collectives  40.5 us (1%)
    unnamed x16, waiting for transfers between devices  280 us
    reduce_scatter x1, waiting for transfers between devices, body(): lax.psum_scatter(totals[5], 'dp', scatter_dimension=0, tiled=True)  271 us
    reduce_scatter x6, waiting for transfers between devices, sum_grads(): lax.psum_scatter(rows_times_t(left, right), 'tensor', scatter_dimension=0...  221 us
    reduce_scatter x6, waiting for transfers between devices, sum_tokens(): lax.psum_scatter(rows_times(left, right), 'tensor', scatter_dimension=0,...  215 us
    reduce_scatter x1, waiting for transfers between devices, body(): lax.psum_scatter(totals[4], 'dp', scatter_dimension=1, tiled=True)  152 us
    reduce_scatter x1, waiting for transfers between devices, body(): lax.psum_scatter(totals[3], 'dp', scatter_dimension=0, tiled=True)  151 us
    reduce_scatter x1, waiting for transfers between devices, body(): lax.psum_scatter(totals[6], 'dp', scatter_dimension=0, tiled=True)  142 us
    all_gather x6, waiting for transfers between devices, gather_grads(): return lax.all_gather(local_rows, 'tensor', axis=0, tiled=True)  133 us
  transfers between devices with their start and end apart: 39, of which 36 were waited for; matrix products, arithmetic and copies ran while one was open for 12% of the time, Pallas kernels for 0%

commit v1 on v0

--- a/solution.py
+++ b/solution.py
@@ -112,47 +112,119 @@
     return (query_grad, keys_grad, values_grad)
 
 
-def project(local_rows, matrix):
-    gathered = lax.all_gather(local_rows, "tensor", axis=0, tiled=True)
-    return (gathered, matmul(gathered, matrix))
-
-
-def weight_grad(kept_rows, grad):
-    return matmul_tn(kept_rows, grad)
-
-
-def rows_times(left, right):
-    return matmul(left, right)
-
-
-def rows_times_t(left, right):
-    return matmul_nt(left, right)
-
-
-def sum_tokens(left, right):
-    return lax.psum_scatter(rows_times(left, right), "tensor", scatter_dimension=0, tiled=True)
-
-
-def sum_grads(left, right):
-    return lax.psum_scatter(rows_times_t(left, right), "tensor", scatter_dimension=0, tiled=True)
-
-
-def gather_grads(local_rows):
-    return lax.all_gather(local_rows, "tensor", axis=0, tiled=True)
-
-
-def fetch_weights(head_mats, text_mats, out_mats, inner_mat, outer_mat, skip_mat, shift_mat):
-    return tuple(
-        (
-            lax.all_gather(head_mats, "dp", axis=0, tiled=True),
-            lax.all_gather(text_mats, "dp", axis=0, tiled=True),
-            lax.all_gather(out_mats, "dp", axis=2, tiled=True),
-            lax.all_gather(inner_mat, "dp", axis=0, tiled=True),
-            lax.all_gather(outer_mat, "dp", axis=1, tiled=True),
-            lax.all_gather(skip_mat, "dp", axis=0, tiled=True),
-            lax.all_gather(shift_mat, "dp", axis=0, tiled=True),
-        )
-    )
+AXES = ("dp", "tensor")
+BF16 = jnp.bfloat16
+F32 = jnp.float32
+
+
+def digits_of(count):
+    found = []
+    while count % 4 == 0:
+        found.append(4)
+        count //= 4
+    if count > 1:
+        found.append(count)
+    return tuple(found)
+
+
+def send(values, move):
+    dp_count, tensor_count = lax.axis_size("dp"), lax.axis_size("tensor")
+    pairs = []
+    for d in range(dp_count):
+        for t in range(tensor_count):
+            d2, t2 = move(d, t)
+            pairs.append((d * tensor_count + t, d2 * tensor_count + t2))
+    return lax.ppermute(values, AXES, pairs)
+
+
+def swap_core(values):
+    return send(values, lambda d, t: (d, t ^ 1))
+
+
+def swap_y(values):
+    return send(values, lambda d, t: (d, t ^ 2))
+
+
+class Digit:
+    def __init__(self, sizes, at):
+        self.size = sizes[at]
+        self.stride = math.prod(sizes[at + 1 :])
+        self.at = at
+        self.mine = (lax.axis_index("dp") // self.stride) % self.size
+
+    def step(self, values):
+        def move(d, t):
+            digit = (d // self.stride) % self.size
+            return (d + ((digit + 1) % self.size - digit) * self.stride, t)
+
+        return send(values, move)
+
+
+def gather_digits(piece, digits, lead=0):
+    done = []
+    for digit in digits:
+        axis = lead + sum(1 for other in done if other < digit.at)
+        shape = piece.shape[:axis] + (digit.size,) + piece.shape[axis:]
+        whole = jnp.zeros(shape, piece.dtype)
+        for k in range(digit.size):
+            if k:
+                piece = digit.step(piece)
+            place = (digit.mine - k) % digit.size
+            whole = lax.dynamic_update_index_in_dim(whole, piece, place, axis)
+        piece = whole
+        done.append(digit.at)
+    return piece
+
+
+def add_low(left, right, dtype=BF16):
+    return (left.astype(F32) + right.astype(F32)).astype(dtype)
+
+
+def reduce_digits(parts, digits, lead=0, last=F32):
+    left = sorted(digit.at for digit in digits)
+    for at, digit in enumerate(digits):
+        axis = lead + left.index(digit.at)
+        left.remove(digit.at)
+
+        def part(k):
+            return lax.dynamic_index_in_dim(
+                parts, (digit.mine - k) % digit.size, axis, keepdims=False
+            )
+
+        moving = part(1)
+        for k in range(2, digit.size + 1):
+            final = k == digit.size and at == len(digits) - 1
+            moving = add_low(digit.step(moving), part(k), last if final else BF16)
+        parts = moving
+    return parts
+
+
+def sum_everywhere(values, dp_only=False):
+    bit = 1
+    if not dp_only:
+        while bit < lax.axis_size("tensor"):
+            values = values + send(values, lambda d, t: (d, t ^ bit))
+            bit *= 2
+    bit = 1
+    while bit < lax.axis_size("dp"):
+        values = values + send(values, lambda d, t: (d ^ bit, t))
+        bit *= 2
+    return values
+
+
+def gather_core(rows):
+    return jnp.concatenate([rows, swap_core(rows)], 0)
+
+
+def sum_core(rows):
+    half = rows.shape[0] // 2
+    return rows[:half] + swap_core(rows[half:].astype(BF16)).astype(F32)
+
+
+def in_order(own, other, place, axis=0):
+    first = jnp.where(place == 0, own, other)
+    second = jnp.where(place == 0, other, own)
+    return jnp.stack([first, second], axis)
 
 
 def lamb_parts(master, first, second, grad):
@@ -212,171 +284,258 @@
     first_head_gains,
     second_head_gains,
 ):
-    cosines, sines = rotary_tables(patch_order)
-    conditions = time_embed(timesteps)
     dp_count = lax.axis_size("dp")
+    tensor_count = lax.axis_size("tensor")
+    me_d = lax.axis_index("dp")
+    me_t = lax.axis_index("tensor")
+    me_y = me_t // 2
+    sizes = digits_of(dp_count)
+    digits = [Digit(sizes, at) for at in range(len(sizes))]
+    backwards = digits[::-1]
     width = latents.shape[2]
+    block = latents.shape[1]
+    rows = 2 * block
+    depth = width // dp_count
+    text_depth = text_inputs.shape[0]
+    text_width = text_depth * dp_count
     head_cols = head_inputs.shape[2]
-    text_width = text_inputs.shape[0] * dp_count
     hidden_cols = mlp_inner.shape[1]
-    low_head = head_inputs.astype(jnp.bfloat16)
-    low_text = text_inputs.astype(jnp.bfloat16)
-    low_out = head_outputs.astype(jnp.bfloat16)
-    low_inner = mlp_inner.astype(jnp.bfloat16)
-    low_outer = mlp_outer.astype(jnp.bfloat16)
-    low_skip = skip_linear.astype(jnp.bfloat16)
-    low_shift = shift_linear.astype(jnp.bfloat16)
-    fetched = fetch_weights(low_head, low_text, low_out, low_inner, low_outer, low_skip, low_shift)
-
-    def micro_step(totals, items):
-        latent, skip_part, text_part, cond, shift_row, cotangent = items
-        head_mats, text_mats, out_mats, inner_mat, outer_mat, skip_mat, shift_mat = fetched
-        local_rows = latent.shape[0]
-        total_rows = local_rows * lax.axis_size("tensor")
-        text_rows = text_part.shape[0]
-        joined = jnp.concatenate([latent, skip_part], -1).astype(jnp.float32)
-        skip_gain = row_gains[0:2].reshape(-1)
-        normed, normed_back = jax.vjp(norm_rows, joined, skip_gain)
-        normed16 = normed.astype(jnp.bfloat16)
-        hidden = matmul(normed16, skip_mat)
-        silu16 = jax.nn.silu(cond).astype(jnp.bfloat16)
-        shift = matmul(silu16[None, :], shift_mat)
-        first_norm, first_back = jax.vjp(norm_rows, hidden, row_gains[2])
-        attn16 = (first_norm + shift).astype(jnp.bfloat16)
-        self_cols = head_mats[:, 0:3, :].reshape(width, 3 * head_cols)
-        attn_kept, self_pre = project(attn16, self_cols)
-        query, query_back = jax.vjp(
-            partial(rope_heads, cosines=cosines, sines=sines),
-            self_pre[:, :head_cols],
-            head_gains[0],
+    latent_count = 2 * dp_count
+
+    low_head = head_inputs.astype(BF16)
+    low_out = head_outputs.astype(BF16)
+    half_depth = skip_linear.shape[0] // 2
+    skip_half = lax.dynamic_slice_in_dim(skip_linear, (me_t % 2) * half_depth, half_depth, 0).astype(BF16)
+    self_pack = jnp.concatenate([low_head[:, 0:3].reshape(depth, 3 * head_cols), low_out[0].T], 1)
+    cross_pack = jnp.concatenate(
+        [
+            jnp.concatenate([low_head[:, 3], low_out[1].T], 1),
+            text_inputs.astype(BF16).reshape(text_depth, 2 * head_cols),
+        ],
+        0,
+    )
+    mlp_pack = jnp.concatenate([mlp_inner.astype(BF16), mlp_outer.T.astype(BF16)], 1)
+
+    def mine_first(pair):
+        return (
+            lax.dynamic_index_in_dim(pair, me_y, 0, keepdims=False),
+            lax.dynamic_index_in_dim(pair, 1 - me_y, 0, keepdims=False),
         )
-        keys, keys_back = jax.vjp(
-            partial(rope_heads, cosines=cosines, sines=sines),
-            self_pre[:, head_cols : 2 * head_cols],
-            head_gains[1],
-        )
-        query16 = query.astype(jnp.bfloat16)
-        keys16 = keys.astype(jnp.bfloat16)
-        values16 = self_pre[:, 2 * head_cols :].reshape(total_rows, -1, HD).astype(jnp.bfloat16)
-        self_out16, self_lse = attend(query16, keys16, values16)
-        self_flat = self_out16.reshape(total_rows, head_cols)
-        after_self = hidden + sum_tokens(self_flat, out_mats[0])
-        third_norm, third_back = jax.vjp(norm_rows, after_self, row_gains[3])
-        cross16 = third_norm.astype(jnp.bfloat16)
-        cross_mat = head_mats[:, 3, :]
-        cross_kept, cross_pre = project(cross16, cross_mat)
-        cross_query, cross_query_back = jax.vjp(
-            partial(rope_heads, cosines=cosines, sines=sines), cross_pre, head_gains[2]
-        )
-        text_pre = matmul(text_part, text_mats.reshape(text_width, 2 * head_cols))
-        text_keys, text_keys_back = jax.vjp(plain_heads, text_pre[:, :head_cols], head_gains[3])
-        cross_query16 = cross_query.astype(jnp.bfloat16)
-        text_keys16 = text_keys.astype(jnp.bfloat16)
-        text_values16 = text_pre[:, head_cols:].reshape(text_rows, -1, HD).astype(jnp.bfloat16)
-        cross_out16, cross_lse = attend(cross_query16, text_keys16, text_values16)
-        cross_flat = cross_out16.reshape(total_rows, head_cols)
-        after_cross = after_self + sum_tokens(cross_flat, out_mats[1])
-        second_norm, second_back = jax.vjp(norm_rows, after_cross, row_gains[4])
-        mlp16 = second_norm.astype(jnp.bfloat16)
-        mlp_kept, inner = project(mlp16, inner_mat)
-        activated, gelu_back = jax.vjp(gelu_tanh, inner)
-        activated16 = activated.astype(jnp.bfloat16)
-        block_out = after_cross + sum_tokens(activated16, outer_mat)
-        mlp_full_grad = gather_grads(cotangent.astype(jnp.bfloat16))
-        outer_grad = matmul_tn(activated16, mlp_full_grad)
-        (inner_grad,) = gelu_back(matmul_nt(mlp_full_grad, outer_mat))
-        inner_grad16 = inner_grad.astype(jnp.bfloat16)
-        inner_wgrad = weight_grad(mlp_kept, inner_grad16)
-        mlp_in_grad = sum_grads(inner_grad16, inner_mat)
-        cross_res_grad, fifth_gain_grad = second_back(mlp_in_grad)
-        after_cross_grad = cotangent + cross_res_grad
-        cross_full_grad = gather_grads(after_cross_grad.astype(jnp.bfloat16))
-        cross_out_wgrad = matmul_tn(cross_flat, cross_full_grad)
-        cross_mixed_grad = (
-            matmul_nt(cross_full_grad, out_mats[1]).astype(jnp.bfloat16).reshape(total_rows, -1, HD)
-        )
-        cq_grad, ck_grad, cv_grad = attend_back(
-            cross_query16, text_keys16, text_values16, cross_lse, cross_mixed_grad
-        )
-        cq_pre_grad, cq_gain_grad = cross_query_back(cq_grad)
-        ck_pre_grad, ck_gain_grad = text_keys_back(ck_grad)
-        text_grad16 = jnp.concatenate(
-            [ck_pre_grad, cv_grad.reshape(text_rows, head_cols)], 1
-        ).astype(jnp.bfloat16)
-        text_wgrad = matmul_tn(text_part, text_grad16).reshape(text_width, 2, head_cols)
-        cq_pre16 = cq_pre_grad.astype(jnp.bfloat16)
-        cross_q_wgrad = weight_grad(cross_kept, cq_pre16)
-        cross_in_grad = sum_grads(cq_pre16, cross_mat)
-        self_res_grad, fourth_gain_grad = third_back(cross_in_grad)
-        after_self_grad = after_cross_grad + self_res_grad
-        self_full_grad = gather_grads(after_self_grad.astype(jnp.bfloat16))
-        self_out_wgrad = matmul_tn(self_flat, self_full_grad)
-        self_mixed_grad = (
-            matmul_nt(self_full_grad, out_mats[0]).astype(jnp.bfloat16).reshape(total_rows, -1, HD)
-        )
-        sq_grad, sk_grad, sv_grad = attend_back(
-            query16, keys16, values16, self_lse, self_mixed_grad
-        )
-        sq_pre_grad, sq_gain_grad = query_back(sq_grad)
-        sk_pre_grad, sk_gain_grad = keys_back(sk_grad)
-        self_pre16 = jnp.concatenate(
-            [sq_pre_grad, sk_pre_grad, sv_grad.reshape(total_rows, head_cols)], 1
-        ).astype(jnp.bfloat16)
-        self_wgrad = weight_grad(attn_kept, self_pre16).reshape(width, 3, head_cols)
-        attn_grad = sum_grads(self_pre16, self_cols)
-        hidden_norm_grad, third_gain_grad = first_back(attn_grad)
-        shift_grad = jnp.sum(attn_grad, axis=0)
-        hidden_grad16 = (after_self_grad + hidden_norm_grad).astype(jnp.bfloat16)
-        skip_wgrad = matmul_tn(normed16, hidden_grad16)
-        joined_grad, skip_gain_grad = normed_back(matmul_nt(hidden_grad16, skip_mat))
-        row_grad = jnp.stack(
-            [
-                skip_gain_grad[:width],
-                skip_gain_grad[width:],
-                third_gain_grad,
-                fourth_gain_grad,
-                fifth_gain_grad,
-            ]
-        )
-        head_grad = jnp.stack([sq_gain_grad, sk_gain_grad, cq_gain_grad, ck_gain_grad])
-        head_in_wgrad = jnp.concatenate([self_wgrad, cross_q_wgrad[:, None, :]], 1)
-        out_wgrad = jnp.stack([self_out_wgrad, cross_out_wgrad])
-        increments = (head_in_wgrad, text_wgrad, out_wgrad, inner_wgrad, outer_grad, skip_wgrad)
-        increments = increments + (silu16.astype(jnp.float32)[:, None] * shift_grad[None, :],)
-        increments = increments + (row_grad, head_grad)
-        totals = tuple((left + right for left, right in zip(totals, increments)))
-        return (totals, (block_out, joined_grad[:, :width], joined_grad[:, width:], shift_grad))
-
-    zero_totals = (
-        jnp.zeros((width, 4, head_cols), jnp.float32),
-        jnp.zeros((text_width, 2, head_cols), jnp.float32),
-        jnp.zeros((2, head_cols, width), jnp.float32),
-        jnp.zeros((width, hidden_cols), jnp.float32),
-        jnp.zeros((hidden_cols, width), jnp.float32),
-        jnp.zeros((2 * width, width), jnp.float32),
-    )
-    zero_totals = zero_totals + (jnp.zeros((width, width), jnp.float32),)
-    zero_totals = zero_totals + (
-        jnp.zeros((5, width), jnp.float32),
-        jnp.zeros((4, HD), jnp.float32),
-    )
-    totals, (block_out, grad_latents, grad_skip_input, shift_grads) = lax.scan(
-        micro_step,
-        zero_totals,
-        (latents, skip_input, text_states, conditions, conditions, out_grad),
-    )
-    row_sum = totals[-2]
-    head_sum = totals[-1]
-    head_in_grad, text_in_grad, head_out_grad, mlp_in_grad, mlp_out_grad, skip_part, shift_part = (
-        lax.psum_scatter(totals[0], "dp", scatter_dimension=0, tiled=True),
-        lax.psum_scatter(totals[1], "dp", scatter_dimension=0, tiled=True),
-        lax.psum_scatter(totals[2], "dp", scatter_dimension=2, tiled=True),
-        lax.psum_scatter(totals[3], "dp", scatter_dimension=0, tiled=True),
-        lax.psum_scatter(totals[4], "dp", scatter_dimension=1, tiled=True),
-        lax.psum_scatter(totals[5], "dp", scatter_dimension=0, tiled=True),
-        lax.psum_scatter(totals[6], "dp", scatter_dimension=0, tiled=True),
-    )
-    skip_mat_grad, shift_mat_grad = lax.psum((skip_part, shift_part), "tensor")
+
+    def by_latent(own, other):
+        return jnp.where(me_y == 0, jnp.stack([own, other]), jnp.stack([other, own]))
+
+    joined_own, joined_other = mine_first(jnp.concatenate([latents, skip_input], -1))
+    joined16 = jnp.concatenate([joined_own, swap_y(joined_other)], 0)
+    skip_got = gather_digits(skip_half, digits)
+    skip_pair = in_order(skip_got, swap_core(skip_got), me_t % 2, len(sizes))
+    skip_mat = skip_pair.reshape(2 * width, width)
+    self_near = gather_digits(self_pack, digits)
+    self_near = self_near.reshape(width, 4 * head_cols)
+    self_far = swap_y(self_near)
+    cross_pair = gather_digits(jnp.stack([cross_pack, swap_y(cross_pack)]), digits, 1)
+    cross_pair = cross_pair.reshape(2, dp_count, depth + text_depth, 2 * head_cols)
+    mlp_got = gather_digits(mlp_pack, digits).reshape(width, 2 * hidden_cols)
+
+    self_mats = [pack[:, : 3 * head_cols] for pack in (self_near, self_far)]
+    self_outs = [pack[:, 3 * head_cols :] for pack in (self_near, self_far)]
+    cross_mat = jnp.concatenate(
+        [cross_pair[k, :, :depth, :head_cols].reshape(width, head_cols) for k in range(2)], 1
+    )
+    cross_out = jnp.concatenate(
+        [cross_pair[k, :, :depth, head_cols:].reshape(width, head_cols) for k in range(2)], 1
+    )
+    text_mat = jnp.concatenate(
+        [cross_pair[k, :, depth:, :head_cols].reshape(text_width, head_cols) for k in range(2)]
+        + [cross_pair[k, :, depth:, head_cols:].reshape(text_width, head_cols) for k in range(2)],
+        1,
+    )
+    self_out = jnp.concatenate(self_outs, 1)
+    inner_mat, outer_mat = mlp_got[:, :hidden_cols], mlp_got[:, hidden_cols:]
+
+    steps = jnp.zeros((dp_count, 2), F32)
+    steps = lax.dynamic_update_slice(steps, timesteps.astype(F32)[None], (me_d, 0))
+    steps = sum_everywhere(steps, dp_only=True).reshape(latent_count)
+    silu16 = jax.nn.silu(time_embed(steps)).astype(BF16)
+    silu_cols = lax.dynamic_slice_in_dim(silu16, me_d * depth, depth, 1)
+    shifts = sum_everywhere(matmul(silu_cols, shift_linear.astype(BF16)), dp_only=True)
+    my_latent = me_d * 2 + me_y
+    shift = lax.dynamic_slice_in_dim(shifts, my_latent, 1, 0)
+
+    places = patch_order.reshape(tensor_count, block)
+    places = jnp.concatenate(
+        [lax.dynamic_index_in_dim(places, me_t ^ k, 0, keepdims=False) for k in (0, 2, 1, 3)]
+    )
+    cosines, sines = rotary_tables(places)
+    text_part = lax.dynamic_index_in_dim(text_states, me_y, 0, keepdims=False)
+
+    cot_own, cot_other = mine_first(out_grad)
+    cot_pair = jnp.concatenate([cot_own, cot_other], 0).astype(BF16)
+    cot_got = swap_y(cot_pair)
+    cotangent = jnp.concatenate([cot_own, cot_got[block:].astype(F32)], 0)
+    mlp_full_grad = gather_core(
+        jnp.concatenate([cot_pair[:block], cot_got[block:], cot_got[:block], cot_pair[block:]], 0)
+    )
+
+    skip_gain = row_gains[0:2].reshape(-1)
+    normed, normed_back = jax.vjp(norm_rows, joined16.astype(F32), skip_gain)
+    normed16 = normed.astype(BF16)
+    hidden = matmul(normed16, skip_mat)
+    first_norm, first_back = jax.vjp(norm_rows, hidden, row_gains[2])
+    attn16 = (first_norm + shift).astype(BF16)
+    attn_full = gather_core(attn16)
+    self_pres = [matmul(attn_full, mat) for mat in self_mats]
+    both = lambda k: jnp.concatenate(
+        [pre[:, k * head_cols : (k + 1) * head_cols] for pre in self_pres], 1
+    )
+    rope = partial(rope_heads, cosines=cosines, sines=sines)
+    query, query_back = jax.vjp(rope, both(0), head_gains[0])
+    keys, keys_back = jax.vjp(rope, both(1), head_gains[1])
+    query16, keys16 = query.astype(BF16), keys.astype(BF16)
+    values16 = both(2).reshape(2 * rows, -1, HD).astype(BF16)
+    self_out16, self_lse = attend(query16, keys16, values16)
+    self_flat = self_out16.reshape(2 * rows, 2 * head_cols)
+    after_self = hidden + sum_core(matmul_nt(self_flat, self_out))
+    third_norm, third_back = jax.vjp(norm_rows, after_self, row_gains[3])
+    cross_kept = gather_core(third_norm.astype(BF16))
+    cross_query, cross_query_back = jax.vjp(rope, matmul(cross_kept, cross_mat), head_gains[2])
+    text_pre = matmul(text_part, text_mat)
+    text_keys, text_keys_back = jax.vjp(plain_heads, text_pre[:, : 2 * head_cols], head_gains[3])
+    cross_query16, text_keys16 = cross_query.astype(BF16), text_keys.astype(BF16)
+    text_rows = text_part.shape[0]
+    text_values16 = text_pre[:, 2 * head_cols :].reshape(text_rows, -1, HD).astype(BF16)
+    cross_out16, cross_lse = attend(cross_query16, text_keys16, text_values16)
+    cross_flat = cross_out16.reshape(2 * rows, 2 * head_cols)
+    after_cross = after_self + sum_core(matmul_nt(cross_flat, cross_out))
+    second_norm, second_back = jax.vjp(norm_rows, after_cross, row_gains[4])
+
+    mlp16 = second_norm.astype(BF16)
+    mlp_kept = gather_core(jnp.concatenate([mlp16, swap_y(mlp16)], 0))
+    inner = matmul(mlp_kept, inner_mat)
+    activated, gelu_back = jax.vjp(gelu_tanh, inner)
+    activated16 = activated.astype(BF16)
+
+    def sum_chips(part):
+        part = sum_core(part)
+        return part[:rows] + swap_y(part[rows:].astype(BF16)).astype(F32)
+
+    result = after_cross + sum_chips(matmul_nt(activated16, outer_mat))
+
+    outer_wgrad = matmul_tn(mlp_full_grad, activated16)
+    (inner_grad,) = gelu_back(matmul(mlp_full_grad, outer_mat))
+    inner_grad16 = inner_grad.astype(BF16)
+    inner_wgrad = matmul_tn(mlp_kept, inner_grad16)
+    mlp_sum = jnp.concatenate([inner_wgrad.astype(BF16), outer_wgrad.astype(BF16)], 1)
+    mlp_sum = reduce_digits(mlp_sum.reshape(*sizes, depth, 2 * hidden_cols), backwards)
+    cross_res_grad, fifth_gain_grad = second_back(sum_chips(matmul_nt(inner_grad16, inner_mat)))
+    after_cross_grad = cotangent + cross_res_grad
+    cross_full_grad = gather_core(after_cross_grad.astype(BF16))
+    cross_out_wgrad = matmul_tn(cross_full_grad, cross_flat).astype(BF16)
+    cross_mixed_grad = matmul(cross_full_grad, cross_out).astype(BF16).reshape(2 * rows, -1, HD)
+    cq_grad, ck_grad, cv_grad = attend_back(
+        cross_query16, text_keys16, text_values16, cross_lse, cross_mixed_grad
+    )
+    cq_pre_grad, cq_gain_grad = cross_query_back(cq_grad)
+    ck_pre_grad, ck_gain_grad = text_keys_back(ck_grad)
+    text_grad16 = jnp.concatenate(
+        [ck_pre_grad, cv_grad.reshape(text_rows, 2 * head_cols)], 1
+    ).astype(BF16)
+    text_wgrad = matmul_tn(text_part, text_grad16).astype(BF16)
+    cq_pre16 = cq_pre_grad.astype(BF16)
+    cross_q_wgrad = matmul_tn(cross_kept, cq_pre16).astype(BF16)
+    cross_parts = []
+    for k in range(2):
+        near = slice(k * head_cols, (k + 1) * head_cols)
+        far = slice((2 + k) * head_cols, (3 + k) * head_cols)
+        top = jnp.concatenate([cross_q_wgrad[:, near], cross_out_wgrad[:, near]], 1)
+        low = jnp.concatenate([text_wgrad[:, near], text_wgrad[:, far]], 1)
+        top = top.reshape(*sizes, depth, 2 * head_cols)
+        low = low.reshape(*sizes, text_depth, 2 * head_cols)
+        cross_parts.append(jnp.concatenate([top, low], -2))
+    cross_sum = reduce_digits(jnp.stack(cross_parts), backwards, 1, BF16)
+    cross_sum = add_low(cross_sum[0], swap_y(cross_sum[1]), F32)
+    self_res_grad, fourth_gain_grad = third_back(sum_core(matmul_nt(cq_pre16, cross_mat)))
+    after_self_grad = after_cross_grad + self_res_grad
+    self_full_grad = gather_core(after_self_grad.astype(BF16))
+    self_out_wgrad = matmul_tn(self_full_grad, self_flat).astype(BF16)
+    self_mixed_grad = matmul(self_full_grad, self_out).astype(BF16).reshape(2 * rows, -1, HD)
+    sq_grad, sk_grad, sv_grad = attend_back(query16, keys16, values16, self_lse, self_mixed_grad)
+    sq_pre_grad, sq_gain_grad = query_back(sq_grad)
+    sk_pre_grad, sk_gain_grad = keys_back(sk_grad)
+    pre_grads = [sq_pre_grad, sk_pre_grad, sv_grad.reshape(2 * rows, 2 * head_cols)]
+    attn_part = 0.0
+    self_parts = []
+    for k in range(2):
+        near = slice(k * head_cols, (k + 1) * head_cols)
+        pre16 = jnp.concatenate([grad[:, near] for grad in pre_grads], 1).astype(BF16)
+        attn_part = attn_part + matmul_nt(pre16, self_mats[k])
+        in_wgrad = matmul_tn(attn_full, pre16).astype(BF16)
+        part = jnp.concatenate([in_wgrad, self_out_wgrad[:, near]], 1)
+        self_parts.append(part.reshape(*sizes, depth, 4 * head_cols))
+    self_sum = add_low(self_parts[0], swap_y(self_parts[1]))
+    self_sum = reduce_digits(self_sum, backwards)
+    attn_grad = sum_core(attn_part)
+    hidden_norm_grad, third_gain_grad = first_back(attn_grad)
+    shift_grad = jnp.sum(attn_grad, axis=0)
+    hidden_grad16 = (after_self_grad + hidden_norm_grad).astype(BF16)
+    skip_wgrad = matmul_tn(normed16, hidden_grad16).astype(BF16)
+    joined_grad, skip_gain_grad = normed_back(matmul_nt(hidden_grad16, skip_mat))
+
+    quarter = half_depth // 2
+    skip_parts = skip_wgrad.reshape(dp_count, 2, 2, quarter, width)
+    mine = lax.dynamic_index_in_dim(skip_parts, me_t % 2, 2, keepdims=False)
+    theirs = lax.dynamic_index_in_dim(skip_parts, 1 - me_t % 2, 2, keepdims=False)
+    skip_parts = add_low(mine, swap_core(theirs))
+    mine = lax.dynamic_index_in_dim(skip_parts, me_y, 1, keepdims=False)
+    theirs = lax.dynamic_index_in_dim(skip_parts, 1 - me_y, 1, keepdims=False)
+    skip_parts = add_low(mine, swap_y(theirs)).reshape(*sizes, quarter, width)
+    skip_sum = reduce_digits(skip_parts, backwards, 0, BF16)
+    skip_pair = in_order(skip_sum, swap_core(skip_sum), me_t % 2)
+    skip_all = in_order(skip_pair, swap_y(skip_pair), me_y)
+    skip_mat_grad = skip_all.reshape(2 * half_depth, width).astype(F32)
+
+    row_grad = jnp.stack(
+        [
+            skip_gain_grad[:width],
+            skip_gain_grad[width:],
+            third_gain_grad,
+            fourth_gain_grad,
+            fifth_gain_grad,
+        ]
+    )
+    head_grad = jnp.stack([sq_gain_grad, sk_gain_grad, cq_gain_grad, ck_gain_grad])
+    single = jnp.zeros((latent_count, width), F32)
+    single = lax.dynamic_update_slice(single, shift_grad[None], (my_latent, 0))
+    head_row = jnp.pad(head_grad.reshape(1, -1), ((0, 0), (0, width - head_grad.size)))
+    single = sum_everywhere(jnp.concatenate([single, row_grad, head_row], 0))
+    row_gain_grad = single[latent_count : latent_count + 5]
+    head_gain_grad = single[latent_count + 5, : head_grad.size].reshape(head_grad.shape)
+    shift_mat_grad = lax.dot_general(
+        silu_cols.astype(F32),
+        single[:latent_count],
+        (((0,), (0,)), ((), ())),
+        precision=lax.Precision.HIGHEST,
+        preferred_element_type=F32,
+    )
+
+    head_in_grad = jnp.concatenate(
+        [
+            self_sum[:, : 3 * head_cols].reshape(depth, 3, head_cols),
+            cross_sum[:depth, None, :head_cols],
+        ],
+        1,
+    )
+    text_in_grad = cross_sum[depth:].reshape(text_depth, 2, head_cols)
+    head_out_grad = jnp.stack([self_sum[:, 3 * head_cols :].T, cross_sum[:depth, head_cols:].T])
+    mlp_in_grad = mlp_sum[:, :hidden_cols]
+    mlp_out_grad = mlp_sum[:, hidden_cols:].T
+
+    def put_back(values):
+        return by_latent(values[:block], swap_y(values[block:].astype(BF16)).astype(F32))
+
+    block_out = put_back(result)
+    grad_latents = put_back(joined_grad[:, :width])
+    grad_skip_input = put_back(joined_grad[:, width:])
     head_in_first, head_in_second, head_in_ratio = lamb_parts(
         head_inputs, first_head_inputs, second_head_inputs, head_in_grad
     )
@@ -420,9 +579,7 @@
             group_squares(shift_mat_ratio, (0, 1)),
         ]
     )
-    weight_squares, ratio_squares, row_gain_grad, head_gain_grad = lax.psum(
-        (weight_squares, ratio_squares, row_sum, head_sum), ("dp", "tensor")
-    )
+    weight_squares, ratio_squares = sum_everywhere(jnp.stack([weight_squares, ratio_squares]))
     correction = jnp.concatenate(
         [jnp.ones((10,), jnp.float32), jnp.full((2,), 1.0 / lax.axis_size("tensor"), jnp.float32)]
     )

time: 3320 us -> 1480 us (0.45)
  waiting for transfers between devices: 2380 us -> 487 us
  matrix products: 394 us -> 311 us
  other arithmetic: 260 us -> 341 us
  starting transfers between devices: 2.21 us -> 63.1 us
  local copies, waits for them, and re-layouts: 210 us -> 263 us
  blocking collectives: 40.5 us -> 0 us
    reduce_scatter x18 -> x0, waiting for transfers between devices: 1290 us -> none  [the longest x1 271 us: body(): lax.psum_scatter(totals[5], 'dp', scatter_dimension=0, tiled=True)]
    all_gather x19 -> x0, waiting for transfers between devices: 742 us -> none  [the longest x6 133 us: gather_grads(): return lax.all_gather(local_rows, 'tensor', axis=0, tiled=True)]
    ppermute x0 -> x77, waiting for transfers between devices: none -> 487 us  [send(): return lax.ppermute(values, AXES, pairs)]
    unnamed x16 -> x0, waiting for transfers between devices: 280 us -> none
    while x579 -> x0, local copies, waits for them, and re-layouts: 76.2 us -> none
    ppermute x0 -> x77, starting transfers between devices: none -> 63.1 us  [send(): return lax.ppermute(values, AXES, pairs)]
    psum x1 -> x0, waiting for transfers between devices: 62.6 us -> none  [body(): skip_mat_grad, shift_mat_grad = lax.psum((skip_part, shift_part), 'tensor')]
    psum x1 -> x0, blocking collectives: 40.5 us -> none  [body(): lax.psum((weight_squares, ratio_squares, row_sum, head_sum), ('dp', 'tens...]
  transfers between devices with their start and end apart: 39 -> 77, of which waited for: 36 -> 38; matrix products, arithmetic and copies ran while one was open for 12% -> 52% of each run, Pallas kernels for 0% -> 0%
where the time goes in v1:
time: 1480 us; the launch traced here: 1470 us
  waiting for transfers between devices  487 us (33%)
  other arithmetic  341 us (23%)
  matrix products  311 us (21%)
  local copies, waits for them, and re-layouts  263 us (18%)
  starting transfers between devices  63.1 us (4%)
    ppermute x77, waiting for transfers between devices, send(): return lax.ppermute(values, AXES, pairs)  487 us
    dot_general x10, matrix products, matmul(): return jnp.dot(left, right, preferred_element_type=jnp.float32)  74.4 us
    dot_general x9, matrix products, matmul_tn(): lax.dot_general(left, right, (((0,), (0,)), ((), ())), preferred_element_...  64.7 us
    ppermute x77, starting transfers between devices, send(): return lax.ppermute(values, AXES, pairs)  63.1 us
    dot_general x8, matrix products, matmul_nt(): lax.dot_general(left, right, (((1,), (1,)), ((), ())), preferred_element_...  60.8 us
    unnamed x540, local copies, waits for them, and re-layouts  41.7 us
    dynamic_update_slice x21, local copies, waits for them, and re-layouts, gather_digits(): whole = lax.dynamic_update_index_in_dim(whole, piece, place, axis)  38.5 us
    reduce_sum x9, other arithmetic, norm_rows(): return center * lax.rsqrt(spread + norm_eps) * factor  38.2 us
  transfers between devices with their start and end apart: 77, of which 38 were waited for; matrix products, arithmetic and copies ran while one was open for 52% of the time, Pallas kernels for 0%

profile of v1, /device:TPU:0, one launch (start us, length us, event | category | flops | bytes accessed | tf_op | source)
XLA Modules:
  0.0 1473.2 jit_solution(14880357902115102877)
XLA Ops:
  41.5 9.2 collective-permute-done.2
  53.4 10.4 collective-permute-done.3
  76.8 6.0 collective-permute-done.7
  96.9 10.3 collective-permute-done.4
  111.8 10.2 collective-permute-done.15
  125.8 39.2 %collective-permute-done.9 = f32[16,1408]{1,0:T(8,128)S(1)} collective-permute-done((f32[16,1408]{1,0:T(8,128)S(1)}, f32[16,1408]{1,0:T(8,128)S(1)}, u32[]{:S(2)}, u32[]{:S(2)}) %collective-permute-start.9) | collective-permute-done | bytes 90144 | tf_op jit(solution)/shard_map/ppermute | solution.py:137
  169.7 26.2 %collective-permute-done.11 = f32[16,1408]{1,0:T(8,128)S(1)} collective-permute-done((f32[16,1408]{1,0:T(8,128)S(1)}, f32[16,1408]{1,0:T(8,128)S(1)}, u32[]{:S(2)}, u32[]{:S(2)}) %collective-permute-start.11) | collective-permute-done | bytes 90144 | tf_op jit(solution)/shard_map/ppermute | solution.py:137
  211.5 6.1 pad_maximum_fusion.1
  217.6 8.5 fusion.200
  236.3 5.1 collective-permute-start.29
  244.6 8.9 collective-permute-done.22
  260.0 26.7 %collective-permute-done.17 = bf16[1408,1408]{1,0:T(8,128)(2,1)} collective-permute-done((bf16[1408,1408]{1,0:T(8,128)(2,1)}, bf16[1408,1408]{1,0:T(8,128)(2,1)}, u32[]{:S(2)}, u32[]{:S(2)}) %collective-permute-start.17) | collective-permute-done | bytes 3964960 | tf_op jit(solution)/shard_map/ppermute | solution.py:137
  289.4 6.1 fusion.56
  297.0 6.1 fusion.59
  363.9 13.6 multiply_reduce_fusion.1
  377.5 13.6 fusion
  391.1 13.6 fusion.71
  422.9 5.5 concatenate.195
  439.9 6.1 fusion.70
  464.0 5.3 reshape.876
  497.4 6.1 pad_maximum_fusion.15
  503.5 23.8 %collective-permute-done.26 = bf16[512,1408]{1,0:T(8,128)(2,1)S(1)} collective-permute-done((bf16[512,1408]{1,0:T(8,128)(2,1)S(1)}, bf16[512,1408]{1,0:T(8,128)(2,1)S(1)}, u32[]{:S(2)}, u32[]{:S(2)}) %collective-permute-start.26) | collective-permute-done | bytes 1441824 | tf_op jit(solution)/shard_map/ppermute | solution.py:137
  539.4 46.6 %collective-permute-done.31 = bf16[4,176,3072]{2,1,0:T(8,128)(2,1)S(1)} collective-permute-done((bf16[4,176,3072]{2,1,0:T(8,128)(2,1)}, bf16[4,176,3072]{2,1,0:T(8,128)(2,1)S(1)}, u32[]{:S(2)}, u32[]{:S(2)}) %collective-permute-start.31) | collective-permute-done | bytes 4325408 | tf_op jit(solution)/shard_map/ppermute | solution.py:137
  586.6 14.5 fusion.42
  601.1 16.0 %convolution_convert_fusion.3 = bf16[1408,1536]{1,0:T(8,128)(2,1)} fusion(bf16[2048,1408]{1,0:T(8,128)(2,1)} %constant_dynamic-update-slice_fusion.2, f32[2048,1536]{1,0:T(8,128)} %fusion.42), kind=kOutput, calls=%fused_computation.42 | convolution fusion | flops 8888844288 | bytes 22675456 | tf_op jit(solution)/shard_map/dot_general | solution.py:28
  617.2 22.8 %fusion.11 = bf16[2048,1536]{1,0:T(8,128)(2,1)} fusion(f32[2048,1536]{1,0:T(8,128)} %fusion.42, bf16[2048,1408]{1,0:T(8,128)(2,1)} %constant_dynamic-update-slice_fusion.2, bf16[1408,3072]{1,0:T(8,128)(2,1)S(1)} %bitcast.457), kind=kOutput, calls=%fused_computation.18 | convolution fusion | flops 8921284608 | bytes 28966912 | tf_op jit(solution)/shard_map/dot_general | solution.py:24
  640.0 16.7 %fusion.36 = f32[2048,1408]{1,0:T(8,128)} fusion(bf16[1408,3072]{1,0:T(8,128)(2,1)S(1)} %bitcast.458, f32[2048,1536]{1,0:T(8,128)} %fusion.42), kind=kOutput, calls=%fused_computation.89 | convolution fusion | flops 8886681600 | bytes 28442624 | tf_op jit(solution)/shard_map/dot_general | solution.py:34
  656.7 14.5 fusion.40
  680.9 12.9 convolution_convert_fusion.4
  693.8 8.0 pad_maximum_fusion
  721.8 26.4 %collective-permute-done.38 = bf16[512,1408]{1,0:T(8,128)(2,1)S(1)} collective-permute-done((bf16[512,1408]{1,0:T(8,128)(2,1)}, bf16[512,1408]{1,0:T(8,128)(2,1)S(1)}, u32[]{:S(2)}, u32[]{:S(2)}) %collective-permute-start.38) | collective-permute-done | bytes 1441824 | tf_op jit(solution)/shard_map/ppermute | solution.py:137
  752.0 26.0 %collective-permute-done.33 = bf16[512,1408]{1,0:T(8,128)(2,1)} collective-permute-done((bf16[512,1408]{1,0:T(8,128)(2,1)}, bf16[512,1408]{1,0:T(8,128)(2,1)}, u32[]{:S(2)}, u32[]{:S(2)}) %collective-permute-start.33) | collective-permute-done | bytes 1441824 | tf_op jit(solution)/shard_map/ppermute | solution.py:137
  782.5 19.8 %collective-permute-done.55 = bf16[4,176,3072]{2,1,0:T(8,128)(2,1)} collective-permute-done((bf16[4,176,3072]{2,1,0:T(8,128)(2,1)}, bf16[4,176,3072]{2,1,0:T(8,128)(2,1)}, u32[]{:S(2)}, u32[]{:S(2)}) %collective-permute-start.55) | collective-permute-done | bytes 4325408 | tf_op jit(solution)/shard_map/ppermute | solution.py:137
  813.1 20.0 %collective-permute-done.56 = bf16[176,3072]{1,0:T(8,128)(2,1)S(1)} collective-permute-done((bf16[176,3072]{1,0:T(8,128)(2,1)S(1)}, bf16[176,3072]{1,0:T(8,128)(2,1)S(1)}, u32[]{:S(2)}, u32[]{:S(2)}) %collective-permute-start.56) | collective-permute-done | bytes 1081376 | tf_op jit(solution)/shard_map/ppermute | solution.py:137
  859.8 5.1 reshape.881
  864.9 5.7 fusion.192
  874.4 5.2 reshape.882
  891.2 6.3 convolution_convert_fusion.7
  932.5 19.7 %collective-permute-done.58 = bf16[176,3072]{1,0:T(8,128)(2,1)S(1)} collective-permute-done((bf16[176,3072]{1,0:T(8,128)(2,1)S(1)}, bf16[176,3072]{1,0:T(8,128)(2,1)S(1)}, u32[]{:S(2)}, u32[]{:S(2)}) %collective-permute-start.58) | collective-permute-done | bytes 1081376 | tf_op jit(solution)/shard_map/ppermute | solution.py:137
  962.1 15.5 %fusion.75 = bf16[8,88,1024]{2,1,0:T(8,128)(2,1)} fusion(bf16[1024,8,88]{0,2,1:T(8,128)(2,1)} %bitcast.481, f32[8,1024,1024]{1,2,0:T(8,128)} %get-tuple-element.236, f32[8,1024]{1,0:T(8,128)S(1)} %log_add_fusion), kind=kOutput, calls=%fused_computation.232 | convolution fusion | flops 1502281728 | bytes 36470784 | tf_op jit(solution)/shard_map/hqk,qhd->khd/dot_general | solution.py:109
  977.6 23.5 %multiply_reduce_fusion = (f32[8,1024]{1,0:T(8,128)S(1)}, f32[8,1024,1024]{1,2,0:T(8,128)}) fusion(f32[8,1024,1024]{1,2,0:T(8,128)} %get-tuple-element.236, f32[8,1024]{1,0:T(8,128)S(1)} %log_add_fusion, bf16[1024,8,88]{0,2,1:T(8,128)(2,1)} %bitcast.482, bf16[1024,8,88]{0,2,1:T(8,128)(2,1)S(1)} %bitcast.479), kind=kOutput, calls=%fused_computation.1 | convolution fusion | flops 1509941248 | bytes 70057984 | tf_op jit(solution)/shard_map/qhd,khd->hqk/dot_general | solution.py:100
  1002.0 28.4 %multiply_convert_fusion = bf16[8,1024,1024]{1,2,0:T(8,128)(2,1)} fusion(f32[8,1024,1024]{1,2,0:T(8,128)} %get-tuple-element.244, f32[8,1024,1024]{1,2,0:T(8,128)} %get-tuple-element.236, f32[8,1024]{1,0:T(8,128)S(1)} %get-tuple-element.243, f32[8,1024]{1,0:T(8,128)S(1)} %log_add_fusion), kind=kLoop, calls=%fused_computation | loop fusion | flops 41943040 | bytes 83951616 | tf_op jit(solution)/shard_map/convert_element_type | solution.py:102
  1030.4 13.1 fusion.201
  1043.6 13.1 bitcast_multiply_fusion.2
  1061.6 5.7 fusion.190
  1081.1 5.7 fusion.191
  1095.7 11.6 multiply_reduce_fusion.12
  1123.7 6.9 convolution_convert_fusion.1
  1133.0 6.3 copy.113
  1139.3 6.7 fusion.54
  1146.0 6.3 convolution_add_fusion
  1156.8 7.2 convolution_convert_fusion.2
  1173.8 9.1 copy.112
  1183.2 11.4 collective-permute-done.51
  1205.6 6.8 fusion.26
  1217.7 6.9 convolution_convert_fusion
  1229.7 43.6 %collective-permute-done.68 = f32[22,1408]{1,0:T(8,128)S(1)} collective-permute-done((f32[22,1408]{1,0:T(8,128)S(1)}, f32[22,1408]{1,0:T(8,128)S(1)}, u32[]{:S(2)}, u32[]{:S(2)}) %collective-permute-start.68) | collective-permute-done | bytes 123936 | tf_op jit(solution)/shard_map/ppermute | solution.py:137
  1274.8 5.7 fusion.170
  1297.4 5.3 add_convert_fusion
  1320.9 23.5 %collective-permute-done.46 = bf16[4,176,1408]{2,1,0:T(8,128)(2,1)S(1)} collective-permute-done((bf16[4,176,1408]{2,1,0:T(8,128)(2,1)S(1)}, bf16[4,176,1408]{2,1,0:T(8,128)(2,1)S(1)}, u32[]{:S(2)}, u32[]{:S(2)}) %collective-permute-start.46) | collective-permute-done | bytes 1982496 | tf_op jit(solution)/shard_map/ppermute | solution.py:137
  1344.9 14.8 %collective-permute-done.60 = bf16[8,88,1408]{2,1,0:T(8,128)(2,1)S(1)} collective-permute-done((bf16[8,88,1408]{2,1,0:T(8,128)(2,1)S(1)}, bf16[8,88,1408]{2,1,0:T(8,128)(2,1)S(1)}, u32[]{:S(2)}, u32[]{:S(2)}) %collective-permute-start.60) | collective-permute-done | bytes 1982496 | tf_op jit(solution)/shard_map/ppermute | solution.py:137
  1368.7 7.5 collective-permute-done.47
  1385.7 8.4 collective-permute-done.62
  1422.8 9.4 collective-permute-done.66
  (1019 shorter events, 610.3 us)
Async XLA Ops:
  3.4 71.2 %collective-permute-start.6 = (f32[8,2]{1,0:T(8,128)}, f32[8,2]{1,0:T(8,128)}, u32[]{:S(2)}, u32[]{:S(2)}) collective-permute-start(f32[8,2]{1,0:T(8,128)} %dynamic_update_slice.92), channel_id=1, source_target_pairs={{0,4},{1,5},{2,6},{3,7},{4,0},{5,1},{6,2},{7,3},{8,12},{9,13},{10,... | collective-permute-start | bytes 200 | tf_op jit(solution)/shard_map/ppermute | solution.py:137
  9.8 80.2 %collective-permute-start.19 = (bf16[304,704]{1,0:T(8,128)(2,1)}, bf16[304,704]{1,0:T(8,128)(2,1)}, u32[]{:S(2)}, u32[]{:S(2)}) collective-permute-start(bf16[304,704]{1,0:T(8,128)(2,1)} %get-tuple-element.203), channel_id=1, source_target_pairs={{0,2},{1,3},{2,0},{3,1},{4,6},{5,7},{6,4},{7,5},{8,10},{9,11},{10,... | collective-permute-start | bytes 1284104 | tf_op jit(solution)/shard_map/ppermute | solution.py:137
  15.0 21.5 %collective-permute-start.1 = (bf16[176,1408]{1,0:T(8,128)(2,1)}, bf16[176,1408]{1,0:T(8,128)(2,1)}, u32[]{:S(2)}, u32[]{:S(2)}) collective-permute-start(bf16[176,1408]{1,0:T(8,128)(2,1)} %get-tuple-element.139), channel_id=1, source_target_pairs={{0,8},{1,9},{2,10},{3,11},{4,12},{5,13},{6,14},{7,15},{8,16},{9,17... | collective-permute-start | bytes 1486856 | tf_op jit(solution)/shard_map/ppermute | solution.py:137
  19.6 55.0 %collective-permute-start.13 = (bf16[176,1408]{1,0:T(8,128)(2,1)}, bf16[176,1408]{1,0:T(8,128)(2,1)}, u32[]{:S(2)}, u32[]{:S(2)}) collective-permute-start(bf16[176,1408]{1,0:T(8,128)(2,1)} %get-tuple-element.137), channel_id=1, source_target_pairs={{0,8},{1,9},{2,10},{3,11},{4,12},{5,13},{6,14},{7,15},{8,16},{9,17... | collective-permute-start | bytes 1486856 | tf_op jit(solution)/shard_map/ppermute | solution.py:137
  29.4 166.7 %collective-permute-start = (bf16[256,2816]{1,0:T(8,128)(2,1)}, bf16[256,2816]{1,0:T(8,128)(2,1)}, u32[]{:S(2)}, u32[]{:S(2)}) collective-permute-start(bf16[256,2816]{1,0:T(8,128)(2,1)} %get-tuple-element.176), channel_id=1, source_target_pairs={{0,2},{1,3},{2,0},{3,1},{4,6},{5,7},{6,4},{7,5},{8,10},{9,11},{10,... | collective-permute-start | bytes 4325384 | tf_op jit(solution)/shard_map/ppermute | solution.py:137
  36.5 14.3 collective-permute-start.2
  50.8 13.1 collective-permute-start.3
  64.7 42.5 %collective-permute-start.4 = (bf16[4,176,1408]{2,1,0:T(8,128)(2,1)}, bf16[4,176,1408]{2,1,0:T(8,128)(2,1)}, u32[]{:S(2)}, u32[]{:S(2)}) collective-permute-start(bf16[4,176,1408]{2,1,0:T(8,128)(2,1)} %bitcast_dynamic-update-slice_fusion.20), channel_id=1, source_target_pairs={{0,4},{1,5},{2,6},{3,7},{4,0},{5,1},{6,2},{7,3},{8,12},{9,13},{10,... | collective-permute-start | bytes 5947400 | tf_op jit(solution)/shard_map/ppermute | solution.py:137
  74.6 17.4 %collective-permute-start.14 = (bf16[176,1408]{1,0:T(8,128)(2,1)}, bf16[176,1408]{1,0:T(8,128)(2,1)S(1)}, u32[]{:S(2)}, u32[]{:S(2)}) collective-permute-start(bf16[176,1408]{1,0:T(8,128)(2,1)} %collective-permute-done.13), channel_id=1, source_target_pairs={{0,8},{1,9},{2,10},{3,11},{4,12},{5,13},{6,14},{7,15},{8,16},{9,17... | collective-permute-start | bytes 1486856 | tf_op jit(solution)/shard_map/ppermute | solution.py:137
  91.1 104.8 %collective-permute-start.20 = (bf16[2,304,704]{2,1,0:T(8,128)(2,1)S(1)}, bf16[2,304,704]{2,1,0:T(8,128)(2,1)S(1)}, u32[]{:S(2)}, u32[]{:S(2)}) collective-permute-start(bf16[2,304,704]{2,1,0:T(8,128)(2,1)S(1)} %pad_maximum_fusion.50), channel_id=1, source_target_pairs={{0,8},{1,9},{2,10},{3,11},{4,12},{5,13},{6,14},{7,15},{8,16},{9,17... | collective-permute-start | bytes 2568200 | tf_op jit(solution)/shard_map/ppermute | solution.py:137
  92.0 30.1 %collective-permute-start.15 = (bf16[176,1408]{1,0:T(8,128)(2,1)S(1)}, bf16[176,1408]{1,0:T(8,128)(2,1)S(1)}, u32[]{:S(2)}, u32[]{:S(2)}) collective-permute-start(bf16[176,1408]{1,0:T(8,128)(2,1)S(1)} %collective-permute-done.14), channel_id=1, source_target_pairs={{0,8},{1,9},{2,10},{3,11},{4,12},{5,13},{6,14},{7,15},{8,16},{9,17... | collective-permute-start | bytes 1486856 | tf_op jit(solution)/shard_map/ppermute | solution.py:137
  109.1 100.1 %collective-permute-start.5 = (bf16[4,2,176,1408]{3,2,1,0:T(8,128)(2,1)S(1)}, bf16[4,2,176,1408]{3,2,1,0:T(8,128)(2,1)S(1)}, u32[]{:S(2)}, u32[]{:S(2)}) collective-permute-start(bf16[4,2,176,1408]{3,2,1,0:T(8,128)(2,1)S(1)} %bitcast_dynamic-update-slice_fusion.7), channel_id=1, source_target_pairs={{0,1},{1,0},{2,3},{3,2},{4,5},{5,4},{6,7},{7,6},{8,9},{9,8},{10,11... | collective-permute-start | bytes 11894792 | tf_op jit(solution)/shard_map/ppermute | solution.py:137
  122.9 82.9 %collective-permute-start.16 = (bf16[4,176,1408]{2,1,0:T(8,128)(2,1)}, bf16[4,176,1408]{2,1,0:T(8,128)(2,1)S(1)}, u32[]{:S(2)}, u32[]{:S(2)}) collective-permute-start(bf16[4,176,1408]{2,1,0:T(8,128)(2,1)} %bitcast_dynamic-update-slice_fusion.16), channel_id=1, source_target_pairs={{0,4},{1,5},{2,6},{3,7},{4,0},{5,1},{6,2},{7,3},{8,12},{9,13},{10,... | collective-permute-start | bytes 5947400 | tf_op jit(solution)/shard_map/ppermute | solution.py:137
  124.6 40.4 %collective-permute-start.9 = (f32[16,1408]{1,0:T(8,128)S(1)}, f32[16,1408]{1,0:T(8,128)S(1)}, u32[]{:S(2)}, u32[]{:S(2)}) collective-permute-start(f32[16,1408]{1,0:T(8,128)S(1)} %fusion.100), channel_id=1, source_target_pairs={{0,4},{1,5},{2,6},{3,7},{4,0},{5,1},{6,2},{7,3},{8,12},{9,13},{10,... | collective-permute-start | bytes 270344 | tf_op jit(solution)/shard_map/ppermute | solution.py:137
  169.6 26.3 %collective-permute-start.11 = (f32[16,1408]{1,0:T(8,128)S(1)}, f32[16,1408]{1,0:T(8,128)S(1)}, u32[]{:S(2)}, u32[]{:S(2)}) collective-permute-start(f32[16,1408]{1,0:T(8,128)S(1)} %add.692), channel_id=1, source_target_pairs={{0,16},{1,17},{2,18},{3,19},{4,20},{5,21},{6,22},{7,23},{8,24},{9,... | collective-permute-start | bytes 270344 | tf_op jit(solution)/shard_map/ppermute | solution.py:137
  195.9 40.4 %collective-permute-start.28 = (bf16[176,3072]{1,0:T(8,128)(2,1)}, bf16[176,3072]{1,0:T(8,128)(2,1)}, u32[]{:S(2)}, u32[]{:S(2)}) collective-permute-start(bf16[176,3072]{1,0:T(8,128)(2,1)} %pad_maximum_fusion.47), channel_id=1, source_target_pairs={{0,8},{1,9},{2,10},{3,11},{4,12},{5,13},{6,14},{7,15},{8,16},{9,17... | collective-permute-start | bytes 3244040 | tf_op jit(solution)/shard_map/ppermute | solution.py:137
  196.0 298.3 %collective-permute-start.35 = (bf16[512,1408]{1,0:T(8,128)(2,1)}, bf16[512,1408]{1,0:T(8,128)(2,1)}, u32[]{:S(2)}, u32[]{:S(2)}) collective-permute-start(bf16[512,1408]{1,0:T(8,128)(2,1)} %pad_maximum_fusion.40), channel_id=1, source_target_pairs={{0,2},{1,3},{2,0},{3,1},{4,6},{5,7},{6,4},{7,5},{8,10},{9,11},{10,... | collective-permute-start | bytes 4325384 | tf_op jit(solution)/shard_map/ppermute | solution.py:137
  196.1 31.7 %collective-permute-start.21 = (bf16[2,304,704]{2,1,0:T(8,128)(2,1)S(1)}, bf16[2,304,704]{2,1,0:T(8,128)(2,1)}, u32[]{:S(2)}, u32[]{:S(2)}) collective-permute-start(bf16[2,304,704]{2,1,0:T(8,128)(2,1)S(1)} %collective-permute-done.20), channel_id=1, source_target_pairs={{0,8},{1,9},{2,10},{3,11},{4,12},{5,13},{6,14},{7,15},{8,16},{9,17... | collective-permute-start | bytes 2568200 | tf_op jit(solution)/shard_map/ppermute | solution.py:137
  207.3 79.5 %collective-permute-start.17 = (bf16[1408,1408]{1,0:T(8,128)(2,1)}, bf16[1408,1408]{1,0:T(8,128)(2,1)}, u32[]{:S(2)}, u32[]{:S(2)}) collective-permute-start(bf16[1408,1408]{1,0:T(8,128)(2,1)} %bitcast.24), channel_id=1, source_target_pairs={{0,2},{1,3},{2,0},{3,1},{4,6},{5,7},{6,4},{7,5},{8,10},{9,11},{10,... | collective-permute-start | bytes 11894792 | tf_op jit(solution)/shard_map/ppermute | solution.py:137
  227.7 61.7 %collective-permute-start.12 = (bf16[512,1408]{1,0:T(8,128)(2,1)S(1)}, bf16[512,1408]{1,0:T(8,128)(2,1)}, u32[]{:S(2)}, u32[]{:S(2)}) collective-permute-start(bf16[512,1408]{1,0:T(8,128)(2,1)S(1)} %add_convert_fusion.8), channel_id=1, source_target_pairs={{0,1},{1,0},{2,3},{3,2},{4,5},{5,4},{6,7},{7,6},{8,9},{9,8},{10,11... | collective-permute-start | bytes 4325384 | tf_op jit(solution)/shard_map/ppermute | solution.py:137
  227.8 25.7 %collective-permute-start.22 = (bf16[2,304,704]{2,1,0:T(8,128)(2,1)}, bf16[2,304,704]{2,1,0:T(8,128)(2,1)}, u32[]{:S(2)}, u32[]{:S(2)}) collective-permute-start(bf16[2,304,704]{2,1,0:T(8,128)(2,1)} %collective-permute-done.21), channel_id=1, source_target_pairs={{0,8},{1,9},{2,10},{3,11},{4,12},{5,13},{6,14},{7,15},{8,16},{9,17... | collective-permute-start | bytes 2568200 | tf_op jit(solution)/shard_map/ppermute | solution.py:137
  236.3 174.3 %collective-permute-start.29 = (bf16[176,3072]{1,0:T(8,128)(2,1)}, bf16[176,3072]{1,0:T(8,128)(2,1)}, u32[]{:S(2)}, u32[]{:S(2)}) collective-permute-start(bf16[176,3072]{1,0:T(8,128)(2,1)} %collective-permute-done.28), channel_id=1, source_target_pairs={{0,8},{1,9},{2,10},{3,11},{4,12},{5,13},{6,14},{7,15},{8,16},{9,17... | collective-permute-start | bytes 3244040 | tf_op jit(solution)/shard_map/ppermute | solution.py:137
  255.8 158.1 %collective-permute-start.23 = (bf16[2,4,304,704]{3,2,1,0:T(8,128)(2,1)}, bf16[2,4,304,704]{3,2,1,0:T(8,128)(2,1)}, u32[]{:S(2)}, u32[]{:S(2)}) collective-permute-start(bf16[2,4,304,704]{3,2,1,0:T(8,128)(2,1)} %bitcast_dynamic-update-slice_fusion.12), channel_id=1, source_target_pairs={{0,4},{1,5},{2,6},{3,7},{4,0},{5,1},{6,2},{7,3},{8,12},{9,13},{10,... | collective-permute-start | bytes 10272776 | tf_op jit(solution)/shard_map/ppermute | solution.py:137
  408.2 8.4 collective-permute-start.18
  410.6 77.6 %collective-permute-start.30 = (bf16[176,3072]{1,0:T(8,128)(2,1)}, bf16[176,3072]{1,0:T(8,128)(2,1)}, u32[]{:S(2)}, u32[]{:S(2)}) collective-permute-start(bf16[176,3072]{1,0:T(8,128)(2,1)} %collective-permute-done.29), channel_id=1, source_target_pairs={{0,8},{1,9},{2,10},{3,11},{4,12},{5,13},{6,14},{7,15},{8,16},{9,17... | collective-permute-start | bytes 3244040 | tf_op jit(solution)/shard_map/ppermute | solution.py:137
  419.7 18.9 %collective-permute-start.24 = (bf16[512,1408]{1,0:T(8,128)(2,1)}, bf16[512,1408]{1,0:T(8,128)(2,1)}, u32[]{:S(2)}, u32[]{:S(2)}) collective-permute-start(bf16[512,1408]{1,0:T(8,128)(2,1)} %multiply_convert_fusion.4), channel_id=1, source_target_pairs={{0,1},{1,0},{2,3},{3,2},{4,5},{5,4},{6,7},{7,6},{8,9},{9,8},{10,11... | collective-permute-start | bytes 4325384 | tf_op jit(solution)/shard_map/ppermute | solution.py:137
  490.5 95.6 %collective-permute-start.31 = (bf16[4,176,3072]{2,1,0:T(8,128)(2,1)}, bf16[4,176,3072]{2,1,0:T(8,128)(2,1)S(1)}, u32[]{:S(2)}, u32[]{:S(2)}) collective-permute-start(bf16[4,176,3072]{2,1,0:T(8,128)(2,1)} %bitcast_dynamic-update-slice_fusion.8), channel_id=1, source_target_pairs={{0,4},{1,5},{2,6},{3,7},{4,0},{5,1},{6,2},{7,3},{8,12},{9,13},{10,... | collective-permute-start | bytes 12976136 | tf_op jit(solution)/shard_map/ppermute | solution.py:137
  494.0 33.3 %collective-permute-start.26 = (bf16[512,1408]{1,0:T(8,128)(2,1)S(1)}, bf16[512,1408]{1,0:T(8,128)(2,1)S(1)}, u32[]{:S(2)}, u32[]{:S(2)}) collective-permute-start(bf16[512,1408]{1,0:T(8,128)(2,1)S(1)} %multiply_convert_fusion.3), channel_id=1, source_target_pairs={{0,2},{1,3},{2,0},{3,1},{4,6},{5,7},{6,4},{7,5},{8,10},{9,11},{10,... | collective-permute-start | bytes 4325384 | tf_op jit(solution)/shard_map/ppermute | solution.py:137
  503.5 32.3 %collective-permute-start.36 = (bf16[1024,1408]{1,0:T(8,128)(2,1)}, bf16[1024,1408]{1,0:T(8,128)(2,1)}, u32[]{:S(2)}, u32[]{:S(2)}) collective-permute-start(bf16[1024,1408]{1,0:T(8,128)(2,1)} %pad_maximum_fusion.15), channel_id=1, source_target_pairs={{0,1},{1,0},{2,3},{3,2},{4,5},{5,4},{6,7},{7,6},{8,9},{9,8},{10,11... | collective-permute-start | bytes 8650760 | tf_op jit(solution)/shard_map/ppermute | solution.py:137
  527.5 59.1 %collective-permute-start.27 = (bf16[1024,1408]{1,0:T(8,128)(2,1)S(1)}, bf16[1024,1408]{1,0:T(8,128)(2,1)}, u32[]{:S(2)}, u32[]{:S(2)}) collective-permute-start(bf16[1024,1408]{1,0:T(8,128)(2,1)S(1)} %pad_maximum_fusion.14), channel_id=1, source_target_pairs={{0,1},{1,0},{2,3},{3,2},{4,5},{5,4},{6,7},{7,6},{8,9},{9,8},{10,11... | collective-permute-start | bytes 8650760 | tf_op jit(solution)/shard_map/ppermute | solution.py:137
  680.4 33.5 %collective-permute-start.32 = (bf16[1024,1408]{1,0:T(8,128)(2,1)}, bf16[1024,1408]{1,0:T(8,128)(2,1)}, u32[]{:S(2)}, u32[]{:S(2)}) collective-permute-start(bf16[1024,1408]{1,0:T(8,128)(2,1)} %slice.627), channel_id=1, source_target_pairs={{0,1},{1,0},{2,3},{3,2},{4,5},{5,4},{6,7},{7,6},{8,9},{9,8},{10,11... | collective-permute-start | bytes 8650760 | tf_op jit(solution)/shard_map/ppermute | solution.py:137
  680.4 27.8 %collective-permute-start.37 = (bf16[1024,1408]{1,0:T(8,128)(2,1)}, bf16[1024,1408]{1,0:T(8,128)(2,1)}, u32[]{:S(2)}, u32[]{:S(2)}) collective-permute-start(bf16[1024,1408]{1,0:T(8,128)(2,1)} %slice.626), channel_id=1, source_target_pairs={{0,1},{1,0},{2,3},{3,2},{4,5},{5,4},{6,7},{7,6},{8,9},{9,8},{10,11... | collective-permute-start | bytes 8650760 | tf_op jit(solution)/shard_map/ppermute | solution.py:137
  706.7 95.6 %collective-permute-start.55 = (bf16[4,176,3072]{2,1,0:T(8,128)(2,1)}, bf16[4,176,3072]{2,1,0:T(8,128)(2,1)}, u32[]{:S(2)}, u32[]{:S(2)}) collective-permute-start(bf16[4,176,3072]{2,1,0:T(8,128)(2,1)} %dynamic-slice_bitcast_fusion), channel_id=1, source_target_pairs={{0,4},{1,5},{2,6},{3,7},{4,0},{5,1},{6,2},{7,3},{8,12},{9,13},{10,... | collective-permute-start | bytes 12976136 | tf_op jit(solution)/shard_map/ppermute | solution.py:137
  713.5 34.7 %collective-permute-start.38 = (bf16[512,1408]{1,0:T(8,128)(2,1)}, bf16[512,1408]{1,0:T(8,128)(2,1)S(1)}, u32[]{:S(2)}, u32[]{:S(2)}) collective-permute-start(bf16[512,1408]{1,0:T(8,128)(2,1)} %slice.630), channel_id=1, source_target_pairs={{0,2},{1,3},{2,0},{3,1},{4,6},{5,7},{6,4},{7,5},{8,10},{9,11},{10,... | collective-permute-start | bytes 4325384 | tf_op jit(solution)/shard_map/ppermute | solution.py:137
  720.0 58.1 %collective-permute-start.33 = (bf16[512,1408]{1,0:T(8,128)(2,1)}, bf16[512,1408]{1,0:T(8,128)(2,1)}, u32[]{:S(2)}, u32[]{:S(2)}) collective-permute-start(bf16[512,1408]{1,0:T(8,128)(2,1)} %slice.631), channel_id=1, source_target_pairs={{0,2},{1,3},{2,0},{3,1},{4,6},{5,7},{6,4},{7,5},{8,10},{9,11},{10,... | collective-permute-start | bytes 4325384 | tf_op jit(solution)/shard_map/ppermute | solution.py:137
  782.1 29.1 %collective-permute-start.34 = (bf16[256,1408]{1,0:T(8,128)(2,1)S(1)}, bf16[256,1408]{1,0:T(8,128)(2,1)S(1)}, u32[]{:S(2)}, u32[]{:S(2)}) collective-permute-start(bf16[256,1408]{1,0:T(8,128)(2,1)S(1)} %slice.634), channel_id=1, source_target_pairs={{0,2},{1,3},{2,0},{3,1},{4,6},{5,7},{6,4},{7,5},{8,10},{9,11},{10,... | collective-permute-start | bytes 2162696 | tf_op jit(solution)/shard_map/ppermute | solution.py:137
  806.0 27.0 %collective-permute-start.56 = (bf16[176,3072]{1,0:T(8,128)(2,1)S(1)}, bf16[176,3072]{1,0:T(8,128)(2,1)S(1)}, u32[]{:S(2)}, u32[]{:S(2)}) collective-permute-start(bf16[176,3072]{1,0:T(8,128)(2,1)S(1)} %dynamic-slice_bitcast_fusion.7), channel_id=1, source_target_pairs={{0,8},{1,9},{2,10},{3,11},{4,12},{5,13},{6,14},{7,15},{8,16},{9,17... | collective-permute-start | bytes 3244040 | tf_op jit(solution)/shard_map/ppermute | solution.py:137
  811.2 23.4 %collective-permute-start.39 = (bf16[512,1408]{1,0:T(8,128)(2,1)S(1)}, bf16[512,1408]{1,0:T(8,128)(2,1)S(1)}, u32[]{:S(2)}, u32[]{:S(2)}) collective-permute-start(bf16[512,1408]{1,0:T(8,128)(2,1)S(1)} %get-tuple-element.125), channel_id=1, source_target_pairs={{0,1},{1,0},{2,3},{3,2},{4,5},{5,4},{6,7},{7,6},{8,9},{9,8},{10,11... | collective-permute-start | bytes 4325384 | tf_op jit(solution)/shard_map/ppermute | solution.py:137
  834.4 87.7 %collective-permute-start.57 = (bf16[176,3072]{1,0:T(8,128)(2,1)}, bf16[176,3072]{1,0:T(8,128)(2,1)}, u32[]{:S(2)}, u32[]{:S(2)}) collective-permute-start(bf16[176,3072]{1,0:T(8,128)(2,1)} %fusion.62), channel_id=1, source_target_pairs={{0,8},{1,9},{2,10},{3,11},{4,12},{5,13},{6,14},{7,15},{8,16},{9,17... | collective-permute-start | bytes 3244040 | tf_op jit(solution)/shard_map/ppermute | solution.py:137
  898.9 26.7 %collective-permute-start.40 = (bf16[512,1408]{1,0:T(8,128)(2,1)}, bf16[512,1408]{1,0:T(8,128)(2,1)}, u32[]{:S(2)}, u32[]{:S(2)}) collective-permute-start(bf16[512,1408]{1,0:T(8,128)(2,1)} %slice.629), channel_id=1, source_target_pairs={{0,1},{1,0},{2,3},{3,2},{4,5},{5,4},{6,7},{7,6},{8,9},{9,8},{10,11... | collective-permute-start | bytes 4325384 | tf_op jit(solution)/shard_map/ppermute | solution.py:137
  920.6 243.4 %collective-permute-start.50 = (bf16[2,4,304,704]{3,2,0,1:T(8,128)(2,1)}, bf16[2,4,304,704]{3,2,0,1:T(8,128)(2,1)}, u32[]{:S(2)}, u32[]{:S(2)}) collective-permute-start(bf16[2,4,304,704]{3,2,0,1:T(8,128)(2,1)} %fusion.47), channel_id=1, source_target_pairs={{0,4},{1,5},{2,6},{3,7},{4,0},{5,1},{6,2},{7,3},{8,12},{9,13},{10,... | collective-permute-start | bytes 10272776 | tf_op jit(solution)/shard_map/ppermute | solution.py:137
  924.1 28.1 %collective-permute-start.58 = (bf16[176,3072]{1,0:T(8,128)(2,1)S(1)}, bf16[176,3072]{1,0:T(8,128)(2,1)S(1)}, u32[]{:S(2)}, u32[]{:S(2)}) collective-permute-start(bf16[176,3072]{1,0:T(8,128)(2,1)S(1)} %fusion.61), channel_id=1, source_target_pairs={{0,8},{1,9},{2,10},{3,11},{4,12},{5,13},{6,14},{7,15},{8,16},{9,17... | collective-permute-start | bytes 3244040 | tf_op jit(solution)/shard_map/ppermute | solution.py:137
  932.3 26.0 %collective-permute-start.41 = (bf16[512,1408]{1,0:T(8,128)(2,1)S(1)}, bf16[512,1408]{1,0:T(8,128)(2,1)S(1)}, u32[]{:S(2)}, u32[]{:S(2)}) collective-permute-start(bf16[512,1408]{1,0:T(8,128)(2,1)S(1)} %fusion.102), channel_id=1, source_target_pairs={{0,1},{1,0},{2,3},{3,2},{4,5},{5,4},{6,7},{7,6},{8,9},{9,8},{10,11... | collective-permute-start | bytes 4325384 | tf_op jit(solution)/shard_map/ppermute | solution.py:137
  1156.0 40.4 %collective-permute-start.42 = (bf16[512,1408]{1,0:T(8,128)(2,1)}, bf16[512,1408]{1,0:T(8,128)(2,1)S(1)}, u32[]{:S(2)}, u32[]{:S(2)}) collective-permute-start(bf16[512,1408]{1,0:T(8,128)(2,1)} %slice.628), channel_id=1, source_target_pairs={{0,1},{1,0},{2,3},{3,2},{4,5},{5,4},{6,7},{7,6},{8,9},{9,8},{10,11... | collective-permute-start | bytes 4325384 | tf_op jit(solution)/shard_map/ppermute | solution.py:137
  1170.1 24.5 %collective-permute-start.51 = (bf16[2,304,704]{2,1,0:T(8,128)(2,1)}, bf16[2,304,704]{2,1,0:T(8,128)(2,1)}, u32[]{:S(2)}, u32[]{:S(2)}) collective-permute-start(bf16[2,304,704]{2,1,0:T(8,128)(2,1)} %dynamic-slice_bitcast_fusion.9), channel_id=1, source_target_pairs={{0,8},{1,9},{2,10},{3,11},{4,12},{5,13},{6,14},{7,15},{8,16},{9,17... | collective-permute-start | bytes 2568200 | tf_op jit(solution)/shard_map/ppermute | solution.py:137
  1182.9 114.5 %collective-permute-start.45 = (bf16[4,2,176,1408]{3,2,1,0:T(8,128)(2,1)}, bf16[4,2,176,1408]{3,2,1,0:T(8,128)(2,1)}, u32[]{:S(2)}, u32[]{:S(2)}) collective-permute-start(bf16[4,2,176,1408]{3,2,1,0:T(8,128)(2,1)} %bitcast.483), channel_id=1, source_target_pairs={{0,2},{1,3},{2,0},{3,1},{4,6},{5,7},{6,4},{7,5},{8,10},{9,11},{10,... | collective-permute-start | bytes 11894792 | tf_op jit(solution)/shard_map/ppermute | solution.py:137
  1196.3 98.9 %collective-permute-start.52 = (bf16[2,304,704]{2,1,0:T(8,128)(2,1)S(1)}, bf16[2,304,704]{2,1,0:T(8,128)(2,1)}, u32[]{:S(2)}, u32[]{:S(2)}) collective-permute-start(bf16[2,304,704]{2,1,0:T(8,128)(2,1)S(1)} %fusion.67), channel_id=1, source_target_pairs={{0,8},{1,9},{2,10},{3,11},{4,12},{5,13},{6,14},{7,15},{8,16},{9,17... | collective-permute-start | bytes 2568200 | tf_op jit(solution)/shard_map/ppermute | solution.py:137
  1217.6 11.7 collective-permute-start.67
  1228.8 74.7 %collective-permute-start.59 = (bf16[8,2,88,1408]{3,2,1,0:T(8,128)(2,1)}, bf16[8,2,88,1408]{3,2,1,0:T(8,128)(2,1)}, u32[]{:S(2)}, u32[]{:S(2)}) collective-permute-start(bf16[8,2,88,1408]{3,2,1,0:T(8,128)(2,1)} %dynamic-slice_bitcast_fusion.1), channel_id=1, source_target_pairs={{0,1},{1,0},{2,3},{3,2},{4,5},{5,4},{6,7},{7,6},{8,9},{9,8},{10,11... | collective-permute-start | bytes 11894792 | tf_op jit(solution)/shard_map/ppermute | solution.py:137
  1229.3 43.9 %collective-permute-start.68 = (f32[22,1408]{1,0:T(8,128)S(1)}, f32[22,1408]{1,0:T(8,128)S(1)}, u32[]{:S(2)}, u32[]{:S(2)}) collective-permute-start(f32[22,1408]{1,0:T(8,128)S(1)} %add.789), channel_id=1, source_target_pairs={{0,2},{1,3},{2,0},{3,1},{4,6},{5,7},{6,4},{7,5},{8,10},{9,11},{10,... | collective-permute-start | bytes 371720 | tf_op jit(solution)/shard_map/ppermute | solution.py:137
  1282.5 160.5 %collective-permute-start.44 = (bf16[256,1408]{1,0:T(8,128)(2,1)}, bf16[256,1408]{1,0:T(8,128)(2,1)}, u32[]{:S(2)}, u32[]{:S(2)}) collective-permute-start(bf16[256,1408]{1,0:T(8,128)(2,1)} %get-tuple-element.160), channel_id=1, source_target_pairs={{0,2},{1,3},{2,0},{3,1},{4,6},{5,7},{6,4},{7,5},{8,10},{9,11},{10,... | collective-permute-start | bytes 2162696 | tf_op jit(solution)/shard_map/ppermute | solution.py:137
  1293.1 154.0 %collective-permute-start.43 = (bf16[256,1408]{1,0:T(8,128)(2,1)}, bf16[256,1408]{1,0:T(8,128)(2,1)}, u32[]{:S(2)}, u32[]{:S(2)}) collective-permute-start(bf16[256,1408]{1,0:T(8,128)(2,1)} %get-tuple-element.161), channel_id=1, source_target_pairs={{0,2},{1,3},{2,0},{3,1},{4,6},{5,7},{6,4},{7,5},{8,10},{9,11},{10,... | collective-permute-start | bytes 2162696 | tf_op jit(solution)/shard_map/ppermute | solution.py:137
  1297.0 20.6 %collective-permute-start.53 = (bf16[2,304,704]{2,1,0:T(8,128)(2,1)S(1)}, bf16[2,304,704]{2,1,0:T(8,128)(2,1)S(1)}, u32[]{:S(2)}, u32[]{:S(2)}) collective-permute-start(bf16[2,304,704]{2,1,0:T(8,128)(2,1)S(1)} %fusion.66), channel_id=1, source_target_pairs={{0,8},{1,9},{2,10},{3,11},{4,12},{5,13},{6,14},{7,15},{8,16},{9,17... | collective-permute-start | bytes 2568200 | tf_op jit(solution)/shard_map/ppermute | solution.py:137
  1302.9 41.5 %collective-permute-start.46 = (bf16[4,176,1408]{2,1,0:T(8,128)(2,1)S(1)}, bf16[4,176,1408]{2,1,0:T(8,128)(2,1)S(1)}, u32[]{:S(2)}, u32[]{:S(2)}) collective-permute-start(bf16[4,176,1408]{2,1,0:T(8,128)(2,1)S(1)} %dynamic-slice_bitcast_fusion.3), channel_id=1, source_target_pairs={{0,4},{1,5},{2,6},{3,7},{4,0},{5,1},{6,2},{7,3},{8,12},{9,13},{10,... | collective-permute-start | bytes 5947400 | tf_op jit(solution)/shard_map/ppermute | solution.py:137
  1306.9 52.8 %collective-permute-start.60 = (bf16[8,88,1408]{2,1,0:T(8,128)(2,1)S(1)}, bf16[8,88,1408]{2,1,0:T(8,128)(2,1)S(1)}, u32[]{:S(2)}, u32[]{:S(2)}) collective-permute-start(bf16[8,88,1408]{2,1,0:T(8,128)(2,1)S(1)} %dynamic-slice_bitcast_fusion.2), channel_id=1, source_target_pairs={{0,2},{1,3},{2,0},{3,1},{4,6},{5,7},{6,4},{7,5},{8,10},{9,11},{10,... | collective-permute-start | bytes 5947400 | tf_op jit(solution)/shard_map/ppermute | solution.py:137
  1319.1 47.7 %collective-permute-start.54 = (bf16[304,704]{1,0:T(8,128)(2,1)S(1)}, bf16[304,704]{1,0:T(8,128)(2,1)S(1)}, u32[]{:S(2)}, u32[]{:S(2)}) collective-permute-start(bf16[304,704]{1,0:T(8,128)(2,1)S(1)} %slice_bitcast_fusion.4), channel_id=1, source_target_pairs={{0,2},{1,3},{2,0},{3,1},{4,6},{5,7},{6,4},{7,5},{8,10},{9,11},{10,... | collective-permute-start | bytes 1284104 | tf_op jit(solution)/shard_map/ppermute | solution.py:137
  1362.5 18.4 %collective-permute-start.61 = (bf16[4,88,1408]{2,1,0:T(8,128)(2,1)}, bf16[4,88,1408]{2,1,0:T(8,128)(2,1)}, u32[]{:S(2)}, u32[]{:S(2)}) collective-permute-start(bf16[4,88,1408]{2,1,0:T(8,128)(2,1)} %dynamic-slice_bitcast_fusion.8), channel_id=1, source_target_pairs={{0,4},{1,5},{2,6},{3,7},{4,0},{5,1},{6,2},{7,3},{8,12},{9,13},{10,... | collective-permute-start | bytes 2973704 | tf_op jit(solution)/shard_map/ppermute | solution.py:137
  1363.8 12.4 collective-permute-start.47
  1377.4 18.2 %collective-permute-start.48 = (bf16[176,1408]{1,0:T(8,128)(2,1)S(1)}, bf16[176,1408]{1,0:T(8,128)(2,1)S(1)}, u32[]{:S(2)}, u32[]{:S(2)}) collective-permute-start(bf16[176,1408]{1,0:T(8,128)(2,1)S(1)} %fusion.94), channel_id=1, source_target_pairs={{0,8},{1,9},{2,10},{3,11},{4,12},{5,13},{6,14},{7,15},{8,16},{9,17... | collective-permute-start | bytes 1486856 | tf_op jit(solution)/shard_map/ppermute | solution.py:137
  1382.7 11.5 collective-permute-start.62
  1394.2 10.5 collective-permute-start.63
  1395.8 14.4 collective-permute-start.49
  1405.5 8.5 collective-permute-start.64
  1418.4 13.7 collective-permute-start.66
  (282 other events, 3355.1 us)

commit v2 on v1

--- a/solution.py
+++ b/solution.py
@@ -1,9 +1,12 @@
 from functools import partial
+import itertools
 import math
 
 import jax
 import jax.numpy as jnp
 from jax import lax
+from jax.experimental import pallas as pl
+from jax.experimental.pallas import tpu as pltpu
 from jax.sharding import PartitionSpec as P
 
 D = 1408
@@ -19,6 +22,9 @@
 learn_rate = 0.3
 step_count = 10.0
 
+BF16 = jnp.bfloat16
+F32 = jnp.float32
+
 
 def matmul(left, right):
     return jnp.dot(left, right, preferred_element_type=jnp.float32)
@@ -42,22 +48,18 @@
     return center * lax.rsqrt(spread + norm_eps) * factor
 
 
-def rotate_pairs(values, cosines, sines):
-    layout = values.shape
-    paired = values.reshape(layout[:-1] + (layout[-1] // 2, 2))
-    turned = jnp.stack([-paired[..., 1], paired[..., 0]], -1).reshape(layout)
-    return values * cosines + turned * sines
-
-
-def rotary_tables(patch_order):
-    grid_row = (patch_order // GRID).astype(jnp.float32)
-    grid_col = (patch_order % GRID).astype(jnp.float32)
+def rotary_tables(places):
+    grid_row = (places // GRID).astype(jnp.float32)
+    grid_col = (places % GRID).astype(jnp.float32)
     quarter = HD // 4
     spacing = 10000.0 ** (-jnp.arange(quarter).astype(jnp.float32) / quarter)
     row_angle = jnp.repeat(grid_row[:, None] * spacing[None, :], 2, axis=1)
     col_angle = jnp.repeat(grid_col[:, None] * spacing[None, :], 2, axis=1)
     angles = jnp.concatenate([row_angle, col_angle], 1)
-    return (jnp.cos(angles)[:, None, :], jnp.sin(angles)[:, None, :])
+    even = jnp.arange(HD) % 2 == 0
+    sines = jnp.sin(angles)
+    tables = (jnp.cos(angles), jnp.where(even, -sines, 0.0), jnp.where(even, 0.0, sines))
+    return tuple(jnp.pad(table, ((0, 0), (0, LANES - HD))) for table in tables)
 
 
 def time_embed(timesteps):
@@ -67,54 +69,206 @@
     return jnp.concatenate([jnp.cos(angles), jnp.sin(angles)], -1)
 
 
-def rope_heads(pre, factor, cosines, sines):
-    return rotate_pairs(norm_rows(pre.reshape(pre.shape[0], -1, HD), factor), cosines, sines)
-
-
-def plain_heads(pre, factor):
-    return norm_rows(pre.reshape(pre.shape[0], -1, HD), factor)
-
-
 def gelu_tanh(values):
     return jax.nn.gelu(values, approximate=True)
 
 
-def attend(query, keys, values):
-    factor = HD ** (-0.5)
-    scores = jnp.einsum("qhd,khd->hqk", query, keys, preferred_element_type=jnp.float32) * factor
-    highest = jnp.max(scores, axis=-1, keepdims=True)
-    raised = jnp.exp(scores - highest)
-    summed = jnp.sum(raised, axis=-1, keepdims=True)
-    chances = raised / summed
-    log_total = highest + jnp.log(summed)
-    mixed = jnp.einsum(
-        "hqk,khd->qhd", chances.astype(jnp.bfloat16), values, preferred_element_type=jnp.float32
-    )
-    return (mixed.astype(jnp.bfloat16), log_total)
-
-
-def attend_back(query, keys, values, log_total, mixed_grad):
-    factor = HD ** (-0.5)
-    scores = jnp.einsum("qhd,khd->hqk", query, keys, preferred_element_type=jnp.float32) * factor
-    chances = jnp.exp(scores - log_total)
-    chance_grad = jnp.einsum("qhd,khd->hqk", mixed_grad, values, preferred_element_type=jnp.float32)
-    centre = jnp.sum(chance_grad * chances, axis=-1, keepdims=True)
-    score_grad = (chances * (chance_grad - centre)).astype(jnp.bfloat16)
-    query_grad = (
-        jnp.einsum("hqk,khd->qhd", score_grad, keys, preferred_element_type=jnp.float32) * factor
-    )
-    keys_grad = (
-        jnp.einsum("hqk,qhd->khd", score_grad, query, preferred_element_type=jnp.float32) * factor
-    )
-    values_grad = jnp.einsum(
-        "hqk,qhd->khd", chances.astype(jnp.bfloat16), mixed_grad, preferred_element_type=jnp.float32
-    )
-    return (query_grad, keys_grad, values_grad)
+LANES = 128
+Q_SCALE = math.log2(math.e) * HD**-0.5
+FAR = -10000.0
+
+
+def head_slice(ref, at):
+    width = ref.shape[1]
+    if at + LANES <= width:
+        values = ref[:, at : at + LANES]
+    else:
+        values = pltpu.roll(ref[:, width - LANES :], width - at, 1)
+    return jnp.where(lanes_of(values) < HD, values, 0.0)
+
+
+def lanes_of(values):
+    return lax.broadcasted_iota(jnp.int32, values.shape, 1)
+
+
+def head_norm(pre):
+    mean = jnp.sum(pre, axis=1, keepdims=True) * (1.0 / HD)
+    center = jnp.where(lanes_of(pre) < HD, pre - mean, 0.0)
+    spread = jnp.sum(center * center, axis=1, keepdims=True) * (1.0 / HD)
+    scale = lax.rsqrt(spread + norm_eps)
+    return center * scale, scale
+
+
+def turn(values, tables):
+    cosines, after, before = (table[...] for table in tables)
+    return (
+        values * cosines
+        + pltpu.roll(values, LANES - 1, 1) * after
+        + pltpu.roll(values, 1, 1) * before
+    )
+
+
+def turn_back(grads, tables):
+    cosines, after, before = (table[...] for table in tables)
+    return (
+        grads * cosines
+        + pltpu.roll(grads * after, 1, 1)
+        + pltpu.roll(grads * before, LANES - 1, 1)
+    )
+
+
+def head_norm_back(grads, gain, normed, scale):
+    gain_grad = jnp.sum(grads * normed, axis=0, keepdims=True)
+    grads = grads * gain
+    mean = jnp.sum(grads, axis=1, keepdims=True) * (1.0 / HD)
+    along = jnp.sum(grads * normed, axis=1, keepdims=True) * (1.0 / HD)
+    back = scale * (grads - mean - normed * along)
+    return jnp.where(lanes_of(back) < HD, back, 0.0), gain_grad
+
+
+def dot_nt(left, right):
+    return lax.dot_general(left, right, (((1,), (1,)), ((), ())), preferred_element_type=F32)
+
+
+def with_pair(values, column, lanes):
+    high = column.astype(BF16).astype(F32)
+    return jnp.where(lanes == HD, high, jnp.where(lanes == HD + 1, column - high, values))
+
+
+def attend_kernel(heads, q_at, k_at, v_at, one_pre, key_rows, *refs):
+    if one_pre:
+        refs = (refs[0],) + refs
+    q_ref, kv_ref, gain_ref, cos_ref, after_ref, before_ref = refs[:6]
+    out_ref, q_ext_ref, k_ext_ref, v_ext_ref, flat_ref = refs[6:]
+    tables = (cos_ref, after_ref, before_ref)
+    rows, keys_count = q_ref.shape[0], kv_ref.shape[0]
+    step = min(rows, 256)
+    for h in range(heads):
+        ext = slice(h * LANES, (h + 1) * LANES)
+        normed, _ = head_norm(head_slice(q_ref, q_at + h * HD))
+        lanes = lanes_of(normed)
+        query = turn(normed * gain_ref[0:1], tables) * Q_SCALE
+        query = jnp.where(lanes == HD + 2, FAR, query)
+        q_ext_ref[:, ext] = query.astype(BF16)
+        normed, _ = head_norm(head_slice(kv_ref, k_at + h * HD))
+        keys = normed * gain_ref[1:2]
+        if one_pre:
+            keys = turn(keys, tables)
+        lanes = lanes_of(keys)
+        keys = jnp.where((lanes == HD) | (lanes == HD + 1), 1.0, keys)
+        if key_rows < keys_count:
+            places = lax.broadcasted_iota(jnp.int32, keys.shape, 0)
+            keys = jnp.where((lanes == HD + 2) & (places >= key_rows), 1.0, keys)
+        keys16 = keys.astype(BF16)
+        k_ext_ref[:, ext] = keys16
+        values = head_slice(kv_ref, v_at + h * HD)
+        values16 = jnp.where((lanes == HD) | (lanes == HD + 1), 1.0, values).astype(BF16)
+        v_ext_ref[:, ext] = values16
+        for at in range(0, rows, step):
+            part = slice(at, at + step)
+            query16 = q_ext_ref[part, ext]
+            raised = jnp.exp2(dot_nt(query16, keys16)).astype(BF16)
+            mixed = jnp.dot(raised, values16, preferred_element_type=F32)
+            total = mixed[:, HD : HD + 1]
+            mixed = mixed * (1.0 / total)
+            flat_ref[part, h * HD : (h + 1) * HD] = mixed[:, :HD]
+            query = query16.astype(F32)
+            query = with_pair(query, -jnp.log2(total), lanes_of(query))
+            q_ext_ref[part, ext] = query.astype(BF16)
+    out_ref[...] = flat_ref[...].astype(BF16)
+
+
+def attend_back_kernel(heads, q_at, k_at, v_at, one_pre, *refs):
+    if one_pre:
+        refs = (refs[0],) + refs
+    q_ref, kv_ref, gain_ref, cos_ref, after_ref, before_ref = refs[:6]
+    out_ref, grad_ref, q_ext_ref, k_ext_ref, v_ext_ref = refs[6:11]
+    if one_pre:
+        pre_grad_ref, gain_grad_ref, flat_ref, out_flat, grad_flat = refs[11:]
+        q_flat = kv_flat = flat_ref
+    else:
+        q_grad_ref, kv_grad_ref, gain_grad_ref, q_flat, kv_flat, out_flat, grad_flat = refs[11:]
+    tables = (cos_ref, after_ref, before_ref)
+    rows, keys_count = q_ref.shape[0], kv_ref.shape[0]
+    step = 256 if keys_count % 256 == 0 else keys_count
+    out_flat[...] = out_ref[...].astype(F32)
+    grad_flat[...] = grad_ref[...].astype(F32)
+    q_gain = jnp.zeros((1, LANES), F32)
+    k_gain = jnp.zeros((1, LANES), F32)
+    for h in range(heads):
+        ext = slice(h * LANES, (h + 1) * LANES)
+        grad = head_slice(grad_flat, h * HD)
+        delta = jnp.sum(grad * head_slice(out_flat, h * HD), axis=1, keepdims=True)
+        grad16 = with_pair(grad, -delta, lanes_of(grad)).astype(BF16)
+        query16 = q_ext_ref[:, ext]
+        query_grad = jnp.zeros((LANES, rows), F32)
+        keys_grad = []
+        for at in range(0, keys_count, step):
+            part = slice(at, at + step)
+            keys16, values16 = k_ext_ref[part, ext], v_ext_ref[part, ext]
+            chances = jnp.exp2(dot_nt(keys16, query16))
+            score_grad = (chances * dot_nt(values16, grad16)).astype(BF16)
+            value_grad = jnp.dot(chances.astype(BF16), grad16, preferred_element_type=F32)
+            kv_flat[part, v_at + h * HD : v_at + (h + 1) * HD] = value_grad[:, :HD]
+            keys_grad.append(jnp.dot(score_grad, query16, preferred_element_type=F32))
+            query_grad = query_grad + lax.dot_general(
+                keys16, score_grad, (((0,), (0,)), ((), ())), preferred_element_type=F32
+            )
+        query_grad = query_grad.T * (HD**-0.5)
+        normed, scale = head_norm(head_slice(q_ref, q_at + h * HD))
+        query_grad = jnp.where(lanes_of(query_grad) < HD, query_grad, 0.0)
+        back, gain_grad = head_norm_back(turn_back(query_grad, tables), gain_ref[0:1], normed, scale)
+        q_gain = q_gain + gain_grad
+        q_flat[:, q_at + h * HD : q_at + (h + 1) * HD] = back[:, :HD]
+        key_grad = jnp.concatenate(keys_grad, 0) * math.log(2.0)
+        key_grad = jnp.where(lanes_of(key_grad) < HD, key_grad, 0.0)
+        if one_pre:
+            key_grad = turn_back(key_grad, tables)
+        normed, scale = head_norm(head_slice(kv_ref, k_at + h * HD))
+        back, gain_grad = head_norm_back(key_grad, gain_ref[1:2], normed, scale)
+        k_gain = k_gain + gain_grad
+        kv_flat[:, k_at + h * HD : k_at + (h + 1) * HD] = back[:, :HD]
+    gain_grad_ref[...] = jnp.concatenate([q_gain, k_gain, jnp.zeros((6, LANES), F32)], 0)
+    if one_pre:
+        pre_grad_ref[...] = flat_ref[...].astype(BF16)
+    else:
+        q_grad_ref[...] = q_flat[...].astype(BF16)
+        kv_grad_ref[...] = kv_flat[...].astype(BF16)
+
+
+VMEM_LIMIT = 60 * 1024 * 1024
+
+
+def attend(pres, gains, tables, heads, places, key_rows):
+    rows, keys_count = pres[0].shape[0], pres[-1].shape[0]
+    return pl.pallas_call(
+        partial(attend_kernel, heads, *places, len(pres) == 1, key_rows),
+        out_shape=(
+            jax.ShapeDtypeStruct((rows, heads * HD), BF16),
+            jax.ShapeDtypeStruct((rows, heads * LANES), BF16),
+            jax.ShapeDtypeStruct((keys_count, heads * LANES), BF16),
+            jax.ShapeDtypeStruct((keys_count, heads * LANES), BF16),
+        ),
+        scratch_shapes=[pltpu.VMEM((rows, heads * HD), F32)],
+        compiler_params=pltpu.CompilerParams(vmem_limit_bytes=VMEM_LIMIT),
+        cost_estimate=pl.CostEstimate(flops=0, bytes_accessed=0, transcendentals=0),
+    )(*pres, gains, *tables)
+
+
+def attend_back(pres, gains, tables, kept, out_grad, heads, places):
+    rows, keys_count = pres[0].shape[0], pres[-1].shape[0]
+    return pl.pallas_call(
+        partial(attend_back_kernel, heads, *places, len(pres) == 1),
+        out_shape=tuple(jax.ShapeDtypeStruct(pre.shape, BF16) for pre in pres)
+        + (jax.ShapeDtypeStruct((8, LANES), F32),),
+        scratch_shapes=[pltpu.VMEM(pre.shape, F32) for pre in pres]
+        + [pltpu.VMEM((rows, heads * HD), F32)] * 2,
+        compiler_params=pltpu.CompilerParams(vmem_limit_bytes=VMEM_LIMIT),
+        cost_estimate=pl.CostEstimate(flops=0, bytes_accessed=0, transcendentals=0),
+    )(*pres, gains, *tables, kept[0], out_grad, *kept[1:])
 
 
 AXES = ("dp", "tensor")
-BF16 = jnp.bfloat16
-F32 = jnp.float32
 
 
 def digits_of(count):
@@ -145,58 +299,264 @@
     return send(values, lambda d, t: (d, t ^ 2))
 
 
-class Digit:
-    def __init__(self, sizes, at):
-        self.size = sizes[at]
-        self.stride = math.prod(sizes[at + 1 :])
-        self.at = at
-        self.mine = (lax.axis_index("dp") // self.stride) % self.size
-
-    def step(self, values):
+def after(values, *others):
+    return lax.optimization_barrier((values, others))[0]
+
+
+def plan(sizes):
+    nodes = list(itertools.product(*map(range, sizes)))
+    have, left, steps = {nodes[0]}, nodes[1:], []
+
+    def ways(node):
+        return [ring for ring in range(len(sizes)) if node[ring] and before(node, ring) in have]
+
+    while left:
+        step, taken = [], set()
+        for ring in range(len(sizes)):
+            ready = [node for node in left if node not in taken and ring in ways(node)]
+            if ready:
+                node = min(ready, key=lambda n: (len(ways(n)), -n[0] if ring == 0 else n[0], n))
+                step.append((ring, node))
+                taken.add(node)
+        have |= taken
+        left = [node for node in left if node not in taken]
+        steps.append(step)
+    return steps
+
+
+def before(node, ring):
+    return node[:ring] + (node[ring] - 1,) + node[ring + 1 :]
+
+
+class Grid:
+    def __init__(self, sizes, with_y):
+        self.sizes = sizes
+        self.with_y = with_y
+        self.strides = [math.prod(sizes[at + 1 :]) for at in range(len(sizes))]
+        me = lax.axis_index("dp")
+        self.mine = [(me // stride) % size for size, stride in zip(sizes, self.strides)]
+        self.steps = plan(sizes + ((2,) if with_y else ()))
+        self.nodes = list(itertools.product(*map(range, sizes + ((2,) if with_y else ()))))
+
+    def shift(self, values, ring, by):
+        if ring == len(self.sizes):
+            return swap_y(values)
+        size, stride = self.sizes[ring], self.strides[ring]
+
         def move(d, t):
-            digit = (d // self.stride) % self.size
-            return (d + ((digit + 1) % self.size - digit) * self.stride, t)
+            digit = (d // stride) % size
+            return (d + ((digit + by) % size - digit) * stride, t)
 
         return send(values, move)
 
-
-def gather_digits(piece, digits, lead=0):
-    done = []
-    for digit in digits:
-        axis = lead + sum(1 for other in done if other < digit.at)
-        shape = piece.shape[:axis] + (digit.size,) + piece.shape[axis:]
-        whole = jnp.zeros(shape, piece.dtype)
-        for k in range(digit.size):
-            if k:
-                piece = digit.step(piece)
-            place = (digit.mine - k) % digit.size
-            whole = lax.dynamic_update_index_in_dim(whole, piece, place, axis)
-        piece = whole
-        done.append(digit.at)
-    return piece
+    def owner(self, node):
+        return sum(
+            ((mine - far) % size) * stride
+            for mine, far, size, stride in zip(self.mine, node, self.sizes, self.strides)
+        )
+
+
+def place_kernel(count, axis, spots_ref, *refs):
+    sources, (out_ref, held_ref, in_sems, out_sems) = refs[:count], refs[count:]
+    before_axis = (slice(None),) * axis
+    reads = [
+        pltpu.make_async_copy(source, held_ref.at[k], in_sems.at[k])
+        for k, source in enumerate(sources)
+    ]
+    writes = [
+        pltpu.make_async_copy(held_ref.at[k], out_ref.at[before_axis + (spots_ref[k],)], out_sems.at[k])
+        for k in range(count)
+    ]
+    for read in reads:
+        read.start()
+    for read, write in zip(reads, writes):
+        read.wait()
+        write.start()
+    for write in writes:
+        write.wait()
+
+
+def place(pieces, spots, axis=0):
+    count = len(pieces)
+    shape = pieces[0].shape
+    return pl.pallas_call(
+        partial(place_kernel, count, axis),
+        out_shape=jax.ShapeDtypeStruct(shape[:axis] + (count,) + shape[axis:], pieces[0].dtype),
+        in_specs=[pl.BlockSpec(memory_space=pltpu.SMEM)]
+        + [pl.BlockSpec(memory_space=pl.ANY)] * count,
+        out_specs=pl.BlockSpec(memory_space=pl.ANY),
+        scratch_shapes=[
+            pltpu.VMEM((count,) + pieces[0].shape, pieces[0].dtype),
+            pltpu.SemaphoreType.DMA((count,)),
+            pltpu.SemaphoreType.DMA((count,)),
+        ],
+        compiler_params=pltpu.CompilerParams(vmem_limit_bytes=VMEM_LIMIT),
+        cost_estimate=pl.CostEstimate(flops=0, bytes_accessed=0, transcendentals=0),
+    )(jnp.stack([jnp.asarray(spot, jnp.int32) for spot in spots]), *pieces)
+
+
+class Fetch:
+    def __init__(self, grid, piece):
+        self.grid = grid
+        self.got = {grid.nodes[0]: piece}
+        self.small = math.prod(grid.sizes) <= 8
+        self.todo = list(grid.steps) if self.small else []
+
+    def advance(self, *waits):
+        new = {}
+        if self.todo:
+            for ring, node in self.todo.pop(0):
+                source = self.got[before(node, ring)]
+                source = after(source, *waits) if waits else source
+                new[node] = self.grid.shift(source, ring, 1)
+        self.got.update(new)
+        return tuple(new.values())
+
+    def finish(self):
+        grid, piece = self.grid, self.got[self.grid.nodes[0]]
+        if not self.small:
+            whole = lax.all_gather(piece, "dp")
+            return jnp.stack([whole, swap_y(whole)]) if grid.with_y else whole
+        count = math.prod(grid.sizes)
+        spots = [grid.owner(node) + (node[-1] * count if grid.with_y else 0) for node in grid.nodes]
+        whole = place([self.got[node] for node in grid.nodes], spots)
+        return whole.reshape((2, count) + piece.shape) if grid.with_y else whole
+
+
+class Sequence:
+    def __init__(self):
+        self.came = ()
+
+    def run(self, *jobs, since=()):
+        waits = self.came + tuple(since)
+        self.came = tuple(got for job in jobs for got in job.advance(*waits))
+        return self.came
+
+
+class Reduction:
+    def __init__(self, grid, part, last=F32):
+        self.grid, self.part, self.last = grid, part, last
+        self.small = math.prod(grid.sizes) <= 8
+        self.sums = {node: [] for node in grid.nodes}
+        self.todo = list(reversed(grid.steps)) if self.small else []
+
+    def total(self, node, dtype):
+        dp_index = self.grid.owner(node)
+        value = self.part(dp_index, node[-1] if self.grid.with_y else 0).astype(F32)
+        for got in self.sums[node]:
+            value = value + got.astype(F32)
+        return value.astype(dtype)
+
+    def advance(self, *waits):
+        came = []
+        if self.todo:
+            for ring, node in self.todo.pop(0):
+                moving = self.total(node, BF16)
+                moving = after(moving, *waits) if waits else moving
+                got = self.grid.shift(moving, ring, -1)
+                self.sums[before(node, ring)].append(got)
+                came.append(got)
+        return came
+
+    def finish(self):
+        while self.todo:
+            self.advance()
+        if self.small:
+            return self.total(self.grid.nodes[0], self.last)
+        count = math.prod(self.grid.sizes)
+        blocks = []
+        for far in range(2 if self.grid.with_y else 1):
+            whole = jnp.stack([self.part(k, far) for k in range(count)]).astype(F32)
+            whole = lax.psum_scatter(whole, "dp", scatter_dimension=0, tiled=False)
+            blocks.append(whole)
+        if self.grid.with_y:
+            return (blocks[0] + swap_y(blocks[1].astype(BF16)).astype(F32)).astype(self.last)
+        return blocks[0].astype(self.last)
+
+
+def mlp_kernel(half_steps, x_ref, grad_ref, mats_ref, act_ref, inner_grad_ref, *part_refs):
+    hidden = act_ref.shape[1]
+    inner_mat, outer_mat = mats_ref[:, :hidden], mats_ref[:, hidden:]
+    inner = jnp.dot(x_ref[...], inner_mat, preferred_element_type=F32)
+    grad = jnp.dot(grad_ref[...], outer_mat, preferred_element_type=F32)
+    square = inner * inner
+    bend = math.sqrt(2.0 / math.pi)
+    turned = jnp.tanh(inner * (bend + (bend * 0.044715) * square))
+    rise = 0.5 + 0.5 * turned
+    slope = rise + (0.5 * inner) * (1.0 - turned * turned) * (bend + (bend * 3 * 0.044715) * square)
+    act_ref[...] = (inner * rise).astype(BF16)
+    inner_grad_ref[...] = (grad * slope).astype(BF16)
+    out = dot_nt(act_ref[...], outer_mat).astype(BF16)
+    in_grad = dot_nt(inner_grad_ref[...], inner_mat).astype(BF16)
+    first = pl.program_id(0) < half_steps
+
+    @pl.when(first)
+    def _():
+        part_refs[0][...] = out
+        part_refs[1][...] = in_grad
+
+    @pl.when(jnp.logical_not(first))
+    def _():
+        part_refs[2][...] = out
+        part_refs[3][...] = in_grad
+
+
+def mlp_both(tokens, grads, mats):
+    count, width = tokens.shape
+    hidden = mats.shape[1] // 2
+    block = 256
+    steps = count // block
+    half = steps // 2
+    row = lambda i: (i, 0)
+    mine = lambda i: (jnp.minimum(i, half - 1), 0)
+    theirs = lambda i: (jnp.maximum(i - half, 0), 0)
+    share = jax.ShapeDtypeStruct((count // 2, width), BF16)
+    return pl.pallas_call(
+        partial(mlp_kernel, half),
+        grid=(steps,),
+        in_specs=[
+            pl.BlockSpec((block, width), row),
+            pl.BlockSpec((block, width), row),
+            pl.BlockSpec((width, 2 * hidden), lambda i: (0, 0)),
+        ],
+        out_specs=[pl.BlockSpec((block, hidden), row)] * 2
+        + [pl.BlockSpec((block, width), mine)] * 2
+        + [pl.BlockSpec((block, width), theirs)] * 2,
+        out_shape=[jax.ShapeDtypeStruct((count, hidden), BF16)] * 2 + [share] * 4,
+        compiler_params=pltpu.CompilerParams(vmem_limit_bytes=VMEM_LIMIT),
+        cost_estimate=pl.CostEstimate(flops=0, bytes_accessed=0, transcendentals=0),
+    )(tokens, grads, mats)
+
+
+def wgrad_kernel(left_ref, right_ref, out_ref, turned_ref):
+    @pl.when(pl.program_id(0) == 0)
+    def _():
+        for at in range(0, left_ref.shape[1], LANES):
+            turned_ref[at : at + LANES] = left_ref[:, at : at + LANES].T
+
+    out_ref[...] = jnp.dot(turned_ref[...], right_ref[...], preferred_element_type=F32).astype(BF16)
+
+
+def wgrad(left, right):
+    (count, rows), columns = left.shape, right.shape[1]
+    block = 512 if columns % 512 == 0 else columns
+    return pl.pallas_call(
+        wgrad_kernel,
+        grid=(columns // block,),
+        in_specs=[
+            pl.BlockSpec((count, rows), lambda i: (0, 0)),
+            pl.BlockSpec((count, block), lambda i: (0, i)),
+        ],
+        out_specs=pl.BlockSpec((rows, block), lambda i: (0, i)),
+        out_shape=jax.ShapeDtypeStruct((rows, columns), BF16),
+        scratch_shapes=[pltpu.VMEM((rows, count), BF16)],
+        compiler_params=pltpu.CompilerParams(vmem_limit_bytes=VMEM_LIMIT),
+        cost_estimate=pl.CostEstimate(flops=0, bytes_accessed=0, transcendentals=0),
+    )(left, right)
 
 
 def add_low(left, right, dtype=BF16):
     return (left.astype(F32) + right.astype(F32)).astype(dtype)
-
-
-def reduce_digits(parts, digits, lead=0, last=F32):
-    left = sorted(digit.at for digit in digits)
-    for at, digit in enumerate(digits):
-        axis = lead + left.index(digit.at)
-        left.remove(digit.at)
-
-        def part(k):
-            return lax.dynamic_index_in_dim(
-                parts, (digit.mine - k) % digit.size, axis, keepdims=False
-            )
-
-        moving = part(1)
-        for k in range(2, digit.size + 1):
-            final = k == digit.size and at == len(digits) - 1
-            moving = add_low(digit.step(moving), part(k), last if final else BF16)
-        parts = moving
-    return parts
 
 
 def sum_everywhere(values, dp_only=False):
@@ -290,8 +650,7 @@
     me_t = lax.axis_index("tensor")
     me_y = me_t // 2
     sizes = digits_of(dp_count)
-    digits = [Digit(sizes, at) for at in range(len(sizes))]
-    backwards = digits[::-1]
+    plane, space = Grid(sizes, False), Grid(sizes, True)
     width = latents.shape[2]
     block = latents.shape[1]
     rows = 2 * block
@@ -326,33 +685,11 @@
         return jnp.where(me_y == 0, jnp.stack([own, other]), jnp.stack([other, own]))
 
     joined_own, joined_other = mine_first(jnp.concatenate([latents, skip_input], -1))
-    joined16 = jnp.concatenate([joined_own, swap_y(joined_other)], 0)
-    skip_got = gather_digits(skip_half, digits)
-    skip_pair = in_order(skip_got, swap_core(skip_got), me_t % 2, len(sizes))
-    skip_mat = skip_pair.reshape(2 * width, width)
-    self_near = gather_digits(self_pack, digits)
-    self_near = self_near.reshape(width, 4 * head_cols)
-    self_far = swap_y(self_near)
-    cross_pair = gather_digits(jnp.stack([cross_pack, swap_y(cross_pack)]), digits, 1)
-    cross_pair = cross_pair.reshape(2, dp_count, depth + text_depth, 2 * head_cols)
-    mlp_got = gather_digits(mlp_pack, digits).reshape(width, 2 * hidden_cols)
-
-    self_mats = [pack[:, : 3 * head_cols] for pack in (self_near, self_far)]
-    self_outs = [pack[:, 3 * head_cols :] for pack in (self_near, self_far)]
-    cross_mat = jnp.concatenate(
-        [cross_pair[k, :, :depth, :head_cols].reshape(width, head_cols) for k in range(2)], 1
-    )
-    cross_out = jnp.concatenate(
-        [cross_pair[k, :, :depth, head_cols:].reshape(width, head_cols) for k in range(2)], 1
-    )
-    text_mat = jnp.concatenate(
-        [cross_pair[k, :, depth:, :head_cols].reshape(text_width, head_cols) for k in range(2)]
-        + [cross_pair[k, :, depth:, head_cols:].reshape(text_width, head_cols) for k in range(2)],
-        1,
-    )
-    self_out = jnp.concatenate(self_outs, 1)
-    inner_mat, outer_mat = mlp_got[:, :hidden_cols], mlp_got[:, hidden_cols:]
-
+    joined_got = swap_y(joined_other)
+    joined16 = jnp.concatenate([joined_own, joined_got], 0)
+    skip_job, self_job = Fetch(plane, skip_half), Fetch(space, self_pack)
+    cross_job, mlp_job = Fetch(space, cross_pack), Fetch(plane, mlp_pack)
+    order = Sequence()
     steps = jnp.zeros((dp_count, 2), F32)
     steps = lax.dynamic_update_slice(steps, timesteps.astype(F32)[None], (me_d, 0))
     steps = sum_everywhere(steps, dp_only=True).reshape(latent_count)
@@ -361,17 +698,30 @@
     shifts = sum_everywhere(matmul(silu_cols, shift_linear.astype(BF16)), dp_only=True)
     my_latent = me_d * 2 + me_y
     shift = lax.dynamic_slice_in_dim(shifts, my_latent, 1, 0)
+    order.run(skip_job)
+    order.run(skip_job, since=(steps,))
+    order.run(skip_job)
+    order.run(skip_job, since=(shifts,))
+    skip_got = skip_job.finish()
+    order.run(self_job)
+    skip_far = swap_core(skip_got)
+    order.run(self_job, since=(skip_far,))
+    skip_mat = place([skip_got, skip_far], [me_t % 2, 1 - me_t % 2], 1)
+    skip_mat = skip_mat.reshape(2 * width, width)
 
     places = patch_order.reshape(tensor_count, block)
     places = jnp.concatenate(
         [lax.dynamic_index_in_dim(places, me_t ^ k, 0, keepdims=False) for k in (0, 2, 1, 3)]
     )
-    cosines, sines = rotary_tables(places)
+    tables = rotary_tables(places)
+    gain_pads = jnp.pad(head_gains, ((0, 0), (0, LANES - HD)))
+    self_gains = jnp.pad(gain_pads[0:2], ((0, 6), (0, 0)))
+    cross_gains = jnp.pad(gain_pads[2:4], ((0, 6), (0, 0)))
     text_part = lax.dynamic_index_in_dim(text_states, me_y, 0, keepdims=False)
 
     cot_own, cot_other = mine_first(out_grad)
     cot_pair = jnp.concatenate([cot_own, cot_other], 0).astype(BF16)
-    cot_got = swap_y(cot_pair)
+    cot_got = swap_y(after(cot_pair, *order.came))
     cotangent = jnp.concatenate([cot_own, cot_got[block:].astype(F32)], 0)
     mlp_full_grad = gather_core(
         jnp.concatenate([cot_pair[:block], cot_got[block:], cot_got[:block], cot_pair[block:]], 0)
@@ -381,118 +731,165 @@
     normed, normed_back = jax.vjp(norm_rows, joined16.astype(F32), skip_gain)
     normed16 = normed.astype(BF16)
     hidden = matmul(normed16, skip_mat)
+    order.run(self_job, cross_job, since=(hidden,))
     first_norm, first_back = jax.vjp(norm_rows, hidden, row_gains[2])
     attn16 = (first_norm + shift).astype(BF16)
+    order.run(self_job, cross_job, since=(attn16,))
+    order.run(self_job)
+    self_got = self_job.finish()
+    self_near = self_got[0].reshape(width, 4 * head_cols)
+    self_far = self_got[1].reshape(width, 4 * head_cols)
+    came = order.run(cross_job, mlp_job, since=(self_got,))
+    self_mats = [pack[:, : 3 * head_cols] for pack in (self_near, self_far)]
+    self_outs = [pack[:, 3 * head_cols :] for pack in (self_near, self_far)]
     attn_full = gather_core(attn16)
-    self_pres = [matmul(attn_full, mat) for mat in self_mats]
-    both = lambda k: jnp.concatenate(
-        [pre[:, k * head_cols : (k + 1) * head_cols] for pre in self_pres], 1
-    )
-    rope = partial(rope_heads, cosines=cosines, sines=sines)
-    query, query_back = jax.vjp(rope, both(0), head_gains[0])
-    keys, keys_back = jax.vjp(rope, both(1), head_gains[1])
-    query16, keys16 = query.astype(BF16), keys.astype(BF16)
-    values16 = both(2).reshape(2 * rows, -1, HD).astype(BF16)
-    self_out16, self_lse = attend(query16, keys16, values16)
-    self_flat = self_out16.reshape(2 * rows, 2 * head_cols)
-    after_self = hidden + sum_core(matmul_nt(self_flat, self_out))
+    heads = head_cols // HD
+    self_places = (0, head_cols, 2 * head_cols)
+    self_pres = [matmul(attn_full, self_mats[0])]
+    self_kept = [attend((self_pres[0],), self_gains, tables, heads, self_places, 2 * rows)]
+    coming = order.run(cross_job, mlp_job, since=self_kept[0][:1])
+    self_pres.append(matmul(after(attn_full, self_kept[0][0], *came), self_mats[1]))
+    self_kept.append(attend((self_pres[1],), self_gains, tables, heads, self_places, 2 * rows))
+    self_flat = after(self_kept[1][0], *coming)
+    order.run(cross_job, mlp_job, since=(self_flat,))
+    after_self = hidden + sum_core(
+        matmul_nt(self_kept[0][0], self_outs[0]) + matmul_nt(self_flat, self_outs[1])
+    )
     third_norm, third_back = jax.vjp(norm_rows, after_self, row_gains[3])
+    cross_pair = cross_job.finish()
+    cross_mat = jnp.concatenate(
+        [cross_pair[k, :, :depth, :head_cols].reshape(width, head_cols) for k in range(2)], 1
+    )
+    cross_out = jnp.concatenate(
+        [cross_pair[k, :, :depth, head_cols:].reshape(width, head_cols) for k in range(2)], 1
+    )
+    text_mat = jnp.concatenate(
+        [cross_pair[k, :, depth:, :head_cols].reshape(text_width, head_cols) for k in range(2)]
+        + [cross_pair[k, :, depth:, head_cols:].reshape(text_width, head_cols) for k in range(2)],
+        1,
+    )
     cross_kept = gather_core(third_norm.astype(BF16))
-    cross_query, cross_query_back = jax.vjp(rope, matmul(cross_kept, cross_mat), head_gains[2])
-    text_pre = matmul(text_part, text_mat)
-    text_keys, text_keys_back = jax.vjp(plain_heads, text_pre[:, : 2 * head_cols], head_gains[3])
-    cross_query16, text_keys16 = cross_query.astype(BF16), text_keys.astype(BF16)
+    came = order.run(mlp_job, since=(cross_kept,))
     text_rows = text_part.shape[0]
-    text_values16 = text_pre[:, 2 * head_cols :].reshape(text_rows, -1, HD).astype(BF16)
-    cross_out16, cross_lse = attend(cross_query16, text_keys16, text_values16)
-    cross_flat = cross_out16.reshape(2 * rows, 2 * head_cols)
-    after_cross = after_self + sum_core(matmul_nt(cross_flat, cross_out))
+    text_pad = jnp.pad(text_part, ((0, -text_rows % LANES), (0, 0)))
+    cross_pres = (matmul(cross_kept, cross_mat), matmul(text_pad, text_mat))
+    cross_places = (0, 0, 2 * head_cols)
+    cross_kept_all = attend(
+        cross_pres, cross_gains, tables, 2 * heads, cross_places, text_rows
+    )
+    cross_flat = cross_kept_all[0]
+    after_cross = after_self + sum_core(matmul_nt(after(cross_flat, *came), cross_out))
     second_norm, second_back = jax.vjp(norm_rows, after_cross, row_gains[4])
 
     mlp16 = second_norm.astype(BF16)
+    mlp_got = mlp_job.finish().reshape(width, 2 * hidden_cols)
     mlp_kept = gather_core(jnp.concatenate([mlp16, swap_y(mlp16)], 0))
-    inner = matmul(mlp_kept, inner_mat)
-    activated, gelu_back = jax.vjp(gelu_tanh, inner)
-    activated16 = activated.astype(BF16)
-
-    def sum_chips(part):
-        part = sum_core(part)
-        return part[:rows] + swap_y(part[rows:].astype(BF16)).astype(F32)
-
-    result = after_cross + sum_chips(matmul_nt(activated16, outer_mat))
-
-    outer_wgrad = matmul_tn(mlp_full_grad, activated16)
-    (inner_grad,) = gelu_back(matmul(mlp_full_grad, outer_mat))
-    inner_grad16 = inner_grad.astype(BF16)
-    inner_wgrad = matmul_tn(mlp_kept, inner_grad16)
-    mlp_sum = jnp.concatenate([inner_wgrad.astype(BF16), outer_wgrad.astype(BF16)], 1)
-    mlp_sum = reduce_digits(mlp_sum.reshape(*sizes, depth, 2 * hidden_cols), backwards)
-    cross_res_grad, fifth_gain_grad = second_back(sum_chips(matmul_nt(inner_grad16, inner_mat)))
+    activated16, inner_grad16, *shares = mlp_both(mlp_kept, mlp_full_grad, mlp_got)
+    out_mine, in_mine, out_theirs, in_theirs = shares
+
+    in_part = add_low(in_mine, swap_core(in_theirs), F32)
+    in_got = swap_y(in_part[rows:].astype(BF16))
+    mlp_in_grad = in_part[:rows] + in_got.astype(F32)
+    inner_wgrad = wgrad(mlp_kept, after(inner_grad16, in_part))
+    outer_wgrad = wgrad(mlp_full_grad, after(activated16, in_part))
+
+    def put_back(values):
+        got = swap_y(values[block:].astype(BF16))
+        return got, by_latent(values[:block], got.astype(F32))
+
+
+    def rows_of(matrix, dp_index, count):
+        return lax.dynamic_slice_in_dim(matrix, dp_index * count, count, 0)
+
+    def mlp_part(at, _):
+        return jnp.concatenate([rows_of(inner_wgrad, at, depth), rows_of(outer_wgrad, at, depth)], 1)
+
+    mlp_run = Reduction(plane, mlp_part)
+    order = Sequence()
+    came = order.run(mlp_run, since=(inner_wgrad, outer_wgrad, in_got))
+    cross_res_grad, fifth_gain_grad = second_back(mlp_in_grad)
     after_cross_grad = cotangent + cross_res_grad
     cross_full_grad = gather_core(after_cross_grad.astype(BF16))
     cross_out_wgrad = matmul_tn(cross_full_grad, cross_flat).astype(BF16)
-    cross_mixed_grad = matmul(cross_full_grad, cross_out).astype(BF16).reshape(2 * rows, -1, HD)
-    cq_grad, ck_grad, cv_grad = attend_back(
-        cross_query16, text_keys16, text_values16, cross_lse, cross_mixed_grad
-    )
-    cq_pre_grad, cq_gain_grad = cross_query_back(cq_grad)
-    ck_pre_grad, ck_gain_grad = text_keys_back(ck_grad)
-    text_grad16 = jnp.concatenate(
-        [ck_pre_grad, cv_grad.reshape(text_rows, 2 * head_cols)], 1
-    ).astype(BF16)
-    text_wgrad = matmul_tn(text_part, text_grad16).astype(BF16)
-    cq_pre16 = cq_pre_grad.astype(BF16)
+    cross_mixed_grad = matmul(cross_full_grad, cross_out).astype(BF16)
+    coming = order.run(mlp_run, since=(cross_mixed_grad,))
+    out_part = add_low(out_mine, swap_core(after(out_theirs, cross_mixed_grad)), F32)
+    cq_pre16, text_grad16, cross_gain_grad = attend_back(
+        cross_pres, after(cross_gains, *came), tables, cross_kept_all, cross_mixed_grad, 2 * heads, cross_places
+    )
+    came = order.run(mlp_run, since=(cq_pre16,))
+    out_got = swap_y(after(out_part[rows:].astype(BF16), cq_pre16))
+    result = after_cross + out_part[:rows] + out_got.astype(F32)
+    text_wgrad = matmul_tn(text_pad, text_grad16).astype(BF16)
     cross_q_wgrad = matmul_tn(cross_kept, cq_pre16).astype(BF16)
-    cross_parts = []
-    for k in range(2):
-        near = slice(k * head_cols, (k + 1) * head_cols)
-        far = slice((2 + k) * head_cols, (3 + k) * head_cols)
-        top = jnp.concatenate([cross_q_wgrad[:, near], cross_out_wgrad[:, near]], 1)
-        low = jnp.concatenate([text_wgrad[:, near], text_wgrad[:, far]], 1)
-        top = top.reshape(*sizes, depth, 2 * head_cols)
-        low = low.reshape(*sizes, text_depth, 2 * head_cols)
-        cross_parts.append(jnp.concatenate([top, low], -2))
-    cross_sum = reduce_digits(jnp.stack(cross_parts), backwards, 1, BF16)
-    cross_sum = add_low(cross_sum[0], swap_y(cross_sum[1]), F32)
-    self_res_grad, fourth_gain_grad = third_back(sum_core(matmul_nt(cq_pre16, cross_mat)))
+
+    def cross_part(at, far):
+        near = slice(far * head_cols, (far + 1) * head_cols)
+        values = slice((2 + far) * head_cols, (3 + far) * head_cols)
+        top = [rows_of(grad[:, near], at, depth) for grad in (cross_q_wgrad, cross_out_wgrad)]
+        low = [rows_of(text_wgrad[:, columns], at, text_depth) for columns in (near, values)]
+        return jnp.concatenate([jnp.concatenate(top, 1), jnp.concatenate(low, 1)], 0)
+
+    cross_run = Reduction(space, cross_part)
+    self_res_grad, fourth_gain_grad = third_back(sum_core(matmul_nt(after(cq_pre16, *coming), cross_mat)))
     after_self_grad = after_cross_grad + self_res_grad
     self_full_grad = gather_core(after_self_grad.astype(BF16))
-    self_out_wgrad = matmul_tn(self_full_grad, self_flat).astype(BF16)
-    self_mixed_grad = matmul(self_full_grad, self_out).astype(BF16).reshape(2 * rows, -1, HD)
-    sq_grad, sk_grad, sv_grad = attend_back(query16, keys16, values16, self_lse, self_mixed_grad)
-    sq_pre_grad, sq_gain_grad = query_back(sq_grad)
-    sk_pre_grad, sk_gain_grad = keys_back(sk_grad)
-    pre_grads = [sq_pre_grad, sk_pre_grad, sv_grad.reshape(2 * rows, 2 * head_cols)]
     attn_part = 0.0
-    self_parts = []
+    self_gain_grad = 0.0
+    coming = order.run(mlp_run, cross_run, since=(self_full_grad,))
+    came = came + (out_got,)
+    pre16 = self_full_grad
+    in_wgrads, out_wgrads = [], []
     for k in range(2):
-        near = slice(k * head_cols, (k + 1) * head_cols)
-        pre16 = jnp.concatenate([grad[:, near] for grad in pre_grads], 1).astype(BF16)
+        mixed_grad = matmul(self_full_grad, self_outs[k]).astype(BF16)
+        pre16, gain_grad = attend_back(
+            (self_pres[k],),
+            after(self_gains, pre16, *came),
+            tables,
+            self_kept[k],
+            mixed_grad,
+            heads,
+            self_places,
+        )
+        self_gain_grad = self_gain_grad + gain_grad
+        came, coming = coming, order.run(cross_run, since=(pre16,))
+        if k == 0:
+            result_got, block_out = put_back(after(result, pre16))
         attn_part = attn_part + matmul_nt(pre16, self_mats[k])
-        in_wgrad = matmul_tn(attn_full, pre16).astype(BF16)
-        part = jnp.concatenate([in_wgrad, self_out_wgrad[:, near]], 1)
-        self_parts.append(part.reshape(*sizes, depth, 4 * head_cols))
-    self_sum = add_low(self_parts[0], swap_y(self_parts[1]))
-    self_sum = reduce_digits(self_sum, backwards)
+        in_wgrads.append(matmul_tn(attn_full, pre16).astype(BF16))
+        out_wgrads.append(matmul_tn(self_full_grad, self_kept[k][0]).astype(BF16))
+
+    def self_part(at, far):
+        return jnp.concatenate(
+            [rows_of(in_wgrads[far], at, depth), rows_of(out_wgrads[far], at, depth)], 1
+        )
+
+    self_run = Reduction(space, self_part)
     attn_grad = sum_core(attn_part)
+    attn_grad = after(attn_grad, result_got, *came)
     hidden_norm_grad, third_gain_grad = first_back(attn_grad)
     shift_grad = jnp.sum(attn_grad, axis=0)
+    order.run(cross_run, self_run, since=(attn_part,))
+    order.run(cross_run, self_run, since=(attn_grad,))
     hidden_grad16 = (after_self_grad + hidden_norm_grad).astype(BF16)
     skip_wgrad = matmul_tn(normed16, hidden_grad16).astype(BF16)
     joined_grad, skip_gain_grad = normed_back(matmul_nt(hidden_grad16, skip_mat))
-
-    quarter = half_depth // 2
-    skip_parts = skip_wgrad.reshape(dp_count, 2, 2, quarter, width)
-    mine = lax.dynamic_index_in_dim(skip_parts, me_t % 2, 2, keepdims=False)
-    theirs = lax.dynamic_index_in_dim(skip_parts, 1 - me_t % 2, 2, keepdims=False)
+    order.run(self_run)
+
+    skip_parts = skip_wgrad.reshape(dp_count, 2, half_depth, width)
+    mine = lax.dynamic_index_in_dim(skip_parts, me_t % 2, 1, keepdims=False)
+    theirs = lax.dynamic_index_in_dim(skip_parts, 1 - me_t % 2, 1, keepdims=False)
     skip_parts = add_low(mine, swap_core(theirs))
-    mine = lax.dynamic_index_in_dim(skip_parts, me_y, 1, keepdims=False)
-    theirs = lax.dynamic_index_in_dim(skip_parts, 1 - me_y, 1, keepdims=False)
-    skip_parts = add_low(mine, swap_y(theirs)).reshape(*sizes, quarter, width)
-    skip_sum = reduce_digits(skip_parts, backwards, 0, BF16)
-    skip_pair = in_order(skip_sum, swap_core(skip_sum), me_t % 2)
-    skip_all = in_order(skip_pair, swap_y(skip_pair), me_y)
-    skip_mat_grad = skip_all.reshape(2 * half_depth, width).astype(F32)
+    skip_run = Reduction(plane, lambda at, _: lax.dynamic_index_in_dim(skip_parts, at, 0, False), BF16)
+    order.run(self_run, skip_run)
+    order.run(self_run, skip_run)
+    order.run(skip_run)
+    order.run(skip_run)
+    mlp_sum, cross_sum, self_sum = mlp_run.finish(), cross_run.finish(), self_run.finish()
+    skip_sum = skip_run.finish()
+    skip_sum = add_low(skip_sum, swap_y(skip_sum))
+    skip_mat_grad = in_order(skip_sum, swap_core(skip_sum), me_t % 2)
+    skip_mat_grad = skip_mat_grad.reshape(2 * half_depth, width).astype(F32)
 
     row_grad = jnp.stack(
         [
@@ -503,7 +900,7 @@
             fifth_gain_grad,
         ]
     )
-    head_grad = jnp.stack([sq_gain_grad, sk_gain_grad, cq_gain_grad, ck_gain_grad])
+    head_grad = jnp.concatenate([self_gain_grad[0:2, :HD], cross_gain_grad[0:2, :HD]], 0)
     single = jnp.zeros((latent_count, width), F32)
     single = lax.dynamic_update_slice(single, shift_grad[None], (my_latent, 0))
     head_row = jnp.pad(head_grad.reshape(1, -1), ((0, 0), (0, width - head_grad.size)))
@@ -530,12 +927,8 @@
     mlp_in_grad = mlp_sum[:, :hidden_cols]
     mlp_out_grad = mlp_sum[:, hidden_cols:].T
 
-    def put_back(values):
-        return by_latent(values[:block], swap_y(values[block:].astype(BF16)).astype(F32))
-
-    block_out = put_back(result)
-    grad_latents = put_back(joined_grad[:, :width])
-    grad_skip_input = put_back(joined_grad[:, width:])
+    _, grad_latents = put_back(joined_grad[:, :width])
+    _, grad_skip_input = put_back(joined_grad[:, width:])
     head_in_first, head_in_second, head_in_ratio = lamb_parts(
         head_inputs, first_head_inputs, second_head_inputs, head_in_grad
     )

time: 1480 us -> 1190 us (0.80)
  Pallas kernels: 0 us -> 267 us
  matrix products: 311 us -> 114 us
  other arithmetic: 341 us -> 181 us
  waiting for transfers between devices: 487 us -> 327 us
  local copies, waits for them, and re-layouts: 263 us -> 143 us
  starting transfers between devices: 63.1 us -> 141 us
    pallas_call x0 -> x14, Pallas kernels: none -> 267 us  [the longest x3 89.7 us: attend_back(): pl.pallas_call(partial(attend_back_kernel, heads, *places, len(pres) == 1...]
    ppermute x77 -> x128, waiting for transfers between devices: 487 us -> 327 us  [send(): return lax.ppermute(values, AXES, pairs)]
    dot_general x12 -> x0, matrix products: 107 us -> none  [the longest x2 26.5 us: attend_back(): jnp.einsum('qhd,khd->hqk', mixed_grad, values, preferred_element_type=jnp...]
    ppermute x77 -> x128, starting transfers between devices: 63.1 us -> 141 us  [send(): return lax.ppermute(values, AXES, pairs)]
    reshape x12 -> x4, local copies, waits for them, and re-layouts: 60.1 us -> 3.97 us  [the longest x2 2.82 us: rotary_tables(): col_angle = jnp.repeat(grid_col[:, None] * spacing[None, :], 2, axis=1)]
    another operation x15 -> x2, other arithmetic: 45.1 us -> 6.09 us  [the longest x6 29.4 us: rotate_pairs(): turned = jnp.stack([-paired[..., 1], paired[..., 0]], -1).reshape(layout)]
    dynamic_update_slice x21 -> x0, local copies, waits for them, and re-layouts: 38.5 us -> none  [gather_digits(): whole = lax.dynamic_update_index_in_dim(whole, piece, place, axis)]
    dot_general x9 -> x8, matrix products: 64.7 us -> 32.2 us  [matmul_tn(): lax.dot_general(left, right, (((0,), (0,)), ((), ())), preferred_element_...]
  transfers between devices with their start and end apart: 77 -> 128, of which waited for: 38 -> 53; matrix products, arithmetic and copies ran while one was open for 52% -> 31% of each run, Pallas kernels for 0% -> 18%
where the time goes in v2:
time: 1190 us; the launch traced here: 1180 us
  waiting for transfers between devices  327 us (27%)
  Pallas kernels  267 us (22%)
  other arithmetic  181 us (15%)
  local copies, waits for them, and re-layouts  143 us (12%)
  starting transfers between devices  141 us (12%)
  matrix products  114 us (10%)
    ppermute x128, waiting for transfers between devices, send(): return lax.ppermute(values, AXES, pairs)  327 us
    ppermute x128, starting transfers between devices, send(): return lax.ppermute(values, AXES, pairs)  141 us
    pallas_call x3, Pallas kernels, attend_back(): pl.pallas_call(partial(attend_back_kernel, heads, *places, len(pres) == 1...  89.7 us
    pallas_call x3, Pallas kernels, attend(): pl.pallas_call(partial(attend_kernel, heads, *places, len(pres) == 1, key...  66.6 us
    pallas_call x1, Pallas kernels, mlp_both(): pl.pallas_call(partial(mlp_kernel, half), grid=(steps,), in_specs=[pl.Blo...  48.4 us
    dot_general x9, matrix products, matmul(): return jnp.dot(left, right, preferred_element_type=jnp.float32)  44.3 us
    convert_element_type x21, other arithmetic, total(): return value.astype(dtype)  34.2 us
    unnamed x451, local copies, waits for them, and re-layouts  32.6 us
  transfers between devices with their start and end apart: 128, of which 53 were waited for; matrix products, arithmetic and copies ran while one was open for 31% of the time, Pallas kernels for 18%

profile of v2, /device:TPU:0, one launch (start us, length us, event | category | flops | bytes accessed | tf_op | source)
XLA Modules:
  0.0 1180.3 jit_solution(2909910656388963079)
XLA Ops:
  8.0 8.5 collective-permute-done.1.refs_1_
  22.3 7.7 collective-permute-done.8
  30.1 4.6 collective-permute-start.9
  41.1 8.8 collective-permute-done.10
  50.1 4.3 collective-permute-done.11
  56.6 4.1 collective-permute-done.12
  62.3 10.1 collective-permute-done.13.refs_7_
  93.1 20.7 %collective-permute-done = bf16[256,2816]{1,0:T(8,128)(2,1)} collective-permute-done((bf16[256,2816]{1,0:T(8,128)(2,1)}, bf16[256,2816]{1,0:T(8,128)(2,1)}, u32[]{:S(2)}, u32[]{:S(2)}) %collective-permute-start) | collective-permute-done | bytes 1441824 | tf_op jit(solution)/shard_map/ppermute | solution.py:291
  116.6 7.1 collective-permute-start.17
  128.5 6.0 collective-permute-done.17.refs_2_
  138.7 6.4 shard_map.633
  145.1 8.5 fusion.109
  158.4 10.8 collective-permute-done.25.refs_4_
  192.6 7.1 collective-permute-done.31.refs_8_
  209.2 4.4 broadcast_select_fusion
  219.8 6.9 shard_map.634
  229.7 4.9 fusion.101
  236.5 7.8 fusion.19.refs_0_
  244.3 28.2 %shard_map.635 = (bf16[1024,352]{1,0:T(8,128)(2,1)}, bf16[1024,512]{1,0:T(8,128)(2,1)}, bf16[1024,512]{1,0:T(8,128)(2,1)}, bf16[1024,512]{1,0:T(8,128)(2,1)}) custom-call(f32[1024,1056]{1,0:T(8,128)} %fusion.19.refs_0_, f32[8,128]{1,0:T(8,128)} %pad.30.refs_1_, f32[1024,128]{1,0:T(8,128)} %pad.31.refs_2_.refs_3_, f32[1024,128]{1,0:T(8,128)} %pad.32.refs_3_.refs_4_, ...), custom_call_target="tpu_custom_call" | custom-call | tf_op jit(solution)/shard_map/pallas_call | solution.py:244
  281.4 5.8 fusion.16.refs_0_
  287.1 16.4 %shard_map.636 = (bf16[1024,352]{1,0:T(8,128)(2,1)}, bf16[1024,512]{1,0:T(8,128)(2,1)}, bf16[1024,512]{1,0:T(8,128)(2,1)}, bf16[1024,512]{1,0:T(8,128)(2,1)}) custom-call(f32[1024,1056]{1,0:T(8,128)} %fusion.16.refs_0_, f32[8,128]{1,0:T(8,128)} %pad.30.refs_1_, f32[1024,128]{1,0:T(8,128)} %pad.31.refs_2_.refs_3_, f32[1024,128]{1,0:T(8,128)} %pad.32.refs_3_.refs_4_, ...), custom_call_target="tpu_custom_call" | custom-call | tf_op jit(solution)/shard_map/pallas_call | solution.py:244
  317.9 29.7 %collective-permute-done.51.refs_15_ = bf16[304,704]{1,0:T(8,128)(2,1)S(1)} collective-permute-done((bf16[304,704]{1,0:T(8,128)(2,1)S(1)}, bf16[304,704]{1,0:T(8,128)(2,1)S(1)}, u32[]{:S(2)}, u32[]{:S(2)}) %collective-permute-start.51) | collective-permute-done | bytes 428064 | tf_op jit(solution)/shard_map/ppermute | solution.py:291
  352.3 6.7 shard_map.637
  362.0 4.7 concatenate.347
  374.2 6.1 fusion.26.refs_0_
  380.3 22.0 %shard_map.638 = (bf16[1024,704]{1,0:T(8,128)(2,1)}, bf16[1024,1024]{1,0:T(8,128)(2,1)}, bf16[384,1024]{1,0:T(8,128)(2,1)}, bf16[384,1024]{1,0:T(8,128)(2,1)}) custom-call(f32[1024,704]{1,0:T(8,128)} %fusion.26.refs_0_, f32[384,1408]{1,0:T(8,128)} %fusion.44.refs_1_, f32[8,128]{1,0:T(8,128)} %pad.35.refs_2_, f32[1024,128]{1,0:T(8,128)} %pad.31.refs_2_.refs_3_, ...), custom_call_target="tpu_custom_call" | custom-call | tf_op jit(solution)/shard_map/pallas_call | solution.py:244
  402.3 4.4 fusion.24
  414.7 30.1 %collective-permute-done.58 = bf16[512,1408]{1,0:T(8,128)(2,1)S(1)} collective-permute-done((bf16[512,1408]{1,0:T(8,128)(2,1)S(1)}, bf16[512,1408]{1,0:T(8,128)(2,1)S(1)}, u32[]{:S(2)}, u32[]{:S(2)}) %collective-permute-start.58) | collective-permute-done | bytes 1441824 | tf_op jit(solution)/shard_map/ppermute | solution.py:291
  446.8 4.7 pad_maximum_fusion.5
  451.6 23.2 %collective-permute-done.56 = bf16[512,1408]{1,0:T(8,128)(2,1)S(1)} collective-permute-done((bf16[512,1408]{1,0:T(8,128)(2,1)S(1)}, bf16[512,1408]{1,0:T(8,128)(2,1)S(1)}, u32[]{:S(2)}, u32[]{:S(2)}) %collective-permute-start.56) | collective-permute-done | bytes 1441824 | tf_op jit(solution)/shard_map/ppermute | solution.py:291
  480.6 7.4 shard_map.639
  488.0 5.6 pad_maximum_fusion.x_ref.left_ref
  493.6 48.4 %shard_map.640 = (bf16[2048,1536]{1,0:T(8,128)(2,1)}, bf16[2048,1536]{1,0:T(8,128)(2,1)}, bf16[1024,1408]{1,0:T(8,128)(2,1)}, bf16[1024,1408]{1,0:T(8,128)(2,1)}...) custom-call(bf16[2048,1408]{1,0:T(8,128)(2,1)} %pad_maximum_fusion.x_ref.left_ref, ...), custom_call_target="tpu_custom_call" | custom-call | tf_op jit(solution)/shard_map/pallas_call | solution.py:514
  542.5 5.1 collective-permute-done.60
  547.6 4.9 convert_add_fusion.2
  556.6 15.7 %shard_map.641 = bf16[1408,1536]{1,0:T(8,128)(2,1)} custom-call(bf16[2048,1408]{1,0:T(8,128)(2,1)} %pad_maximum_fusion.x_ref.left_ref, bf16[2048,1536]{1,0:T(8,128)(2,1)} %get-tuple-element.191.right_ref), custom_call_target="tpu_custom_call" | custom-call | tf_op jit(solution)/shard_map/pallas_call | solution.py:543
  572.3 15.5 %shard_map.642 = bf16[1408,1536]{1,0:T(8,128)(2,1)} custom-call(bf16[2048,1408]{1,0:T(8,128)(2,1)} %constant_dynamic-update-slice_fusion.2.grad_ref.left_ref, bf16[2048,1536]{1,0:T(8,128)(2,1)} %get-tuple-element.193.right_ref), custom_call_target="tpu_custom_call" | custom-call | tf_op jit(solution)/shard_map/pallas_call | solution.py:543
  587.8 5.4 constant_dynamic-slice_fusion
  608.7 12.3 %collective-permute-done.64 = bf16[176,3072]{1,0:T(8,128)(2,1)S(1)} collective-permute-done((bf16[176,3072]{1,0:T(8,128)(2,1)S(1)}, bf16[176,3072]{1,0:T(8,128)(2,1)S(1)}, u32[]{:S(2)}, u32[]{:S(2)}) %collective-permute-start.64) | collective-permute-done | bytes 1081376 | tf_op jit(solution)/shard_map/ppermute | solution.py:291
  626.8 4.7 collective-permute-start.66
  631.5 34.2 %shard_map.643 = (bf16[1024,704]{1,0:T(8,128)(2,1)}, bf16[384,1408]{1,0:T(8,128)(2,1)}, f32[8,128]{1,0:T(8,128)}) custom-call(f32[1024,704]{1,0:T(8,128)} %fusion.26.refs_0_, f32[384,1408]{1,0:T(8,128)} %fusion.44.refs_1_, f32[8,128]{1,0:T(8,128)} %pad.35.refs_2_, f32[1024,128]{1,0:T(8,128)} %pad.31.refs_2_.refs_3_, f32[1024,128]{1,0:T(8,128)} %pad.32.refs_3_.refs_4_, ...), custom_call_target="tpu_custom_call" | custom-call | tf_op jit(solution)/shard_map/pallas_call | solution.py:260
  665.7 4.9 convolution_convert_fusion.5
  706.3 18.8 %collective-permute-done.71 = bf16[176,3072]{1,0:T(8,128)(2,1)S(1)} collective-permute-done((bf16[176,3072]{1,0:T(8,128)(2,1)S(1)}, bf16[176,3072]{1,0:T(8,128)(2,1)S(1)}, u32[]{:S(2)}, u32[]{:S(2)}) %collective-permute-start.71) | collective-permute-done | bytes 1081376 | tf_op jit(solution)/shard_map/ppermute | solution.py:291
  748.8 4.5 convolution_convert_fusion.9
  763.5 7.0 collective-permute-done.65
  772.9 27.5 %shard_map.644 = (bf16[1024,1056]{1,0:T(8,128)(2,1)}, f32[8,128]{1,0:T(8,128)}) custom-call(f32[1024,1056]{1,0:T(8,128)} %fusion.19.refs_0_, f32[8,128]{1,0:T(8,128)} %pad.30.refs_1_, f32[1024,128]{1,0:T(8,128)} %pad.31.refs_2_.refs_3_, f32[1024,128]{1,0:T(8,128)} %pad.32.refs_3_.refs_4_, f32[1024,128]{1,0:T(8,128)} %pad.33.refs_4_.refs_5_, ...), custom_call_target="tpu_custom_call" | custom-call | tf_op jit(solution)/shard_map/pallas_call | solution.py:260
  803.9 5.6 convolution_convert_fusion.2
  819.7 28.0 %shard_map.645 = (bf16[1024,1056]{1,0:T(8,128)(2,1)}, f32[8,128]{1,0:T(8,128)}) custom-call(f32[1024,1056]{1,0:T(8,128)} %fusion.16.refs_0_, f32[8,128]{1,0:T(8,128)} %pad.30.refs_1_, f32[1024,128]{1,0:T(8,128)} %pad.31.refs_2_.refs_3_, f32[1024,128]{1,0:T(8,128)} %pad.32.refs_3_.refs_4_, f32[1024,128]{1,0:T(8,128)} %pad.33.refs_4_.refs_5_, ...), custom_call_target="tpu_custom_call" | custom-call | tf_op jit(solution)/shard_map/pallas_call | solution.py:260
  850.6 6.9 fusion.14
  857.6 4.3 convolution_add_fusion.1
  864.3 5.5 convolution_convert_fusion.1
  891.9 6.5 collective-permute-done.86
  937.4 6.8 fusion.10
  950.7 6.8 convolution_convert_fusion
  969.5 5.5 fusion.92
  977.8 4.5 collective-permute-done.120
  990.2 5.8 collective-permute-done.96
  1017.0 9.1 collective-permute-done.122
  1037.8 10.0 collective-permute-done.104
  1050.7 4.3 fusion
  1059.0 8.9 collective-permute-done.106
  1078.0 5.2 multiply_reduce_fusion.18
  1098.9 6.1 collective-permute-done.113
  1125.9 6.0 collective-permute-done.116
  (951 shorter events, 495.4 us)
Async XLA Ops:
  36.7 24.7 %collective-permute-start.5 = (bf16[176,1408]{1,0:T(8,128)(2,1)}, bf16[176,1408]{1,0:T(8,128)(2,1)}, u32[]{:S(2)}, u32[]{:S(2)}) collective-permute-start(bf16[176,1408]{1,0:T(8,128)(2,1)} %collective-permute-done.4.refs_4_), channel_id=1, source_target_pairs={{0,4},{1,5},{2,6},{3,7},{4,0},{5,1},{6,2},{7,3},{8,12},{9,13},{10,... | collective-permute-start | bytes 1486856 | tf_op jit(solution)/shard_map/ppermute | solution.py:291
  38.0 23.5 %collective-permute-start.6 = (bf16[176,1408]{1,0:T(8,128)(2,1)}, bf16[176,1408]{1,0:T(8,128)(2,1)}, u32[]{:S(2)}, u32[]{:S(2)}) collective-permute-start(bf16[176,1408]{1,0:T(8,128)(2,1)} %collective-permute-done.4.refs_4_), channel_id=1, source_target_pairs={{0,8},{1,9},{2,10},{3,11},{4,12},{5,13},{6,14},{7,15},{8,16},{9,17... | collective-permute-start | bytes 1486856 | tf_op jit(solution)/shard_map/ppermute | solution.py:291
  76.5 61.4 %collective-permute-start.14 = (bf16[8,176,1408]{2,1,0:T(8,128)(2,1)}, bf16[8,176,1408]{2,1,0:T(8,128)(2,1)}, u32[]{:S(2)}, u32[]{:S(2)}) collective-permute-start(bf16[8,176,1408]{2,1,0:T(8,128)(2,1)} %shard_map.632.refs_0_), channel_id=1, source_target_pairs={{0,1},{1,0},{2,3},{3,2},{4,5},{5,4},{6,7},{7,6},{8,9},{9,8},{10,11... | collective-permute-start | bytes 11894792 | tf_op jit(solution)/shard_map/ppermute | solution.py:291
  79.5 34.3 %collective-permute-start = (bf16[256,2816]{1,0:T(8,128)(2,1)}, bf16[256,2816]{1,0:T(8,128)(2,1)}, u32[]{:S(2)}, u32[]{:S(2)}) collective-permute-start(bf16[256,2816]{1,0:T(8,128)(2,1)} %get-tuple-element.554), channel_id=1, source_target_pairs={{0,2},{1,3},{2,0},{3,1},{4,6},{5,7},{6,4},{7,5},{8,10},{9,11},{10,... | collective-permute-start | bytes 4325384 | tf_op jit(solution)/shard_map/ppermute | solution.py:291
  116.6 18.0 %collective-permute-start.17 = (bf16[176,1408]{1,0:T(8,128)(2,1)S(1)}, bf16[176,1408]{1,0:T(8,128)(2,1)S(1)}, u32[]{:S(2)}, u32[]{:S(2)}) collective-permute-start(bf16[176,1408]{1,0:T(8,128)(2,1)S(1)} %pad_maximum_fusion.33.refs_0_), channel_id=1, source_target_pairs={{0,4},{1,5},{2,6},{3,7},{4,0},{5,1},{6,2},{7,3},{8,12},{9,13},{10,... | collective-permute-start | bytes 1486856 | tf_op jit(solution)/shard_map/ppermute | solution.py:291
  154.2 18.9 %collective-permute-start.26 = (bf16[304,704]{1,0:T(8,128)(2,1)S(1)}, bf16[304,704]{1,0:T(8,128)(2,1)S(1)}, u32[]{:S(2)}, u32[]{:S(2)}) collective-permute-start(bf16[304,704]{1,0:T(8,128)(2,1)S(1)} %pad_maximum_fusion.37.refs_0_), channel_id=1, source_target_pairs={{0,4},{1,5},{2,6},{3,7},{4,0},{5,1},{6,2},{7,3},{8,12},{9,13},{10,... | collective-permute-start | bytes 1284104 | tf_op jit(solution)/shard_map/ppermute | solution.py:291
  157.5 19.4 %collective-permute-start.22 = (bf16[176,1408]{1,0:T(8,128)(2,1)}, bf16[176,1408]{1,0:T(8,128)(2,1)S(1)}, u32[]{:S(2)}, u32[]{:S(2)}) collective-permute-start(bf16[176,1408]{1,0:T(8,128)(2,1)} %collective-permute-done.21.refs_8_), channel_id=1, source_target_pairs={{0,8},{1,9},{2,10},{3,11},{4,12},{5,13},{6,14},{7,15},{8,16},{9,17... | collective-permute-start | bytes 1486856 | tf_op jit(solution)/shard_map/ppermute | solution.py:291
  158.1 18.8 %collective-permute-start.23 = (bf16[176,1408]{1,0:T(8,128)(2,1)}, bf16[176,1408]{1,0:T(8,128)(2,1)S(1)}, u32[]{:S(2)}, u32[]{:S(2)}) collective-permute-start(bf16[176,1408]{1,0:T(8,128)(2,1)} %collective-permute-done.21.refs_8_), channel_id=1, source_target_pairs={{0,4},{1,5},{2,6},{3,7},{4,0},{5,1},{6,2},{7,3},{8,12},{9,13},{10,... | collective-permute-start | bytes 1486856 | tf_op jit(solution)/shard_map/ppermute | solution.py:291
  187.4 17.6 %collective-permute-start.29 = (bf16[176,1408]{1,0:T(8,128)(2,1)}, bf16[176,1408]{1,0:T(8,128)(2,1)}, u32[]{:S(2)}, u32[]{:S(2)}) collective-permute-start(bf16[176,1408]{1,0:T(8,128)(2,1)} %copy-done.146), channel_id=1, source_target_pairs={{0,8},{1,9},{2,10},{3,11},{4,12},{5,13},{6,14},{7,15},{8,16},{9,17... | collective-permute-start | bytes 1486856 | tf_op jit(solution)/shard_map/ppermute | solution.py:291
  199.6 35.0 %collective-permute-start.15 = (bf16[512,1408]{1,0:T(8,128)(2,1)}, bf16[512,1408]{1,0:T(8,128)(2,1)}, u32[]{:S(2)}, u32[]{:S(2)}) collective-permute-start(bf16[512,1408]{1,0:T(8,128)(2,1)} %add_convert_fusion.1), channel_id=1, source_target_pairs={{0,1},{1,0},{2,3},{3,2},{4,5},{5,4},{6,7},{7,6},{8,9},{9,8},{10,11... | collective-permute-start | bytes 4325384 | tf_op jit(solution)/shard_map/ppermute | solution.py:291
  226.7 45.8 %collective-permute-start.40 = (bf16[176,3072]{1,0:T(8,128)(2,1)}, bf16[176,3072]{1,0:T(8,128)(2,1)}, u32[]{:S(2)}, u32[]{:S(2)}) collective-permute-start(bf16[176,3072]{1,0:T(8,128)(2,1)} %pad_maximum_fusion.19.refs_0_), channel_id=1, source_target_pairs={{0,8},{1,9},{2,10},{3,11},{4,12},{5,13},{6,14},{7,15},{8,16},{9,17... | collective-permute-start | bytes 3244040 | tf_op jit(solution)/shard_map/ppermute | solution.py:291
  227.2 45.4 %collective-permute-start.41 = (bf16[176,3072]{1,0:T(8,128)(2,1)}, bf16[176,3072]{1,0:T(8,128)(2,1)}, u32[]{:S(2)}, u32[]{:S(2)}) collective-permute-start(bf16[176,3072]{1,0:T(8,128)(2,1)} %pad_maximum_fusion.19.refs_0_), channel_id=1, source_target_pairs={{0,4},{1,5},{2,6},{3,7},{4,0},{5,1},{6,2},{7,3},{8,12},{9,13},{10,... | collective-permute-start | bytes 3244040 | tf_op jit(solution)/shard_map/ppermute | solution.py:291
  227.8 44.7 %collective-permute-start.37 = (bf16[304,704]{1,0:T(8,128)(2,1)}, bf16[304,704]{1,0:T(8,128)(2,1)S(1)}, u32[]{:S(2)}, u32[]{:S(2)}) collective-permute-start(bf16[304,704]{1,0:T(8,128)(2,1)} %collective-permute-done.31.refs_8_), channel_id=1, source_target_pairs={{0,8},{1,9},{2,10},{3,11},{4,12},{5,13},{6,14},{7,15},{8,16},{9,17... | collective-permute-start | bytes 1284104 | tf_op jit(solution)/shard_map/ppermute | solution.py:291
  228.5 44.0 %collective-permute-start.38 = (bf16[304,704]{1,0:T(8,128)(2,1)}, bf16[304,704]{1,0:T(8,128)(2,1)}, u32[]{:S(2)}, u32[]{:S(2)}) collective-permute-start(bf16[304,704]{1,0:T(8,128)(2,1)} %collective-permute-done.31.refs_8_), channel_id=1, source_target_pairs={{0,4},{1,5},{2,6},{3,7},{4,0},{5,1},{6,2},{7,3},{8,12},{9,13},{10,... | collective-permute-start | bytes 1284104 | tf_op jit(solution)/shard_map/ppermute | solution.py:291
  234.6 37.9 %collective-permute-start.39 = (bf16[304,704]{1,0:T(8,128)(2,1)}, bf16[304,704]{1,0:T(8,128)(2,1)}, u32[]{:S(2)}, u32[]{:S(2)}) collective-permute-start(bf16[304,704]{1,0:T(8,128)(2,1)} %collective-permute-done.31.refs_8_), channel_id=1, source_target_pairs={{0,2},{1,3},{2,0},{3,1},{4,6},{5,7},{6,4},{7,5},{8,10},{9,11},{10,... | collective-permute-start | bytes 1284104 | tf_op jit(solution)/shard_map/ppermute | solution.py:291
  272.6 31.2 %collective-permute-start.45 = (bf16[176,3072]{1,0:T(8,128)(2,1)}, bf16[176,3072]{1,0:T(8,128)(2,1)}, u32[]{:S(2)}, u32[]{:S(2)}) collective-permute-start(bf16[176,3072]{1,0:T(8,128)(2,1)} %collective-permute-done.40.refs_2_), channel_id=1, source_target_pairs={{0,8},{1,9},{2,10},{3,11},{4,12},{5,13},{6,14},{7,15},{8,16},{9,17... | collective-permute-start | bytes 3244040 | tf_op jit(solution)/shard_map/ppermute | solution.py:291
  274.7 29.0 %collective-permute-start.46 = (bf16[176,3072]{1,0:T(8,128)(2,1)}, bf16[176,3072]{1,0:T(8,128)(2,1)}, u32[]{:S(2)}, u32[]{:S(2)}) collective-permute-start(bf16[176,3072]{1,0:T(8,128)(2,1)} %collective-permute-done.40.refs_2_), channel_id=1, source_target_pairs={{0,4},{1,5},{2,6},{3,7},{4,0},{5,1},{6,2},{7,3},{8,12},{9,13},{10,... | collective-permute-start | bytes 3244040 | tf_op jit(solution)/shard_map/ppermute | solution.py:291
  277.2 26.3 %collective-permute-start.44 = (bf16[304,704]{1,0:T(8,128)(2,1)}, bf16[304,704]{1,0:T(8,128)(2,1)S(1)}, u32[]{:S(2)}, u32[]{:S(2)}) collective-permute-start(bf16[304,704]{1,0:T(8,128)(2,1)} %collective-permute-done.38.refs_10_), channel_id=1, source_target_pairs={{0,2},{1,3},{2,0},{3,1},{4,6},{5,7},{6,4},{7,5},{8,10},{9,11},{10,... | collective-permute-start | bytes 1284104 | tf_op jit(solution)/shard_map/ppermute | solution.py:291
  278.2 25.6 %collective-permute-start.43 = (bf16[304,704]{1,0:T(8,128)(2,1)S(1)}, bf16[304,704]{1,0:T(8,128)(2,1)S(1)}, u32[]{:S(2)}, u32[]{:S(2)}) collective-permute-start(bf16[304,704]{1,0:T(8,128)(2,1)S(1)} %copy-done.151), channel_id=1, source_target_pairs={{0,4},{1,5},{2,6},{3,7},{4,0},{5,1},{6,2},{7,3},{8,12},{9,13},{10,... | collective-permute-start | bytes 1284104 | tf_op jit(solution)/shard_map/ppermute | solution.py:291
  279.3 24.4 %collective-permute-start.42 = (bf16[304,704]{1,0:T(8,128)(2,1)}, bf16[304,704]{1,0:T(8,128)(2,1)S(1)}, u32[]{:S(2)}, u32[]{:S(2)}) collective-permute-start(bf16[304,704]{1,0:T(8,128)(2,1)} %collective-permute-done.39.refs_9_), channel_id=1, source_target_pairs={{0,8},{1,9},{2,10},{3,11},{4,12},{5,13},{6,14},{7,15},{8,16},{9,17... | collective-permute-start | bytes 1284104 | tf_op jit(solution)/shard_map/ppermute | solution.py:291
  311.2 55.6 %collective-permute-start.52 = (bf16[176,3072]{1,0:T(8,128)(2,1)}, bf16[176,3072]{1,0:T(8,128)(2,1)}, u32[]{:S(2)}, u32[]{:S(2)}) collective-permute-start(bf16[176,3072]{1,0:T(8,128)(2,1)} %collective-permute-done.45.refs_4_), channel_id=1, source_target_pairs={{0,4},{1,5},{2,6},{3,7},{4,0},{5,1},{6,2},{7,3},{8,12},{9,13},{10,... | collective-permute-start | bytes 3244040 | tf_op jit(solution)/shard_map/ppermute | solution.py:291
  312.1 54.6 %collective-permute-start.53 = (bf16[176,3072]{1,0:T(8,128)(2,1)}, bf16[176,3072]{1,0:T(8,128)(2,1)}, u32[]{:S(2)}, u32[]{:S(2)}) collective-permute-start(bf16[176,3072]{1,0:T(8,128)(2,1)} %collective-permute-done.45.refs_4_), channel_id=1, source_target_pairs={{0,8},{1,9},{2,10},{3,11},{4,12},{5,13},{6,14},{7,15},{8,16},{9,17... | collective-permute-start | bytes 3244040 | tf_op jit(solution)/shard_map/ppermute | solution.py:291
  312.6 35.1 %collective-permute-start.51 = (bf16[304,704]{1,0:T(8,128)(2,1)S(1)}, bf16[304,704]{1,0:T(8,128)(2,1)S(1)}, u32[]{:S(2)}, u32[]{:S(2)}) collective-permute-start(bf16[304,704]{1,0:T(8,128)(2,1)S(1)} %collective-permute-done.42.refs_13_), channel_id=1, source_target_pairs={{0,4},{1,5},{2,6},{3,7},{4,0},{5,1},{6,2},{7,3},{8,12},{9,13},{10,... | collective-permute-start | bytes 1284104 | tf_op jit(solution)/shard_map/ppermute | solution.py:291
  313.6 37.2 %collective-permute-start.50 = (bf16[304,704]{1,0:T(8,128)(2,1)}, bf16[304,704]{1,0:T(8,128)(2,1)S(1)}, u32[]{:S(2)}, u32[]{:S(2)}) collective-permute-start(bf16[304,704]{1,0:T(8,128)(2,1)} %collective-permute-done.38.refs_10_), channel_id=1, source_target_pairs={{0,8},{1,9},{2,10},{3,11},{4,12},{5,13},{6,14},{7,15},{8,16},{9,17... | collective-permute-start | bytes 1284104 | tf_op jit(solution)/shard_map/ppermute | solution.py:291
  314.4 36.4 %collective-permute-start.49 = (bf16[304,704]{1,0:T(8,128)(2,1)S(1)}, bf16[304,704]{1,0:T(8,128)(2,1)S(1)}, u32[]{:S(2)}, u32[]{:S(2)}) collective-permute-start(bf16[304,704]{1,0:T(8,128)(2,1)S(1)} %collective-permute-done.43.refs_6_), channel_id=1, source_target_pairs={{0,2},{1,3},{2,0},{3,1},{4,6},{5,7},{6,4},{7,5},{8,10},{9,11},{10,... | collective-permute-start | bytes 1284104 | tf_op jit(solution)/shard_map/ppermute | solution.py:291
  347.7 26.5 %collective-permute-start.48 = (bf16[512,1408]{1,0:T(8,128)(2,1)}, bf16[512,1408]{1,0:T(8,128)(2,1)}, u32[]{:S(2)}, u32[]{:S(2)}) collective-permute-start(bf16[512,1408]{1,0:T(8,128)(2,1)} %multiply_convert_fusion.1), channel_id=1, source_target_pairs={{0,1},{1,0},{2,3},{3,2},{4,5},{5,4},{6,7},{7,6},{8,9},{9,8},{10,11... | collective-permute-start | bytes 4325384 | tf_op jit(solution)/shard_map/ppermute | solution.py:291
  366.7 35.5 %collective-permute-start.54 = (bf16[176,3072]{1,0:T(8,128)(2,1)}, bf16[176,3072]{1,0:T(8,128)(2,1)S(1)}, u32[]{:S(2)}, u32[]{:S(2)}) collective-permute-start(bf16[176,3072]{1,0:T(8,128)(2,1)} %collective-permute-done.52.refs_5_), channel_id=1, source_target_pairs={{0,8},{1,9},{2,10},{3,11},{4,12},{5,13},{6,14},{7,15},{8,16},{9,17... | collective-permute-start | bytes 3244040 | tf_op jit(solution)/shard_map/ppermute | solution.py:291
  410.3 34.5 %collective-permute-start.58 = (bf16[512,1408]{1,0:T(8,128)(2,1)S(1)}, bf16[512,1408]{1,0:T(8,128)(2,1)S(1)}, u32[]{:S(2)}, u32[]{:S(2)}) collective-permute-start(bf16[512,1408]{1,0:T(8,128)(2,1)S(1)} %pad_maximum_fusion.14), channel_id=1, source_target_pairs={{0,2},{1,3},{2,0},{3,1},{4,6},{5,7},{6,4},{7,5},{8,10},{9,11},{10,... | collective-permute-start | bytes 4325384 | tf_op jit(solution)/shard_map/ppermute | solution.py:291
  413.5 61.3 %collective-permute-start.56 = (bf16[512,1408]{1,0:T(8,128)(2,1)S(1)}, bf16[512,1408]{1,0:T(8,128)(2,1)S(1)}, u32[]{:S(2)}, u32[]{:S(2)}) collective-permute-start(bf16[512,1408]{1,0:T(8,128)(2,1)S(1)} %multiply_convert_fusion), channel_id=1, source_target_pairs={{0,2},{1,3},{2,0},{3,1},{4,6},{5,7},{6,4},{7,5},{8,10},{9,11},{10,... | collective-permute-start | bytes 4325384 | tf_op jit(solution)/shard_map/ppermute | solution.py:291
  451.6 27.2 %collective-permute-start.59 = (bf16[1024,1408]{1,0:T(8,128)(2,1)S(1)}, bf16[1024,1408]{1,0:T(8,128)(2,1)S(1)}, u32[]{:S(2)}, u32[]{:S(2)}) collective-permute-start(bf16[1024,1408]{1,0:T(8,128)(2,1)S(1)} %pad_maximum_fusion.5), channel_id=1, source_target_pairs={{0,1},{1,0},{2,3},{3,2},{4,5},{5,4},{6,7},{7,6},{8,9},{9,8},{10,11... | collective-permute-start | bytes 8650760 | tf_op jit(solution)/shard_map/ppermute | solution.py:291
  555.5 38.9 %collective-permute-start.61 = (bf16[512,1408]{1,0:T(8,128)(2,1)}, bf16[512,1408]{1,0:T(8,128)(2,1)}, u32[]{:S(2)}, u32[]{:S(2)}) collective-permute-start(bf16[512,1408]{1,0:T(8,128)(2,1)} %slice.504), channel_id=1, source_target_pairs={{0,2},{1,3},{2,0},{3,1},{4,6},{5,7},{6,4},{7,5},{8,10},{9,11},{10,... | collective-permute-start | bytes 4325384 | tf_op jit(solution)/shard_map/ppermute | solution.py:291
  594.4 26.5 %collective-permute-start.64 = (bf16[176,3072]{1,0:T(8,128)(2,1)S(1)}, bf16[176,3072]{1,0:T(8,128)(2,1)S(1)}, u32[]{:S(2)}, u32[]{:S(2)}) collective-permute-start(bf16[176,3072]{1,0:T(8,128)(2,1)S(1)} %pad_maximum_fusion.20), channel_id=1, source_target_pairs={{0,24},{1,25},{2,26},{3,27},{4,28},{5,29},{6,30},{7,31},{8,0},{9,1... | collective-permute-start | bytes 3244040 | tf_op jit(solution)/shard_map/ppermute | solution.py:291
  626.0 63.3 %collective-permute-start.67 = (bf16[176,3072]{1,0:T(8,128)(2,1)}, bf16[176,3072]{1,0:T(8,128)(2,1)}, u32[]{:S(2)}, u32[]{:S(2)}) collective-permute-start(bf16[176,3072]{1,0:T(8,128)(2,1)} %add_convert_fusion.4), channel_id=1, source_target_pairs={{0,4},{1,5},{2,6},{3,7},{4,0},{5,1},{6,2},{7,3},{8,12},{9,13},{10,... | collective-permute-start | bytes 3244040 | tf_op jit(solution)/shard_map/ppermute | solution.py:291
  626.8 62.4 %collective-permute-start.66 = (bf16[176,3072]{1,0:T(8,128)(2,1)}, bf16[176,3072]{1,0:T(8,128)(2,1)}, u32[]{:S(2)}, u32[]{:S(2)}) collective-permute-start(bf16[176,3072]{1,0:T(8,128)(2,1)} %pad_maximum_fusion.21), channel_id=1, source_target_pairs={{0,24},{1,25},{2,26},{3,27},{4,28},{5,29},{6,30},{7,31},{8,0},{9,1... | collective-permute-start | bytes 3244040 | tf_op jit(solution)/shard_map/ppermute | solution.py:291
  681.5 48.0 %collective-permute-start.63 = (bf16[1024,1408]{1,0:T(8,128)(2,1)S(1)}, bf16[1024,1408]{1,0:T(8,128)(2,1)S(1)}, u32[]{:S(2)}, u32[]{:S(2)}) collective-permute-start(bf16[1024,1408]{1,0:T(8,128)(2,1)S(1)} %copy-done.211), channel_id=1, source_target_pairs={{0,1},{1,0},{2,3},{3,2},{4,5},{5,4},{6,7},{7,6},{8,9},{9,8},{10,11... | collective-permute-start | bytes 8650760 | tf_op jit(solution)/shard_map/ppermute | solution.py:291
  699.2 25.8 %collective-permute-start.71 = (bf16[176,3072]{1,0:T(8,128)(2,1)S(1)}, bf16[176,3072]{1,0:T(8,128)(2,1)S(1)}, u32[]{:S(2)}, u32[]{:S(2)}) collective-permute-start(bf16[176,3072]{1,0:T(8,128)(2,1)S(1)} %copy-done.99), channel_id=1, source_target_pairs={{0,4},{1,5},{2,6},{3,7},{4,0},{5,1},{6,2},{7,3},{8,12},{9,13},{10,... | collective-permute-start | bytes 3244040 | tf_op jit(solution)/shard_map/ppermute | solution.py:291
  702.5 25.6 %collective-permute-start.70 = (bf16[176,3072]{1,0:T(8,128)(2,1)S(1)}, bf16[176,3072]{1,0:T(8,128)(2,1)S(1)}, u32[]{:S(2)}, u32[]{:S(2)}) collective-permute-start(bf16[176,3072]{1,0:T(8,128)(2,1)S(1)} %add_convert_fusion.3), channel_id=1, source_target_pairs={{0,24},{1,25},{2,26},{3,27},{4,28},{5,29},{6,30},{7,31},{8,0},{9,1... | collective-permute-start | bytes 3244040 | tf_op jit(solution)/shard_map/ppermute | solution.py:291
  706.3 30.4 %collective-permute-start.69 = (bf16[512,1408]{1,0:T(8,128)(2,1)S(1)}, bf16[512,1408]{1,0:T(8,128)(2,1)S(1)}, u32[]{:S(2)}, u32[]{:S(2)}) collective-permute-start(bf16[512,1408]{1,0:T(8,128)(2,1)S(1)} %fusion.50), channel_id=1, source_target_pairs={{0,1},{1,0},{2,3},{3,2},{4,5},{5,4},{6,7},{7,6},{8,9},{9,8},{10,11... | collective-permute-start | bytes 4325384 | tf_op jit(solution)/shard_map/ppermute | solution.py:291
  735.6 34.8 %collective-permute-start.65 = (bf16[512,1408]{1,0:T(8,128)(2,1)}, bf16[512,1408]{1,0:T(8,128)(2,1)}, u32[]{:S(2)}, u32[]{:S(2)}) collective-permute-start(bf16[512,1408]{1,0:T(8,128)(2,1)} %slice.503), channel_id=1, source_target_pairs={{0,2},{1,3},{2,0},{3,1},{4,6},{5,7},{6,4},{7,5},{8,10},{9,11},{10,... | collective-permute-start | bytes 4325384 | tf_op jit(solution)/shard_map/ppermute | solution.py:291
  743.7 70.8 %collective-permute-start.77 = (bf16[304,704]{1,0:T(8,128)(2,1)}, bf16[304,704]{1,0:T(8,128)(2,1)}, u32[]{:S(2)}, u32[]{:S(2)}) collective-permute-start(bf16[304,704]{1,0:T(8,128)(2,1)} %maximum_maximum_fusion.2), channel_id=1, source_target_pairs={{0,2},{1,3},{2,0},{3,1},{4,6},{5,7},{6,4},{7,5},{8,10},{9,11},{10,... | collective-permute-start | bytes 1284104 | tf_op jit(solution)/shard_map/ppermute | solution.py:291
  744.7 72.9 %collective-permute-start.76 = (bf16[304,704]{1,0:T(8,128)(2,1)}, bf16[304,704]{1,0:T(8,128)(2,1)}, u32[]{:S(2)}, u32[]{:S(2)}) collective-permute-start(bf16[304,704]{1,0:T(8,128)(2,1)} %maximum_maximum_fusion.1), channel_id=1, source_target_pairs={{0,4},{1,5},{2,6},{3,7},{4,0},{5,1},{6,2},{7,3},{8,12},{9,13},{10,... | collective-permute-start | bytes 1284104 | tf_op jit(solution)/shard_map/ppermute | solution.py:291
  745.8 73.9 %collective-permute-start.75 = (bf16[304,704]{1,0:T(8,128)(2,1)}, bf16[304,704]{1,0:T(8,128)(2,1)}, u32[]{:S(2)}, u32[]{:S(2)}) collective-permute-start(bf16[304,704]{1,0:T(8,128)(2,1)} %maximum_maximum_fusion), channel_id=1, source_target_pairs={{0,24},{1,25},{2,26},{3,27},{4,28},{5,29},{6,30},{7,31},{8,0},{9,1... | collective-permute-start | bytes 1284104 | tf_op jit(solution)/shard_map/ppermute | solution.py:291
  747.9 71.8 %collective-permute-start.74 = (bf16[176,3072]{1,0:T(8,128)(2,1)}, bf16[176,3072]{1,0:T(8,128)(2,1)}, u32[]{:S(2)}, u32[]{:S(2)}) collective-permute-start(bf16[176,3072]{1,0:T(8,128)(2,1)} %pad_maximum_fusion.23), channel_id=1, source_target_pairs={{0,4},{1,5},{2,6},{3,7},{4,0},{5,1},{6,2},{7,3},{8,12},{9,13},{10,... | collective-permute-start | bytes 3244040 | tf_op jit(solution)/shard_map/ppermute | solution.py:291
  770.5 49.2 %collective-permute-start.73 = (bf16[176,3072]{1,0:T(8,128)(2,1)}, bf16[176,3072]{1,0:T(8,128)(2,1)}, u32[]{:S(2)}, u32[]{:S(2)}) collective-permute-start(bf16[176,3072]{1,0:T(8,128)(2,1)} %add_convert_fusion.2), channel_id=1, source_target_pairs={{0,24},{1,25},{2,26},{3,27},{4,28},{5,29},{6,30},{7,31},{8,0},{9,1... | collective-permute-start | bytes 3244040 | tf_op jit(solution)/shard_map/ppermute | solution.py:291
  814.5 76.2 %collective-permute-start.72 = (bf16[256,1408]{1,0:T(8,128)(2,1)}, bf16[256,1408]{1,0:T(8,128)(2,1)}, u32[]{:S(2)}, u32[]{:S(2)}) collective-permute-start(bf16[256,1408]{1,0:T(8,128)(2,1)} %slice.507), channel_id=1, source_target_pairs={{0,2},{1,3},{2,0},{3,1},{4,6},{5,7},{6,4},{7,5},{8,10},{9,11},{10,... | collective-permute-start | bytes 2162696 | tf_op jit(solution)/shard_map/ppermute | solution.py:291
  848.5 38.4 %collective-permute-start.81 = (bf16[304,704]{1,0:T(8,128)(2,1)}, bf16[304,704]{1,0:T(8,128)(2,1)S(1)}, u32[]{:S(2)}, u32[]{:S(2)}) collective-permute-start(bf16[304,704]{1,0:T(8,128)(2,1)} %maximum_maximum_fusion.3), channel_id=1, source_target_pairs={{0,2},{1,3},{2,0},{3,1},{4,6},{5,7},{6,4},{7,5},{8,10},{9,11},{10,... | collective-permute-start | bytes 1284104 | tf_op jit(solution)/shard_map/ppermute | solution.py:291
  849.5 37.4 %collective-permute-start.80 = (bf16[304,704]{1,0:T(8,128)(2,1)}, bf16[304,704]{1,0:T(8,128)(2,1)S(1)}, u32[]{:S(2)}, u32[]{:S(2)}) collective-permute-start(bf16[304,704]{1,0:T(8,128)(2,1)} %add_convert_fusion.18), channel_id=1, source_target_pairs={{0,4},{1,5},{2,6},{3,7},{4,0},{5,1},{6,2},{7,3},{8,12},{9,13},{10,... | collective-permute-start | bytes 1284104 | tf_op jit(solution)/shard_map/ppermute | solution.py:291
  850.6 35.9 %collective-permute-start.79 = (bf16[304,704]{1,0:T(8,128)(2,1)}, bf16[304,704]{1,0:T(8,128)(2,1)S(1)}, u32[]{:S(2)}, u32[]{:S(2)}) collective-permute-start(bf16[304,704]{1,0:T(8,128)(2,1)} %add_convert_fusion.19), channel_id=1, source_target_pairs={{0,24},{1,25},{2,26},{3,27},{4,28},{5,29},{6,30},{7,31},{8,0},{9,1... | collective-permute-start | bytes 1284104 | tf_op jit(solution)/shard_map/ppermute | solution.py:291
  863.1 65.5 %collective-permute-start.78 = (bf16[512,1408]{1,0:T(8,128)(2,1)}, bf16[512,1408]{1,0:T(8,128)(2,1)}, u32[]{:S(2)}, u32[]{:S(2)}) collective-permute-start(bf16[512,1408]{1,0:T(8,128)(2,1)} %slice.501), channel_id=1, source_target_pairs={{0,1},{1,0},{2,3},{3,2},{4,5},{5,4},{6,7},{7,6},{8,9},{9,8},{10,11... | collective-permute-start | bytes 4325384 | tf_op jit(solution)/shard_map/ppermute | solution.py:291
  901.5 18.0 %collective-permute-start.90 = (bf16[304,704]{1,0:T(8,128)(2,1)}, bf16[304,704]{1,0:T(8,128)(2,1)}, u32[]{:S(2)}, u32[]{:S(2)}) collective-permute-start(bf16[304,704]{1,0:T(8,128)(2,1)} %maximum_maximum_fusion.6), channel_id=1, source_target_pairs={{0,2},{1,3},{2,0},{3,1},{4,6},{5,7},{6,4},{7,5},{8,10},{9,11},{10,... | collective-permute-start | bytes 1284104 | tf_op jit(solution)/shard_map/ppermute | solution.py:291
  919.5 42.9 %collective-permute-start.91 = (bf16[176,1408]{1,0:T(8,128)(2,1)}, bf16[176,1408]{1,0:T(8,128)(2,1)}, u32[]{:S(2)}, u32[]{:S(2)}) collective-permute-start(bf16[176,1408]{1,0:T(8,128)(2,1)} %pad_maximum_fusion.34), channel_id=1, source_target_pairs={{0,24},{1,25},{2,26},{3,27},{4,28},{5,29},{6,30},{7,31},{8,0},{9,1... | collective-permute-start | bytes 1486856 | tf_op jit(solution)/shard_map/ppermute | solution.py:291
  950.6 17.8 %collective-permute-start.118 = (f32[22,1408]{1,0:T(8,128)S(1)}, f32[22,1408]{1,0:T(8,128)S(1)}, u32[]{:S(2)}, u32[]{:S(2)}) collective-permute-start(f32[22,1408]{1,0:T(8,128)S(1)} %concatenate.432), channel_id=1, source_target_pairs={{0,1},{1,0},{2,3},{3,2},{4,5},{5,4},{6,7},{7,6},{8,9},{9,8},{10,11... | collective-permute-start | bytes 371720 | tf_op jit(solution)/shard_map/ppermute | solution.py:291
  961.9 88.8 %collective-permute-start.105 = (bf16[8,176,1408]{2,1,0:T(8,128)(2,1)}, bf16[8,176,1408]{2,1,0:T(8,128)(2,1)}, u32[]{:S(2)}, u32[]{:S(2)}) collective-permute-start(bf16[8,176,1408]{2,1,0:T(8,128)(2,1)} %dynamic-slice_bitcast_fusion), channel_id=1, source_target_pairs={{0,1},{1,0},{2,3},{3,2},{4,5},{5,4},{6,7},{7,6},{8,9},{9,8},{10,11... | collective-permute-start | bytes 11894792 | tf_op jit(solution)/shard_map/ppermute | solution.py:291
  964.5 35.2 %collective-permute-start.97 = (bf16[176,1408]{1,0:T(8,128)(2,1)}, bf16[176,1408]{1,0:T(8,128)(2,1)}, u32[]{:S(2)}, u32[]{:S(2)}) collective-permute-start(bf16[176,1408]{1,0:T(8,128)(2,1)} %copy.265), channel_id=1, source_target_pairs={{0,24},{1,25},{2,26},{3,27},{4,28},{5,29},{6,30},{7,31},{8,0},{9,1... | collective-permute-start | bytes 1486856 | tf_op jit(solution)/shard_map/ppermute | solution.py:291
  966.3 21.7 %collective-permute-start.94 = (bf16[304,704]{1,0:T(8,128)(2,1)}, bf16[304,704]{1,0:T(8,128)(2,1)}, u32[]{:S(2)}, u32[]{:S(2)}) collective-permute-start(bf16[304,704]{1,0:T(8,128)(2,1)} %add_convert_fusion.14), channel_id=1, source_target_pairs={{0,24},{1,25},{2,26},{3,27},{4,28},{5,29},{6,30},{7,31},{8,0},{9,1... | collective-permute-start | bytes 1284104 | tf_op jit(solution)/shard_map/ppermute | solution.py:291
  967.3 21.8 %collective-permute-start.95 = (bf16[304,704]{1,0:T(8,128)(2,1)S(1)}, bf16[304,704]{1,0:T(8,128)(2,1)}, u32[]{:S(2)}, u32[]{:S(2)}) collective-permute-start(bf16[304,704]{1,0:T(8,128)(2,1)S(1)} %copy-done.148), channel_id=1, source_target_pairs={{0,4},{1,5},{2,6},{3,7},{4,0},{5,1},{6,2},{7,3},{8,12},{9,13},{10,... | collective-permute-start | bytes 1284104 | tf_op jit(solution)/shard_map/ppermute | solution.py:291
  1005.2 21.0 %collective-permute-start.101 = (bf16[176,1408]{1,0:T(8,128)(2,1)}, bf16[176,1408]{1,0:T(8,128)(2,1)}, u32[]{:S(2)}, u32[]{:S(2)}) collective-permute-start(bf16[176,1408]{1,0:T(8,128)(2,1)} %copy.268), channel_id=1, source_target_pairs={{0,2},{1,3},{2,0},{3,1},{4,6},{5,7},{6,4},{7,5},{8,10},{9,11},{10,... | collective-permute-start | bytes 1486856 | tf_op jit(solution)/shard_map/ppermute | solution.py:291
  1007.8 18.5 %collective-permute-start.100 = (bf16[176,1408]{1,0:T(8,128)(2,1)S(1)}, bf16[176,1408]{1,0:T(8,128)(2,1)}, u32[]{:S(2)}, u32[]{:S(2)}) collective-permute-start(bf16[176,1408]{1,0:T(8,128)(2,1)S(1)} %add_convert_fusion.11), channel_id=1, source_target_pairs={{0,4},{1,5},{2,6},{3,7},{4,0},{5,1},{6,2},{7,3},{8,12},{9,13},{10,... | collective-permute-start | bytes 1486856 | tf_op jit(solution)/shard_map/ppermute | solution.py:291
  1027.3 20.8 %collective-permute-start.103 = (bf16[176,1408]{1,0:T(8,128)(2,1)}, bf16[176,1408]{1,0:T(8,128)(2,1)}, u32[]{:S(2)}, u32[]{:S(2)}) collective-permute-start(bf16[176,1408]{1,0:T(8,128)(2,1)} %copy.269), channel_id=1, source_target_pairs={{0,2},{1,3},{2,0},{3,1},{4,6},{5,7},{6,4},{7,5},{8,10},{9,11},{10,... | collective-permute-start | bytes 1486856 | tf_op jit(solution)/shard_map/ppermute | solution.py:291
  1073.6 17.7 %collective-permute-start.107 = (bf16[176,1408]{1,0:T(8,128)(2,1)}, bf16[176,1408]{1,0:T(8,128)(2,1)}, u32[]{:S(2)}, u32[]{:S(2)}) collective-permute-start(bf16[176,1408]{1,0:T(8,128)(2,1)} %add_convert_fusion.9), channel_id=1, source_target_pairs={{0,24},{1,25},{2,26},{3,27},{4,28},{5,29},{6,30},{7,31},{8,0},{9,1... | collective-permute-start | bytes 1486856 | tf_op jit(solution)/shard_map/ppermute | solution.py:291
  1073.6 21.3 %collective-permute-start.108 = (bf16[176,1408]{1,0:T(8,128)(2,1)}, bf16[176,1408]{1,0:T(8,128)(2,1)}, u32[]{:S(2)}, u32[]{:S(2)}) collective-permute-start(bf16[176,1408]{1,0:T(8,128)(2,1)} %pad_maximum_fusion.36), channel_id=1, source_target_pairs={{0,4},{1,5},{2,6},{3,7},{4,0},{5,1},{6,2},{7,3},{8,12},{9,13},{10,... | collective-permute-start | bytes 1486856 | tf_op jit(solution)/shard_map/ppermute | solution.py:291
  1076.9 18.1 %collective-permute-start.109 = (bf16[176,1408]{1,0:T(8,128)(2,1)}, bf16[176,1408]{1,0:T(8,128)(2,1)S(1)}, u32[]{:S(2)}, u32[]{:S(2)}) collective-permute-start(bf16[176,1408]{1,0:T(8,128)(2,1)} %copy.272), channel_id=1, source_target_pairs={{0,2},{1,3},{2,0},{3,1},{4,6},{5,7},{6,4},{7,5},{8,10},{9,11},{10,... | collective-permute-start | bytes 1486856 | tf_op jit(solution)/shard_map/ppermute | solution.py:291
  1083.9 65.9 %collective-permute-start.83 = (bf16[256,1408]{1,0:T(8,128)(2,1)}, bf16[256,1408]{1,0:T(8,128)(2,1)}, u32[]{:S(2)}, u32[]{:S(2)}) collective-permute-start(bf16[256,1408]{1,0:T(8,128)(2,1)} %get-tuple-element.547), channel_id=1, source_target_pairs={{0,2},{1,3},{2,0},{3,1},{4,6},{5,7},{6,4},{7,5},{8,10},{9,11},{10,... | collective-permute-start | bytes 2162696 | tf_op jit(solution)/shard_map/ppermute | solution.py:291
  1087.2 66.2 %collective-permute-start.82 = (bf16[256,1408]{1,0:T(8,128)(2,1)}, bf16[256,1408]{1,0:T(8,128)(2,1)}, u32[]{:S(2)}, u32[]{:S(2)}) collective-permute-start(bf16[256,1408]{1,0:T(8,128)(2,1)} %get-tuple-element.548), channel_id=1, source_target_pairs={{0,2},{1,3},{2,0},{3,1},{4,6},{5,7},{6,4},{7,5},{8,10},{9,11},{10,... | collective-permute-start | bytes 2162696 | tf_op jit(solution)/shard_map/ppermute | solution.py:291
  (288 other events, 3329.3 us)

commit v3 on v2

--- a/solution.py
+++ b/solution.py
@@ -528,31 +528,41 @@
     )(tokens, grads, mats)
 
 
-def wgrad_kernel(left_ref, right_ref, out_ref, turned_ref):
-    @pl.when(pl.program_id(0) == 0)
-    def _():
-        for at in range(0, left_ref.shape[1], LANES):
-            turned_ref[at : at + LANES] = left_ref[:, at : at + LANES].T
-
-    out_ref[...] = jnp.dot(turned_ref[...], right_ref[...], preferred_element_type=F32).astype(BF16)
-
-
-def wgrad(left, right):
+def wgrad_kernel(half, left_ref, right_ref, next_left_ref, next_right_ref, out_ref, turned_ref):
+    def part(place, left, right):
+        @pl.when(pl.program_id(0) == place)
+        def _():
+            for at in range(0, left.shape[1], LANES):
+                turned_ref[at : at + LANES] = left[:, at : at + LANES].T
+
+        @pl.when((pl.program_id(0) >= place) & (pl.program_id(0) < place + half))
+        def _():
+            product = jnp.dot(turned_ref[...], right[...], preferred_element_type=F32)
+            out_ref[...] = product.astype(BF16)
+
+    part(0, left_ref, right_ref)
+    part(half, next_left_ref, next_right_ref)
+
+
+def wgrad_pair(left, right, next_left, next_right):
     (count, rows), columns = left.shape, right.shape[1]
-    block = 512 if columns % 512 == 0 else columns
+    block = 512
+    half = columns // block
     return pl.pallas_call(
-        wgrad_kernel,
-        grid=(columns // block,),
+        partial(wgrad_kernel, half),
+        grid=(2 * half,),
         in_specs=[
             pl.BlockSpec((count, rows), lambda i: (0, 0)),
-            pl.BlockSpec((count, block), lambda i: (0, i)),
+            pl.BlockSpec((count, block), lambda i: (0, jnp.minimum(i, half - 1))),
+            pl.BlockSpec((count, rows), lambda i: (0, 0)),
+            pl.BlockSpec((count, block), lambda i: (0, jnp.maximum(i - half, 0))),
         ],
         out_specs=pl.BlockSpec((rows, block), lambda i: (0, i)),
-        out_shape=jax.ShapeDtypeStruct((rows, columns), BF16),
+        out_shape=jax.ShapeDtypeStruct((rows, 2 * columns), BF16),
         scratch_shapes=[pltpu.VMEM((rows, count), BF16)],
         compiler_params=pltpu.CompilerParams(vmem_limit_bytes=VMEM_LIMIT),
         cost_estimate=pl.CostEstimate(flops=0, bytes_accessed=0, transcendentals=0),
-    )(left, right)
+    )(left, right, next_left, next_right)
 
 
 def add_low(left, right, dtype=BF16):
@@ -700,12 +710,12 @@
     shift = lax.dynamic_slice_in_dim(shifts, my_latent, 1, 0)
     order.run(skip_job)
     order.run(skip_job, since=(steps,))
-    order.run(skip_job)
-    order.run(skip_job, since=(shifts,))
+    order.run(skip_job, self_job, since=(joined_got,))
+    order.run(skip_job, self_job, since=(shifts,))
     skip_got = skip_job.finish()
     order.run(self_job)
     skip_far = swap_core(skip_got)
-    order.run(self_job, since=(skip_far,))
+    order.run(self_job, cross_job, since=(skip_far,))
     skip_mat = place([skip_got, skip_far], [me_t % 2, 1 - me_t % 2], 1)
     skip_mat = skip_mat.reshape(2 * width, width)
 
@@ -718,14 +728,6 @@
     self_gains = jnp.pad(gain_pads[0:2], ((0, 6), (0, 0)))
     cross_gains = jnp.pad(gain_pads[2:4], ((0, 6), (0, 0)))
     text_part = lax.dynamic_index_in_dim(text_states, me_y, 0, keepdims=False)
-
-    cot_own, cot_other = mine_first(out_grad)
-    cot_pair = jnp.concatenate([cot_own, cot_other], 0).astype(BF16)
-    cot_got = swap_y(after(cot_pair, *order.came))
-    cotangent = jnp.concatenate([cot_own, cot_got[block:].astype(F32)], 0)
-    mlp_full_grad = gather_core(
-        jnp.concatenate([cot_pair[:block], cot_got[block:], cot_got[:block], cot_pair[block:]], 0)
-    )
 
     skip_gain = row_gains[0:2].reshape(-1)
     normed, normed_back = jax.vjp(norm_rows, joined16.astype(F32), skip_gain)
@@ -734,12 +736,20 @@
     order.run(self_job, cross_job, since=(hidden,))
     first_norm, first_back = jax.vjp(norm_rows, hidden, row_gains[2])
     attn16 = (first_norm + shift).astype(BF16)
-    order.run(self_job, cross_job, since=(attn16,))
-    order.run(self_job)
+    order.run(cross_job, since=(attn16,))
     self_got = self_job.finish()
     self_near = self_got[0].reshape(width, 4 * head_cols)
     self_far = self_got[1].reshape(width, 4 * head_cols)
     came = order.run(cross_job, mlp_job, since=(self_got,))
+
+    cot_own, cot_other = mine_first(out_grad)
+    cot_pair = jnp.concatenate([cot_own, cot_other], 0).astype(BF16)
+    cot_got = swap_y(after(cot_pair, self_got))
+    cotangent = jnp.concatenate([cot_own, cot_got[block:].astype(F32)], 0)
+    mlp_full_grad = gather_core(
+        jnp.concatenate([cot_pair[:block], cot_got[block:], cot_got[:block], cot_pair[block:]], 0)
+    )
+
     self_mats = [pack[:, : 3 * head_cols] for pack in (self_near, self_far)]
     self_outs = [pack[:, 3 * head_cols :] for pack in (self_near, self_far)]
     attn_full = gather_core(attn16)
@@ -748,10 +758,9 @@
     self_pres = [matmul(attn_full, self_mats[0])]
     self_kept = [attend((self_pres[0],), self_gains, tables, heads, self_places, 2 * rows)]
     coming = order.run(cross_job, mlp_job, since=self_kept[0][:1])
-    self_pres.append(matmul(after(attn_full, self_kept[0][0], *came), self_mats[1]))
+    self_pres.append(matmul(after(attn_full, self_kept[0][0], cot_got, *came), self_mats[1]))
     self_kept.append(attend((self_pres[1],), self_gains, tables, heads, self_places, 2 * rows))
     self_flat = after(self_kept[1][0], *coming)
-    order.run(cross_job, mlp_job, since=(self_flat,))
     after_self = hidden + sum_core(
         matmul_nt(self_kept[0][0], self_outs[0]) + matmul_nt(self_flat, self_outs[1])
     )
@@ -775,23 +784,25 @@
     cross_pres = (matmul(cross_kept, cross_mat), matmul(text_pad, text_mat))
     cross_places = (0, 0, 2 * head_cols)
     cross_kept_all = attend(
-        cross_pres, cross_gains, tables, 2 * heads, cross_places, text_rows
+        cross_pres, after(cross_gains, mlp_full_grad), tables, 2 * heads, cross_places, text_rows
     )
     cross_flat = cross_kept_all[0]
     after_cross = after_self + sum_core(matmul_nt(after(cross_flat, *came), cross_out))
     second_norm, second_back = jax.vjp(norm_rows, after_cross, row_gains[4])
 
     mlp16 = second_norm.astype(BF16)
+    came = order.run(mlp_job, since=(mlp16,))
     mlp_got = mlp_job.finish().reshape(width, 2 * hidden_cols)
-    mlp_kept = gather_core(jnp.concatenate([mlp16, swap_y(mlp16)], 0))
+    mlp_kept = gather_core(jnp.concatenate([mlp16, after(swap_y(mlp16), *came)], 0))
     activated16, inner_grad16, *shares = mlp_both(mlp_kept, mlp_full_grad, mlp_got)
     out_mine, in_mine, out_theirs, in_theirs = shares
 
     in_part = add_low(in_mine, swap_core(in_theirs), F32)
     in_got = swap_y(in_part[rows:].astype(BF16))
     mlp_in_grad = in_part[:rows] + in_got.astype(F32)
-    inner_wgrad = wgrad(mlp_kept, after(inner_grad16, in_part))
-    outer_wgrad = wgrad(mlp_full_grad, after(activated16, in_part))
+    mlp_wgrad = wgrad_pair(
+        mlp_kept, after(inner_grad16, in_part), mlp_full_grad, after(activated16, in_part)
+    )
 
     def put_back(values):
         got = swap_y(values[block:].astype(BF16))
@@ -802,11 +813,11 @@
         return lax.dynamic_slice_in_dim(matrix, dp_index * count, count, 0)
 
     def mlp_part(at, _):
-        return jnp.concatenate([rows_of(inner_wgrad, at, depth), rows_of(outer_wgrad, at, depth)], 1)
+        return rows_of(mlp_wgrad, at, depth)
 
     mlp_run = Reduction(plane, mlp_part)
     order = Sequence()
-    came = order.run(mlp_run, since=(inner_wgrad, outer_wgrad, in_got))
+    came = order.run(mlp_run, since=(mlp_wgrad, in_got))
     cross_res_grad, fifth_gain_grad = second_back(mlp_in_grad)
     after_cross_grad = cotangent + cross_res_grad
     cross_full_grad = gather_core(after_cross_grad.astype(BF16))
@@ -817,18 +828,22 @@
     cq_pre16, text_grad16, cross_gain_grad = attend_back(
         cross_pres, after(cross_gains, *came), tables, cross_kept_all, cross_mixed_grad, 2 * heads, cross_places
     )
-    came = order.run(mlp_run, since=(cq_pre16,))
-    out_got = swap_y(after(out_part[rows:].astype(BF16), cq_pre16))
-    result = after_cross + out_part[:rows] + out_got.astype(F32)
     text_wgrad = matmul_tn(text_pad, text_grad16).astype(BF16)
     cross_q_wgrad = matmul_tn(cross_kept, cq_pre16).astype(BF16)
 
+    cross_wgrads = []
+    for k in range(2):
+        near = slice(k * head_cols, (k + 1) * head_cols)
+        values = slice((2 + k) * head_cols, (3 + k) * head_cols)
+        top = jnp.concatenate([cross_q_wgrad[:, near], cross_out_wgrad[:, near]], 1)
+        low = jnp.concatenate([text_wgrad[:, near], text_wgrad[:, values]], 1)
+        top = top.reshape(dp_count, depth, 2 * head_cols)
+        low = low.reshape(dp_count, text_depth, 2 * head_cols)
+        cross_wgrads.append(jnp.concatenate([top, low], 1))
+    cross_wgrads = after(tuple(cross_wgrads))
+
     def cross_part(at, far):
-        near = slice(far * head_cols, (far + 1) * head_cols)
-        values = slice((2 + far) * head_cols, (3 + far) * head_cols)
-        top = [rows_of(grad[:, near], at, depth) for grad in (cross_q_wgrad, cross_out_wgrad)]
-        low = [rows_of(text_wgrad[:, columns], at, text_depth) for columns in (near, values)]
-        return jnp.concatenate([jnp.concatenate(top, 1), jnp.concatenate(low, 1)], 0)
+        return lax.dynamic_index_in_dim(cross_wgrads[far], at, 0, keepdims=False)
 
     cross_run = Reduction(space, cross_part)
     self_res_grad, fourth_gain_grad = third_back(sum_core(matmul_nt(after(cq_pre16, *coming), cross_mat)))
@@ -837,7 +852,9 @@
     attn_part = 0.0
     self_gain_grad = 0.0
     coming = order.run(mlp_run, cross_run, since=(self_full_grad,))
-    came = came + (out_got,)
+    out_got = swap_y(after(out_part[rows:].astype(BF16), self_full_grad))
+    result = after_cross + out_part[:rows] + out_got.astype(F32)
+    came = ()
     pre16 = self_full_grad
     in_wgrads, out_wgrads = [], []
     for k in range(2):
@@ -852,39 +869,37 @@
             self_places,
         )
         self_gain_grad = self_gain_grad + gain_grad
-        came, coming = coming, order.run(cross_run, since=(pre16,))
         if k == 0:
+            came = coming + (out_got,)
+            order.run(mlp_run, cross_run, since=(pre16,))
             result_got, block_out = put_back(after(result, pre16))
         attn_part = attn_part + matmul_nt(pre16, self_mats[k])
         in_wgrads.append(matmul_tn(attn_full, pre16).astype(BF16))
         out_wgrads.append(matmul_tn(self_full_grad, self_kept[k][0]).astype(BF16))
 
+    self_wgrads = after(
+        tuple(jnp.concatenate([in_wgrads[k], out_wgrads[k]], 1) for k in range(2))
+    )
+
     def self_part(at, far):
-        return jnp.concatenate(
-            [rows_of(in_wgrads[far], at, depth), rows_of(out_wgrads[far], at, depth)], 1
-        )
+        return rows_of(self_wgrads[far], at, depth)
 
     self_run = Reduction(space, self_part)
     attn_grad = sum_core(attn_part)
-    attn_grad = after(attn_grad, result_got, *came)
     hidden_norm_grad, third_gain_grad = first_back(attn_grad)
     shift_grad = jnp.sum(attn_grad, axis=0)
-    order.run(cross_run, self_run, since=(attn_part,))
-    order.run(cross_run, self_run, since=(attn_grad,))
     hidden_grad16 = (after_self_grad + hidden_norm_grad).astype(BF16)
     skip_wgrad = matmul_tn(normed16, hidden_grad16).astype(BF16)
     joined_grad, skip_gain_grad = normed_back(matmul_nt(hidden_grad16, skip_mat))
-    order.run(self_run)
 
     skip_parts = skip_wgrad.reshape(dp_count, 2, half_depth, width)
     mine = lax.dynamic_index_in_dim(skip_parts, me_t % 2, 1, keepdims=False)
     theirs = lax.dynamic_index_in_dim(skip_parts, 1 - me_t % 2, 1, keepdims=False)
     skip_parts = add_low(mine, swap_core(theirs))
     skip_run = Reduction(plane, lambda at, _: lax.dynamic_index_in_dim(skip_parts, at, 0, False), BF16)
-    order.run(self_run, skip_run)
-    order.run(self_run, skip_run)
-    order.run(skip_run)
-    order.run(skip_run)
+    order.run(cross_run, self_run, skip_run, since=(skip_parts, result_got))
+    for _ in range(4):
+        order.run(cross_run, self_run, skip_run)
     mlp_sum, cross_sum, self_sum = mlp_run.finish(), cross_run.finish(), self_run.finish()
     skip_sum = skip_run.finish()
     skip_sum = add_low(skip_sum, swap_y(skip_sum))

time: 1190 us -> 1130 us (0.950)
  waiting for transfers between devices: 327 us -> 257 us
  Pallas kernels: 267 us -> 254 us
  local copies, waits for them, and re-layouts: 143 us -> 155 us
    ppermute x128, waiting for transfers between devices: 327 us -> 257 us  [send(): return lax.ppermute(values, AXES, pairs)]
    convert_element_type x21 -> x19, other arithmetic: 34.2 us -> 44.9 us  [total(): return value.astype(dtype)]
    unnamed x451 -> x373, local copies, waits for them, and re-layouts: 32.6 us -> 37.8 us
    pallas_call x2 -> x1, Pallas kernels: 31.2 us -> 29.3 us  [wgrad_pair(): pl.pallas_call(partial(wgrad_kernel, half), grid=(2 * half,), in_specs=[p...]
  transfers between devices with their start and end apart: 128 -> 128, of which waited for: 53 -> 50; matrix products, arithmetic and copies ran while one was open for 31% -> 34% of each run, Pallas kernels for 18% -> 18%
where the time goes in v3:
time: 1130 us; the launch traced here: 1120 us
  waiting for transfers between devices  257 us (23%)
  Pallas kernels  254 us (22%)
  other arithmetic  182 us (16%)
  local copies, waits for them, and re-layouts  155 us (14%)
  starting transfers between devices  146 us (13%)
  matrix products  124 us (11%)
    ppermute x128, waiting for transfers between devices, send(): return lax.ppermute(values, AXES, pairs)  257 us
    ppermute x128, starting transfers between devices, send(): return lax.ppermute(values, AXES, pairs)  146 us
    pallas_call x3, Pallas kernels, attend_back(): pl.pallas_call(partial(attend_back_kernel, heads, *places, len(pres) == 1...  89.4 us
    pallas_call x3, Pallas kernels, attend(): pl.pallas_call(partial(attend_kernel, heads, *places, len(pres) == 1, key...  55.4 us
    pallas_call x1, Pallas kernels, mlp_both(): pl.pallas_call(partial(mlp_kernel, half), grid=(steps,), in_specs=[pl.Blo...  48.3 us
    dot_general x9, matrix products, matmul(): return jnp.dot(left, right, preferred_element_type=jnp.float32)  47.3 us
    convert_element_type x19, other arithmetic, total(): return value.astype(dtype)  44.9 us
    unnamed x373, local copies, waits for them, and re-layouts  37.8 us
  transfers between devices with their start and end apart: 128, of which 50 were waited for; matrix products, arithmetic and copies ran while one was open for 34% of the time, Pallas kernels for 18%

profile of v3, /device:TPU:0, one launch (start us, length us, event | category | flops | bytes accessed | tf_op | source)
XLA Modules:
  0.0 1123.0 jit_solution(12133509881912940207)
XLA Ops:
  52.6 15.0 %collective-permute-done.15 = f32[16,1408]{1,0:T(8,128)S(1)} collective-permute-done((f32[16,1408]{1,0:T(8,128)S(1)}, f32[16,1408]{1,0:T(8,128)S(1)}, u32[]{:S(2)}, u32[]{:S(2)}) %collective-permute-start.15) | collective-permute-done | bytes 90144 | tf_op jit(solution)/shard_map/ppermute | solution.py:291
  71.0 12.7 %collective-permute-done.6.refs_6_ = bf16[176,1408]{1,0:T(8,128)(2,1)S(1)} collective-permute-done((bf16[176,1408]{1,0:T(8,128)(2,1)}, bf16[176,1408]{1,0:T(8,128)(2,1)S(1)}, u32[]{:S(2)}, u32[]{:S(2)}) %collective-permute-start.6) | collective-permute-done | bytes 495648 | tf_op jit(solution)/shard_map/ppermute | solution.py:291
  85.1 10.4 collective-permute-done.16.refs_7_
  110.7 4.7 broadcast_select_fusion
  119.8 12.0 %collective-permute-done.20.refs_5_ = bf16[176,1408]{1,0:T(8,128)(2,1)S(1)} collective-permute-done((bf16[176,1408]{1,0:T(8,128)(2,1)S(1)}, bf16[176,1408]{1,0:T(8,128)(2,1)S(1)}, u32[]{:S(2)}, u32[]{:S(2)}) %collective-permute-start.20) | collective-permute-done | bytes 495648 | tf_op jit(solution)/shard_map/ppermute | solution.py:291
  160.0 6.3 shard_map.633
  168.2 8.5 fusion.124
  184.3 7.0 collective-permute-done.36.refs_3_
  210.4 6.9 shard_map.634
  221.8 4.9 fusion.116
  227.9 26.7 %collective-permute-done.43.refs_11_ = bf16[304,704]{1,0:T(8,128)(2,1)S(1)} collective-permute-done((bf16[304,704]{1,0:T(8,128)(2,1)}, bf16[304,704]{1,0:T(8,128)(2,1)S(1)}, u32[]{:S(2)}, u32[]{:S(2)}) %collective-permute-start.43) | collective-permute-done | bytes 428064 | tf_op jit(solution)/shard_map/ppermute | solution.py:291
  255.4 7.7 fusion.19.refs_0_
  263.1 16.8 %shard_map.635 = (bf16[1024,352]{1,0:T(8,128)(2,1)}, bf16[1024,512]{1,0:T(8,128)(2,1)}, bf16[1024,512]{1,0:T(8,128)(2,1)}, bf16[1024,512]{1,0:T(8,128)(2,1)}) custom-call(f32[1024,1056]{1,0:T(8,128)} %fusion.19.refs_0_, f32[8,128]{1,0:T(8,128)} %pad.30.refs_1_, f32[1024,128]{1,0:T(8,128)} %pad.31.refs_2_.refs_3_, f32[1024,128]{1,0:T(8,128)} %pad.32.refs_3_.refs_4_, ...), custom_call_target="tpu_custom_call" | custom-call | tf_op jit(solution)/shard_map/pallas_call | solution.py:244
  288.6 5.8 fusion.16.refs_0_
  294.4 16.4 %shard_map.636 = (bf16[1024,352]{1,0:T(8,128)(2,1)}, bf16[1024,512]{1,0:T(8,128)(2,1)}, bf16[1024,512]{1,0:T(8,128)(2,1)}, bf16[1024,512]{1,0:T(8,128)(2,1)}) custom-call(f32[1024,1056]{1,0:T(8,128)} %fusion.16.refs_0_, f32[8,128]{1,0:T(8,128)} %pad.30.refs_1_, f32[1024,128]{1,0:T(8,128)} %pad.31.refs_2_.refs_3_, f32[1024,128]{1,0:T(8,128)} %pad.32.refs_3_.refs_4_, ...), custom_call_target="tpu_custom_call" | custom-call | tf_op jit(solution)/shard_map/pallas_call | solution.py:244
  323.3 5.9 pad_maximum_fusion.8
  336.6 6.7 shard_map.637
  346.2 4.7 concatenate.156
  353.7 4.8 fusion.58.refs_1_
  362.4 5.2 constant_dynamic-update-slice_fusion.2.grad_ref.next_left_ref
  367.5 6.0 fusion.26.refs_0_
  373.6 22.1 %shard_map.638 = (bf16[1024,704]{1,0:T(8,128)(2,1)}, bf16[1024,1024]{1,0:T(8,128)(2,1)}, bf16[384,1024]{1,0:T(8,128)(2,1)}, bf16[384,1024]{1,0:T(8,128)(2,1)}) custom-call(f32[1024,704]{1,0:T(8,128)} %fusion.26.refs_0_, f32[384,1408]{1,0:T(8,128)} %fusion.58.refs_1_, f32[8,128]{1,0:T(8,128)} %pad.35.refs_2_, f32[1024,128]{1,0:T(8,128)} %pad.31.refs_2_.refs_3_, ...), custom_call_target="tpu_custom_call" | custom-call | tf_op jit(solution)/shard_map/pallas_call | solution.py:244
  395.7 4.4 fusion.24
  406.5 27.1 %collective-permute-done.58.refs_7_ = bf16[176,3072]{1,0:T(8,128)(2,1)} collective-permute-done((bf16[176,3072]{1,0:T(8,128)(2,1)}, bf16[176,3072]{1,0:T(8,128)(2,1)}, u32[]{:S(2)}, u32[]{:S(2)}) %collective-permute-start.58) | collective-permute-done | bytes 1081376 | tf_op jit(solution)/shard_map/ppermute | solution.py:291
  433.6 5.4 collective-permute-done.57
  441.0 7.3 shard_map.639
  448.3 5.6 pad_maximum_fusion.x_ref.left_ref
  453.9 48.3 %shard_map.640 = (bf16[2048,1536]{1,0:T(8,128)(2,1)}, bf16[2048,1536]{1,0:T(8,128)(2,1)}, bf16[1024,1408]{1,0:T(8,128)(2,1)}, bf16[1024,1408]{1,0:T(8,128)(2,1)}...) custom-call(bf16[2048,1408]{1,0:T(8,128)(2,1)} %pad_maximum_fusion.x_ref.left_ref, ...), custom_call_target="tpu_custom_call" | custom-call | tf_op jit(solution)/shard_map/pallas_call | solution.py:514
  502.7 5.1 collective-permute-done.60
  514.2 29.3 %shard_map.641 = bf16[1408,3072]{1,0:T(8,128)(2,1)} custom-call(bf16[2048,1408]{1,0:T(8,128)(2,1)} %pad_maximum_fusion.x_ref.left_ref, bf16[2048,1536]{1,0:T(8,128)(2,1)} %get-tuple-element.198.right_ref, bf16[2048,1408]{1,0:T(8,128)(2,1)} %constant_dynamic-update-slice_fusion.2.grad_ref.next_left_ref, bf16[2048,1536]{1,0:T(8,128)(2,1)} %get-tuple-element.200.next_right_ref), custom_call_target="tpu_custom_call" | custom-call | tf_op jit(solution)/shard_map/pallas_call | solution.py:551
  543.5 4.5 constant_dynamic-slice_fusion.7
  558.4 16.1 %collective-permute-done.64 = bf16[176,3072]{1,0:T(8,128)(2,1)} collective-permute-done((bf16[176,3072]{1,0:T(8,128)(2,1)}, bf16[176,3072]{1,0:T(8,128)(2,1)}, u32[]{:S(2)}, u32[]{:S(2)}) %collective-permute-start.64) | collective-permute-done | bytes 1081376 | tf_op jit(solution)/shard_map/ppermute | solution.py:291
  577.4 5.5 fusion.23.refs_7_
  584.4 4.2 collective-permute-start.65
  588.6 34.2 %shard_map.642 = (bf16[1024,704]{1,0:T(8,128)(2,1)}, bf16[384,1408]{1,0:T(8,128)(2,1)}, f32[8,128]{1,0:T(8,128)}) custom-call(f32[1024,704]{1,0:T(8,128)} %fusion.26.refs_0_, f32[384,1408]{1,0:T(8,128)} %fusion.58.refs_1_, f32[8,128]{1,0:T(8,128)} %pad.35.refs_2_, f32[1024,128]{1,0:T(8,128)} %pad.31.refs_2_.refs_3_, f32[1024,128]{1,0:T(8,128)} %pad.32.refs_3_.refs_4_, ...), custom_call_target="tpu_custom_call" | custom-call | tf_op jit(solution)/shard_map/pallas_call | solution.py:260
  622.8 4.7 convolution_convert_fusion.5
  629.0 4.2 convolution_convert_fusion.4
  639.6 4.1 copy.331
  643.7 4.7 fusion.25
  667.1 4.2 add_convert_fusion.3
  685.9 27.6 %shard_map.643 = (bf16[1024,1056]{1,0:T(8,128)(2,1)}, f32[8,128]{1,0:T(8,128)}) custom-call(f32[1024,1056]{1,0:T(8,128)} %fusion.19.refs_0_, f32[8,128]{1,0:T(8,128)} %pad.30.refs_1_, f32[1024,128]{1,0:T(8,128)} %pad.31.refs_2_.refs_3_, f32[1024,128]{1,0:T(8,128)} %pad.32.refs_3_.refs_4_, f32[1024,128]{1,0:T(8,128)} %pad.33.refs_4_.refs_5_, ...), custom_call_target="tpu_custom_call" | custom-call | tf_op jit(solution)/shard_map/pallas_call | solution.py:260
  713.5 4.3 convolution_convert_fusion.6
  717.8 5.3 convolution_convert_fusion.2
  731.8 4.3 convolution_convert_fusion.7
  738.2 5.2 collective-permute-done.73
  751.5 27.6 %shard_map.644 = (bf16[1024,1056]{1,0:T(8,128)(2,1)}, f32[8,128]{1,0:T(8,128)}) custom-call(f32[1024,1056]{1,0:T(8,128)} %fusion.16.refs_0_, f32[8,128]{1,0:T(8,128)} %pad.30.refs_1_, f32[1024,128]{1,0:T(8,128)} %pad.31.refs_2_.refs_3_, f32[1024,128]{1,0:T(8,128)} %pad.32.refs_3_.refs_4_, f32[1024,128]{1,0:T(8,128)} %pad.33.refs_4_.refs_5_, ...), custom_call_target="tpu_custom_call" | custom-call | tf_op jit(solution)/shard_map/pallas_call | solution.py:260
  779.1 7.4 fusion.14
  786.5 4.2 convolution_add_fusion.1
  795.7 5.1 convolution_convert_fusion.1
  837.9 6.8 fusion.10
  851.4 6.8 convolution_convert_fusion
  863.5 5.1 collective-permute-done.119
  870.0 5.5 fusion.107
  888.3 5.2 multiply_reduce_fusion.18
  894.3 4.3 fusion
  908.3 4.4 collective-permute-done.88
  919.6 6.0 collective-permute-done.91
  944.5 7.4 collective-permute-done.94
  968.5 6.1 collective-permute-done.92
  974.6 4.7 collective-permute-start.103
  985.8 4.4 collective-permute-done.103
  1021.2 15.7 %collective-permute-done.109 = bf16[176,1408]{1,0:T(8,128)(2,1)} collective-permute-done((bf16[176,1408]{1,0:T(8,128)(2,1)}, bf16[176,1408]{1,0:T(8,128)(2,1)}, u32[]{:S(2)}, u32[]{:S(2)}) %collective-permute-start.109) | collective-permute-done | bytes 495648 | tf_op jit(solution)/shard_map/ppermute | solution.py:291
  1040.9 5.2 collective-permute-done.111
  1059.0 4.6 collective-permute-done.115
  (851 shorter events, 497.4 us)
Async XLA Ops:
  2.9 27.3 %collective-permute-start.1 = (bf16[176,1408]{1,0:T(8,128)(2,1)}, bf16[176,1408]{1,0:T(8,128)(2,1)}, u32[]{:S(2)}, u32[]{:S(2)}) collective-permute-start(bf16[176,1408]{1,0:T(8,128)(2,1)} %dynamic-slice_convert_fusion.1.refs_0_), channel_id=1, source_target_pairs={{0,4},{1,5},{2,6},{3,7},{4,0},{5,1},{6,2},{7,3},{8,12},{9,13},{10,... | collective-permute-start | bytes 1486856 | tf_op jit(solution)/shard_map/ppermute | solution.py:291
  5.9 24.4 %collective-permute-start.2 = (bf16[176,1408]{1,0:T(8,128)(2,1)}, bf16[176,1408]{1,0:T(8,128)(2,1)}, u32[]{:S(2)}, u32[]{:S(2)}) collective-permute-start(bf16[176,1408]{1,0:T(8,128)(2,1)} %dynamic-slice_convert_fusion.1.refs_0_), channel_id=1, source_target_pairs={{0,8},{1,9},{2,10},{3,11},{4,12},{5,13},{6,14},{7,15},{8,16},{9,17... | collective-permute-start | bytes 1486856 | tf_op jit(solution)/shard_map/ppermute | solution.py:291
  14.4 34.3 %collective-permute-start = (bf16[256,2816]{1,0:T(8,128)(2,1)}, bf16[256,2816]{1,0:T(8,128)(2,1)}, u32[]{:S(2)}, u32[]{:S(2)}) collective-permute-start(bf16[256,2816]{1,0:T(8,128)(2,1)} %get-tuple-element.597), channel_id=1, source_target_pairs={{0,2},{1,3},{2,0},{3,1},{4,6},{5,7},{6,4},{7,5},{8,10},{9,11},{10,... | collective-permute-start | bytes 4325384 | tf_op jit(solution)/shard_map/ppermute | solution.py:291
  30.3 18.4 %collective-permute-start.3 = (bf16[176,1408]{1,0:T(8,128)(2,1)}, bf16[176,1408]{1,0:T(8,128)(2,1)}, u32[]{:S(2)}, u32[]{:S(2)}) collective-permute-start(bf16[176,1408]{1,0:T(8,128)(2,1)} %collective-permute-done.2.refs_2_), channel_id=1, source_target_pairs={{0,4},{1,5},{2,6},{3,7},{4,0},{5,1},{6,2},{7,3},{8,12},{9,13},{10,... | collective-permute-start | bytes 1486856 | tf_op jit(solution)/shard_map/ppermute | solution.py:291
  46.0 21.6 %collective-permute-start.15 = (f32[16,1408]{1,0:T(8,128)S(1)}, f32[16,1408]{1,0:T(8,128)S(1)}, u32[]{:S(2)}, u32[]{:S(2)}) collective-permute-start(f32[16,1408]{1,0:T(8,128)S(1)} %add.982), channel_id=1, source_target_pairs={{0,16},{1,17},{2,18},{3,19},{4,20},{5,21},{6,22},{7,23},{8,24},{9,... | collective-permute-start | bytes 270344 | tf_op jit(solution)/shard_map/ppermute | solution.py:291
  48.7 19.6 %collective-permute-start.7 = (bf16[176,1408]{1,0:T(8,128)(2,1)S(1)}, bf16[176,1408]{1,0:T(8,128)(2,1)S(1)}, u32[]{:S(2)}, u32[]{:S(2)}) collective-permute-start(bf16[176,1408]{1,0:T(8,128)(2,1)S(1)} %pad_maximum_fusion.32.refs_0_), channel_id=1, source_target_pairs={{0,8},{1,9},{2,10},{3,11},{4,12},{5,13},{6,14},{7,15},{8,16},{9,17... | collective-permute-start | bytes 1486856 | tf_op jit(solution)/shard_map/ppermute | solution.py:291
  49.3 19.0 %collective-permute-start.8 = (bf16[176,1408]{1,0:T(8,128)(2,1)S(1)}, bf16[176,1408]{1,0:T(8,128)(2,1)S(1)}, u32[]{:S(2)}, u32[]{:S(2)}) collective-permute-start(bf16[176,1408]{1,0:T(8,128)(2,1)S(1)} %pad_maximum_fusion.32.refs_0_), channel_id=1, source_target_pairs={{0,4},{1,5},{2,6},{3,7},{4,0},{5,1},{6,2},{7,3},{8,12},{9,13},{10,... | collective-permute-start | bytes 1486856 | tf_op jit(solution)/shard_map/ppermute | solution.py:291
  49.8 18.5 %collective-permute-start.9 = (bf16[176,1408]{1,0:T(8,128)(2,1)S(1)}, bf16[176,1408]{1,0:T(8,128)(2,1)S(1)}, u32[]{:S(2)}, u32[]{:S(2)}) collective-permute-start(bf16[176,1408]{1,0:T(8,128)(2,1)S(1)} %pad_maximum_fusion.32.refs_0_), channel_id=1, source_target_pairs={{0,2},{1,3},{2,0},{3,1},{4,6},{5,7},{6,4},{7,5},{8,10},{9,11},{10,... | collective-permute-start | bytes 1486856 | tf_op jit(solution)/shard_map/ppermute | solution.py:291
  51.4 19.7 %collective-permute-start.5 = (bf16[176,1408]{1,0:T(8,128)(2,1)}, bf16[176,1408]{1,0:T(8,128)(2,1)}, u32[]{:S(2)}, u32[]{:S(2)}) collective-permute-start(bf16[176,1408]{1,0:T(8,128)(2,1)} %collective-permute-done.4.refs_4_), channel_id=1, source_target_pairs={{0,4},{1,5},{2,6},{3,7},{4,0},{5,1},{6,2},{7,3},{8,12},{9,13},{10,... | collective-permute-start | bytes 1486856 | tf_op jit(solution)/shard_map/ppermute | solution.py:291
  99.5 51.8 %collective-permute-start.17 = (bf16[8,176,1408]{2,1,0:T(8,128)(2,1)}, bf16[8,176,1408]{2,1,0:T(8,128)(2,1)}, u32[]{:S(2)}, u32[]{:S(2)}) collective-permute-start(bf16[8,176,1408]{2,1,0:T(8,128)(2,1)} %shard_map.632.refs_0_), channel_id=1, source_target_pairs={{0,1},{1,0},{2,3},{3,2},{4,5},{5,4},{6,7},{7,6},{8,9},{9,8},{10,11... | collective-permute-start | bytes 11894792 | tf_op jit(solution)/shard_map/ppermute | solution.py:291
  154.1 22.6 %collective-permute-start.29 = (bf16[304,704]{1,0:T(8,128)(2,1)S(1)}, bf16[304,704]{1,0:T(8,128)(2,1)}, u32[]{:S(2)}, u32[]{:S(2)}) collective-permute-start(bf16[304,704]{1,0:T(8,128)(2,1)S(1)} %pad_maximum_fusion.33.refs_0_), channel_id=1, source_target_pairs={{0,4},{1,5},{2,6},{3,7},{4,0},{5,1},{6,2},{7,3},{8,12},{9,13},{10,... | collective-permute-start | bytes 1284104 | tf_op jit(solution)/shard_map/ppermute | solution.py:291
  155.6 21.2 %collective-permute-start.30 = (bf16[304,704]{1,0:T(8,128)(2,1)S(1)}, bf16[304,704]{1,0:T(8,128)(2,1)}, u32[]{:S(2)}, u32[]{:S(2)}) collective-permute-start(bf16[304,704]{1,0:T(8,128)(2,1)S(1)} %pad_maximum_fusion.33.refs_0_), channel_id=1, source_target_pairs={{0,2},{1,3},{2,0},{3,1},{4,6},{5,7},{6,4},{7,5},{8,10},{9,11},{10,... | collective-permute-start | bytes 1284104 | tf_op jit(solution)/shard_map/ppermute | solution.py:291
  155.9 21.5 %collective-permute-start.27 = (bf16[176,1408]{1,0:T(8,128)(2,1)}, bf16[176,1408]{1,0:T(8,128)(2,1)}, u32[]{:S(2)}, u32[]{:S(2)}) collective-permute-start(bf16[176,1408]{1,0:T(8,128)(2,1)} %collective-permute-done.23.refs_10_), channel_id=1, source_target_pairs={{0,2},{1,3},{2,0},{3,1},{4,6},{5,7},{6,4},{7,5},{8,10},{9,11},{10,... | collective-permute-start | bytes 1486856 | tf_op jit(solution)/shard_map/ppermute | solution.py:291
  157.6 19.8 %collective-permute-start.26 = (bf16[176,1408]{1,0:T(8,128)(2,1)}, bf16[176,1408]{1,0:T(8,128)(2,1)}, u32[]{:S(2)}, u32[]{:S(2)}) collective-permute-start(bf16[176,1408]{1,0:T(8,128)(2,1)} %collective-permute-done.24.refs_9_), channel_id=1, source_target_pairs={{0,8},{1,9},{2,10},{3,11},{4,12},{5,13},{6,14},{7,15},{8,16},{9,17... | collective-permute-start | bytes 1486856 | tf_op jit(solution)/shard_map/ppermute | solution.py:291
  182.9 18.3 %collective-permute-start.32 = (bf16[176,1408]{1,0:T(8,128)(2,1)}, bf16[176,1408]{1,0:T(8,128)(2,1)S(1)}, u32[]{:S(2)}, u32[]{:S(2)}) collective-permute-start(bf16[176,1408]{1,0:T(8,128)(2,1)} %collective-permute-done.23.refs_10_), channel_id=1, source_target_pairs={{0,8},{1,9},{2,10},{3,11},{4,12},{5,13},{6,14},{7,15},{8,16},{9,17... | collective-permute-start | bytes 1486856 | tf_op jit(solution)/shard_map/ppermute | solution.py:291
  194.4 32.3 %collective-permute-start.18 = (bf16[512,1408]{1,0:T(8,128)(2,1)S(1)}, bf16[512,1408]{1,0:T(8,128)(2,1)}, u32[]{:S(2)}, u32[]{:S(2)}) collective-permute-start(bf16[512,1408]{1,0:T(8,128)(2,1)S(1)} %add_convert_fusion.1), channel_id=1, source_target_pairs={{0,1},{1,0},{2,3},{3,2},{4,5},{5,4},{6,7},{7,6},{8,9},{9,8},{10,11... | collective-permute-start | bytes 4325384 | tf_op jit(solution)/shard_map/ppermute | solution.py:291
  217.3 68.5 %collective-permute-start.34 = (bf16[512,1408]{1,0:T(8,128)(2,1)}, bf16[512,1408]{1,0:T(8,128)(2,1)}, u32[]{:S(2)}, u32[]{:S(2)}) collective-permute-start(bf16[512,1408]{1,0:T(8,128)(2,1)} %pad_maximum_fusion.22), channel_id=1, source_target_pairs={{0,2},{1,3},{2,0},{3,1},{4,6},{5,7},{6,4},{7,5},{8,10},{9,11},{10,... | collective-permute-start | bytes 4325384 | tf_op jit(solution)/shard_map/ppermute | solution.py:291
  219.1 60.9 %collective-permute-start.44 = (bf16[176,3072]{1,0:T(8,128)(2,1)S(1)}, bf16[176,3072]{1,0:T(8,128)(2,1)}, u32[]{:S(2)}, u32[]{:S(2)}) collective-permute-start(bf16[176,3072]{1,0:T(8,128)(2,1)S(1)} %pad_maximum_fusion.27.refs_0_), channel_id=1, source_target_pairs={{0,8},{1,9},{2,10},{3,11},{4,12},{5,13},{6,14},{7,15},{8,16},{9,17... | collective-permute-start | bytes 3244040 | tf_op jit(solution)/shard_map/ppermute | solution.py:291
  220.3 59.7 %collective-permute-start.45 = (bf16[176,3072]{1,0:T(8,128)(2,1)S(1)}, bf16[176,3072]{1,0:T(8,128)(2,1)}, u32[]{:S(2)}, u32[]{:S(2)}) collective-permute-start(bf16[176,3072]{1,0:T(8,128)(2,1)S(1)} %pad_maximum_fusion.27.refs_0_), channel_id=1, source_target_pairs={{0,4},{1,5},{2,6},{3,7},{4,0},{5,1},{6,2},{7,3},{8,12},{9,13},{10,... | collective-permute-start | bytes 3244040 | tf_op jit(solution)/shard_map/ppermute | solution.py:291
  221.7 32.9 %collective-permute-start.43 = (bf16[304,704]{1,0:T(8,128)(2,1)}, bf16[304,704]{1,0:T(8,128)(2,1)S(1)}, u32[]{:S(2)}, u32[]{:S(2)}) collective-permute-start(bf16[304,704]{1,0:T(8,128)(2,1)} %collective-permute-done.40.refs_10_), channel_id=1, source_target_pairs={{0,2},{1,3},{2,0},{3,1},{4,6},{5,7},{6,4},{7,5},{8,10},{9,11},{10,... | collective-permute-start | bytes 1284104 | tf_op jit(solution)/shard_map/ppermute | solution.py:291
  226.7 53.2 %collective-permute-start.42 = (bf16[304,704]{1,0:T(8,128)(2,1)}, bf16[304,704]{1,0:T(8,128)(2,1)}, u32[]{:S(2)}, u32[]{:S(2)}) collective-permute-start(bf16[304,704]{1,0:T(8,128)(2,1)} %collective-permute-done.28.refs_4_), channel_id=1, source_target_pairs={{0,4},{1,5},{2,6},{3,7},{4,0},{5,1},{6,2},{7,3},{8,12},{9,13},{10,... | collective-permute-start | bytes 1284104 | tf_op jit(solution)/shard_map/ppermute | solution.py:291
  254.6 25.3 %collective-permute-start.41 = (bf16[304,704]{1,0:T(8,128)(2,1)S(1)}, bf16[304,704]{1,0:T(8,128)(2,1)}, u32[]{:S(2)}, u32[]{:S(2)}) collective-permute-start(bf16[304,704]{1,0:T(8,128)(2,1)S(1)} %collective-permute-done.38.refs_9_), channel_id=1, source_target_pairs={{0,8},{1,9},{2,10},{3,11},{4,12},{5,13},{6,14},{7,15},{8,16},{9,17... | collective-permute-start | bytes 1284104 | tf_op jit(solution)/shard_map/ppermute | solution.py:291
  280.0 32.9 %collective-permute-start.49 = (bf16[176,3072]{1,0:T(8,128)(2,1)}, bf16[176,3072]{1,0:T(8,128)(2,1)S(1)}, u32[]{:S(2)}, u32[]{:S(2)}) collective-permute-start(bf16[176,3072]{1,0:T(8,128)(2,1)} %collective-permute-done.44.refs_2_), channel_id=1, source_target_pairs={{0,8},{1,9},{2,10},{3,11},{4,12},{5,13},{6,14},{7,15},{8,16},{9,17... | collective-permute-start | bytes 3244040 | tf_op jit(solution)/shard_map/ppermute | solution.py:291
  281.4 31.5 %collective-permute-start.50 = (bf16[176,3072]{1,0:T(8,128)(2,1)}, bf16[176,3072]{1,0:T(8,128)(2,1)}, u32[]{:S(2)}, u32[]{:S(2)}) collective-permute-start(bf16[176,3072]{1,0:T(8,128)(2,1)} %collective-permute-done.44.refs_2_), channel_id=1, source_target_pairs={{0,4},{1,5},{2,6},{3,7},{4,0},{5,1},{6,2},{7,3},{8,12},{9,13},{10,... | collective-permute-start | bytes 3244040 | tf_op jit(solution)/shard_map/ppermute | solution.py:291
  283.7 27.1 %collective-permute-start.48 = (bf16[304,704]{1,0:T(8,128)(2,1)}, bf16[304,704]{1,0:T(8,128)(2,1)S(1)}, u32[]{:S(2)}, u32[]{:S(2)}) collective-permute-start(bf16[304,704]{1,0:T(8,128)(2,1)} %collective-permute-done.42.refs_6_), channel_id=1, source_target_pairs={{0,2},{1,3},{2,0},{3,1},{4,6},{5,7},{6,4},{7,5},{8,10},{9,11},{10,... | collective-permute-start | bytes 1284104 | tf_op jit(solution)/shard_map/ppermute | solution.py:291
  284.5 26.3 %collective-permute-start.47 = (bf16[304,704]{1,0:T(8,128)(2,1)}, bf16[304,704]{1,0:T(8,128)(2,1)S(1)}, u32[]{:S(2)}, u32[]{:S(2)}) collective-permute-start(bf16[304,704]{1,0:T(8,128)(2,1)} %collective-permute-done.41.refs_13_), channel_id=1, source_target_pairs={{0,4},{1,5},{2,6},{3,7},{4,0},{5,1},{6,2},{7,3},{8,12},{9,13},{10,... | collective-permute-start | bytes 1284104 | tf_op jit(solution)/shard_map/ppermute | solution.py:291
  285.9 27.0 %collective-permute-start.46 = (bf16[304,704]{1,0:T(8,128)(2,1)}, bf16[304,704]{1,0:T(8,128)(2,1)S(1)}, u32[]{:S(2)}, u32[]{:S(2)}) collective-permute-start(bf16[304,704]{1,0:T(8,128)(2,1)} %collective-permute-done.40.refs_10_), channel_id=1, source_target_pairs={{0,8},{1,9},{2,10},{3,11},{4,12},{5,13},{6,14},{7,15},{8,16},{9,17... | collective-permute-start | bytes 1284104 | tf_op jit(solution)/shard_map/ppermute | solution.py:291
  329.2 33.1 %collective-permute-start.53 = (bf16[1024,1408]{1,0:T(8,128)(2,1)}, bf16[1024,1408]{1,0:T(8,128)(2,1)}, u32[]{:S(2)}, u32[]{:S(2)}) collective-permute-start(bf16[1024,1408]{1,0:T(8,128)(2,1)} %pad_maximum_fusion.8), channel_id=1, source_target_pairs={{0,1},{1,0},{2,3},{3,2},{4,5},{5,4},{6,7},{7,6},{8,9},{9,8},{10,11... | collective-permute-start | bytes 8650760 | tf_op jit(solution)/shard_map/ppermute | solution.py:291
  334.2 33.3 %collective-permute-start.52 = (bf16[512,1408]{1,0:T(8,128)(2,1)}, bf16[512,1408]{1,0:T(8,128)(2,1)}, u32[]{:S(2)}, u32[]{:S(2)}) collective-permute-start(bf16[512,1408]{1,0:T(8,128)(2,1)} %multiply_convert_fusion.1), channel_id=1, source_target_pairs={{0,1},{1,0},{2,3},{3,2},{4,5},{5,4},{6,7},{7,6},{8,9},{9,8},{10,11... | collective-permute-start | bytes 4325384 | tf_op jit(solution)/shard_map/ppermute | solution.py:291
  351.0 44.7 %collective-permute-start.54 = (bf16[176,3072]{1,0:T(8,128)(2,1)}, bf16[176,3072]{1,0:T(8,128)(2,1)S(1)}, u32[]{:S(2)}, u32[]{:S(2)}) collective-permute-start(bf16[176,3072]{1,0:T(8,128)(2,1)} %copy-done.92), channel_id=1, source_target_pairs={{0,8},{1,9},{2,10},{3,11},{4,12},{5,13},{6,14},{7,15},{8,16},{9,17... | collective-permute-start | bytes 3244040 | tf_op jit(solution)/shard_map/ppermute | solution.py:291
  353.0 42.7 %collective-permute-start.55 = (bf16[176,3072]{1,0:T(8,128)(2,1)}, bf16[176,3072]{1,0:T(8,128)(2,1)}, u32[]{:S(2)}, u32[]{:S(2)}) collective-permute-start(bf16[176,3072]{1,0:T(8,128)(2,1)} %copy-done.92), channel_id=1, source_target_pairs={{0,4},{1,5},{2,6},{3,7},{4,0},{5,1},{6,2},{7,3},{8,12},{9,13},{10,... | collective-permute-start | bytes 3244040 | tf_op jit(solution)/shard_map/ppermute | solution.py:291
  405.2 33.7 %collective-permute-start.57 = (bf16[512,1408]{1,0:T(8,128)(2,1)S(1)}, bf16[512,1408]{1,0:T(8,128)(2,1)S(1)}, u32[]{:S(2)}, u32[]{:S(2)}) collective-permute-start(bf16[512,1408]{1,0:T(8,128)(2,1)S(1)} %multiply_convert_fusion), channel_id=1, source_target_pairs={{0,2},{1,3},{2,0},{3,1},{4,6},{5,7},{6,4},{7,5},{8,10},{9,11},{10,... | collective-permute-start | bytes 4325384 | tf_op jit(solution)/shard_map/ppermute | solution.py:291
  405.4 28.2 %collective-permute-start.58 = (bf16[176,3072]{1,0:T(8,128)(2,1)}, bf16[176,3072]{1,0:T(8,128)(2,1)}, u32[]{:S(2)}, u32[]{:S(2)}) collective-permute-start(bf16[176,3072]{1,0:T(8,128)(2,1)} %collective-permute-done.55.refs_5_), channel_id=1, source_target_pairs={{0,8},{1,9},{2,10},{3,11},{4,12},{5,13},{6,14},{7,15},{8,16},{9,17... | collective-permute-start | bytes 3244040 | tf_op jit(solution)/shard_map/ppermute | solution.py:291
  513.9 34.2 %collective-permute-start.61 = (bf16[512,1408]{1,0:T(8,128)(2,1)}, bf16[512,1408]{1,0:T(8,128)(2,1)}, u32[]{:S(2)}, u32[]{:S(2)}) collective-permute-start(bf16[512,1408]{1,0:T(8,128)(2,1)} %slice.456), channel_id=1, source_target_pairs={{0,2},{1,3},{2,0},{3,1},{4,6},{5,7},{6,4},{7,5},{8,10},{9,11},{10,... | collective-permute-start | bytes 4325384 | tf_op jit(solution)/shard_map/ppermute | solution.py:291
  548.1 26.4 %collective-permute-start.64 = (bf16[176,3072]{1,0:T(8,128)(2,1)}, bf16[176,3072]{1,0:T(8,128)(2,1)}, u32[]{:S(2)}, u32[]{:S(2)}) collective-permute-start(bf16[176,3072]{1,0:T(8,128)(2,1)} %get-tuple-element.201), channel_id=1, source_target_pairs={{0,24},{1,25},{2,26},{3,27},{4,28},{5,29},{6,30},{7,31},{8,0},{9,1... | collective-permute-start | bytes 3244040 | tf_op jit(solution)/shard_map/ppermute | solution.py:291
  557.8 19.6 %collective-permute-start.62 = (bf16[512,1408]{1,0:T(8,128)(2,1)}, bf16[512,1408]{1,0:T(8,128)(2,1)}, u32[]{:S(2)}, u32[]{:S(2)}) collective-permute-start(bf16[512,1408]{1,0:T(8,128)(2,1)} %get-tuple-element.539), channel_id=1, source_target_pairs={{0,1},{1,0},{2,3},{3,2},{4,5},{5,4},{6,7},{7,6},{8,9},{9,8},{10,11... | collective-permute-start | bytes 4325384 | tf_op jit(solution)/shard_map/ppermute | solution.py:291
  582.9 60.8 %collective-permute-start.66 = (bf16[176,3072]{1,0:T(8,128)(2,1)}, bf16[176,3072]{1,0:T(8,128)(2,1)}, u32[]{:S(2)}, u32[]{:S(2)}) collective-permute-start(bf16[176,3072]{1,0:T(8,128)(2,1)} %add_convert_fusion.4), channel_id=1, source_target_pairs={{0,4},{1,5},{2,6},{3,7},{4,0},{5,1},{6,2},{7,3},{8,12},{9,13},{10,... | collective-permute-start | bytes 3244040 | tf_op jit(solution)/shard_map/ppermute | solution.py:291
  584.4 59.3 %collective-permute-start.65 = (bf16[176,3072]{1,0:T(8,128)(2,1)}, bf16[176,3072]{1,0:T(8,128)(2,1)}, u32[]{:S(2)}, u32[]{:S(2)}) collective-permute-start(bf16[176,3072]{1,0:T(8,128)(2,1)} %get-tuple-element.207), channel_id=1, source_target_pairs={{0,24},{1,25},{2,26},{3,27},{4,28},{5,29},{6,30},{7,31},{8,0},{9,1... | collective-permute-start | bytes 3244040 | tf_op jit(solution)/shard_map/ppermute | solution.py:291
  675.8 62.4 %collective-permute-start.75 = (bf16[304,704]{1,0:T(8,128)(2,1)}, bf16[304,704]{1,0:T(8,128)(2,1)}, u32[]{:S(2)}, u32[]{:S(2)}) collective-permute-start(bf16[304,704]{1,0:T(8,128)(2,1)} %get-tuple-element.224), channel_id=1, source_target_pairs={{0,2},{1,3},{2,0},{3,1},{4,6},{5,7},{6,4},{7,5},{8,10},{9,11},{10,... | collective-permute-start | bytes 1284104 | tf_op jit(solution)/shard_map/ppermute | solution.py:291
  677.5 54.3 %collective-permute-start.74 = (bf16[304,704]{1,0:T(8,128)(2,1)}, bf16[304,704]{1,0:T(8,128)(2,1)}, u32[]{:S(2)}, u32[]{:S(2)}) collective-permute-start(bf16[304,704]{1,0:T(8,128)(2,1)} %get-tuple-element.223), channel_id=1, source_target_pairs={{0,4},{1,5},{2,6},{3,7},{4,0},{5,1},{6,2},{7,3},{8,12},{9,13},{10,... | collective-permute-start | bytes 1284104 | tf_op jit(solution)/shard_map/ppermute | solution.py:291
  678.2 65.1 %collective-permute-start.72 = (bf16[176,3072]{1,0:T(8,128)(2,1)}, bf16[176,3072]{1,0:T(8,128)(2,1)}, u32[]{:S(2)}, u32[]{:S(2)}) collective-permute-start(bf16[176,3072]{1,0:T(8,128)(2,1)} %get-tuple-element.218), channel_id=1, source_target_pairs={{0,4},{1,5},{2,6},{3,7},{4,0},{5,1},{6,2},{7,3},{8,12},{9,13},{10,... | collective-permute-start | bytes 3244040 | tf_op jit(solution)/shard_map/ppermute | solution.py:291
  679.5 63.9 %collective-permute-start.71 = (bf16[176,3072]{1,0:T(8,128)(2,1)}, bf16[176,3072]{1,0:T(8,128)(2,1)}, u32[]{:S(2)}, u32[]{:S(2)}) collective-permute-start(bf16[176,3072]{1,0:T(8,128)(2,1)} %add_convert_fusion.3), channel_id=1, source_target_pairs={{0,24},{1,25},{2,26},{3,27},{4,28},{5,29},{6,30},{7,31},{8,0},{9,1... | collective-permute-start | bytes 3244040 | tf_op jit(solution)/shard_map/ppermute | solution.py:291
  685.5 66.0 %collective-permute-start.69 = (bf16[512,1408]{1,0:T(8,128)(2,1)}, bf16[512,1408]{1,0:T(8,128)(2,1)}, u32[]{:S(2)}, u32[]{:S(2)}) collective-permute-start(bf16[512,1408]{1,0:T(8,128)(2,1)} %slice.455), channel_id=1, source_target_pairs={{0,2},{1,3},{2,0},{3,1},{4,6},{5,7},{6,4},{7,5},{8,10},{9,11},{10,... | collective-permute-start | bytes 4325384 | tf_op jit(solution)/shard_map/ppermute | solution.py:291
  743.3 66.9 %collective-permute-start.83 = (bf16[304,704]{1,0:T(8,128)(2,1)}, bf16[304,704]{1,0:T(8,128)(2,1)}, u32[]{:S(2)}, u32[]{:S(2)}) collective-permute-start(bf16[304,704]{1,0:T(8,128)(2,1)} %get-tuple-element.236), channel_id=1, source_target_pairs={{0,2},{1,3},{2,0},{3,1},{4,6},{5,7},{6,4},{7,5},{8,10},{9,11},{10,... | collective-permute-start | bytes 1284104 | tf_op jit(solution)/shard_map/ppermute | solution.py:291
  744.9 68.6 %collective-permute-start.81 = (bf16[304,704]{1,0:T(8,128)(2,1)}, bf16[304,704]{1,0:T(8,128)(2,1)}, u32[]{:S(2)}, u32[]{:S(2)}) collective-permute-start(bf16[304,704]{1,0:T(8,128)(2,1)} %fusion.56), channel_id=1, source_target_pairs={{0,24},{1,25},{2,26},{3,27},{4,28},{5,29},{6,30},{7,31},{8,0},{9,1... | collective-permute-start | bytes 1284104 | tf_op jit(solution)/shard_map/ppermute | solution.py:291
  747.0 69.9 %collective-permute-start.80 = (bf16[176,3072]{1,0:T(8,128)(2,1)}, bf16[176,3072]{1,0:T(8,128)(2,1)}, u32[]{:S(2)}, u32[]{:S(2)}) collective-permute-start(bf16[176,3072]{1,0:T(8,128)(2,1)} %get-tuple-element.233), channel_id=1, source_target_pairs={{0,4},{1,5},{2,6},{3,7},{4,0},{5,1},{6,2},{7,3},{8,12},{9,13},{10,... | collective-permute-start | bytes 3244040 | tf_op jit(solution)/shard_map/ppermute | solution.py:291
  751.2 65.7 %collective-permute-start.79 = (bf16[176,3072]{1,0:T(8,128)(2,1)}, bf16[176,3072]{1,0:T(8,128)(2,1)}, u32[]{:S(2)}, u32[]{:S(2)}) collective-permute-start(bf16[176,3072]{1,0:T(8,128)(2,1)} %add_convert_fusion.2), channel_id=1, source_target_pairs={{0,24},{1,25},{2,26},{3,27},{4,28},{5,29},{6,30},{7,31},{8,0},{9,1... | collective-permute-start | bytes 3244040 | tf_op jit(solution)/shard_map/ppermute | solution.py:291
  792.1 37.2 %collective-permute-start.76 = (bf16[512,1408]{1,0:T(8,128)(2,1)}, bf16[512,1408]{1,0:T(8,128)(2,1)}, u32[]{:S(2)}, u32[]{:S(2)}) collective-permute-start(bf16[512,1408]{1,0:T(8,128)(2,1)} %slice.453), channel_id=1, source_target_pairs={{0,1},{1,0},{2,3},{3,2},{4,5},{5,4},{6,7},{7,6},{8,9},{9,8},{10,11... | collective-permute-start | bytes 4325384 | tf_op jit(solution)/shard_map/ppermute | solution.py:291
  813.5 85.1 %collective-permute-start.82 = (bf16[304,704]{1,0:T(8,128)(2,1)}, bf16[304,704]{1,0:T(8,128)(2,1)}, u32[]{:S(2)}, u32[]{:S(2)}) collective-permute-start(bf16[304,704]{1,0:T(8,128)(2,1)} %get-tuple-element.235), channel_id=1, source_target_pairs={{0,4},{1,5},{2,6},{3,7},{4,0},{5,1},{6,2},{7,3},{8,12},{9,13},{10,... | collective-permute-start | bytes 1284104 | tf_op jit(solution)/shard_map/ppermute | solution.py:291
  862.6 31.7 %collective-permute-start.84 = (bf16[8,176,1408]{2,1,0:T(8,128)(2,1)}, bf16[8,176,1408]{2,1,0:T(8,128)(2,1)}, u32[]{:S(2)}, u32[]{:S(2)}) collective-permute-start(bf16[8,176,1408]{2,1,0:T(8,128)(2,1)} %dynamic-slice_bitcast_fusion), channel_id=1, source_target_pairs={{0,1},{1,0},{2,3},{3,2},{4,5},{5,4},{6,7},{7,6},{8,9},{9,8},{10,11... | collective-permute-start | bytes 11894792 | tf_op jit(solution)/shard_map/ppermute | solution.py:291
  904.9 20.7 %collective-permute-start.91 = (bf16[176,1408]{1,0:T(8,128)(2,1)}, bf16[176,1408]{1,0:T(8,128)(2,1)}, u32[]{:S(2)}, u32[]{:S(2)}) collective-permute-start(bf16[176,1408]{1,0:T(8,128)(2,1)} %get-tuple-element.243), channel_id=1, source_target_pairs={{0,24},{1,25},{2,26},{3,27},{4,28},{5,29},{6,30},{7,31},{8,0},{9,1... | collective-permute-start | bytes 1486856 | tf_op jit(solution)/shard_map/ppermute | solution.py:291
  906.9 20.8 %collective-permute-start.85 = (bf16[176,1408]{1,0:T(8,128)(2,1)}, bf16[176,1408]{1,0:T(8,128)(2,1)S(1)}, u32[]{:S(2)}, u32[]{:S(2)}) collective-permute-start(bf16[176,1408]{1,0:T(8,128)(2,1)} %copy.337), channel_id=1, source_target_pairs={{0,2},{1,3},{2,0},{3,1},{4,6},{5,7},{6,4},{7,5},{8,10},{9,11},{10,... | collective-permute-start | bytes 1486856 | tf_op jit(solution)/shard_map/ppermute | solution.py:291
  913.4 18.2 %collective-permute-start.89 = (bf16[176,1408]{1,0:T(8,128)(2,1)}, bf16[176,1408]{1,0:T(8,128)(2,1)S(1)}, u32[]{:S(2)}, u32[]{:S(2)}) collective-permute-start(bf16[176,1408]{1,0:T(8,128)(2,1)} %get-tuple-element.241), channel_id=1, source_target_pairs={{0,24},{1,25},{2,26},{3,27},{4,28},{5,29},{6,30},{7,31},{8,0},{9,1... | collective-permute-start | bytes 1486856 | tf_op jit(solution)/shard_map/ppermute | solution.py:291
  931.6 34.6 %collective-permute-start.99 = (bf16[176,1408]{1,0:T(8,128)(2,1)}, bf16[176,1408]{1,0:T(8,128)(2,1)}, u32[]{:S(2)}, u32[]{:S(2)}) collective-permute-start(bf16[176,1408]{1,0:T(8,128)(2,1)} %fusion.37), channel_id=1, source_target_pairs={{0,4},{1,5},{2,6},{3,7},{4,0},{5,1},{6,2},{7,3},{8,12},{9,13},{10,... | collective-permute-start | bytes 1486856 | tf_op jit(solution)/shard_map/ppermute | solution.py:291
  932.9 33.3 %collective-permute-start.98 = (bf16[176,1408]{1,0:T(8,128)(2,1)}, bf16[176,1408]{1,0:T(8,128)(2,1)}, u32[]{:S(2)}, u32[]{:S(2)}) collective-permute-start(bf16[176,1408]{1,0:T(8,128)(2,1)} %get-tuple-element.250), channel_id=1, source_target_pairs={{0,24},{1,25},{2,26},{3,27},{4,28},{5,29},{6,30},{7,31},{8,0},{9,1... | collective-permute-start | bytes 1486856 | tf_op jit(solution)/shard_map/ppermute | solution.py:291
  936.9 18.7 %collective-permute-start.95 = (bf16[304,704]{1,0:T(8,128)(2,1)S(1)}, bf16[304,704]{1,0:T(8,128)(2,1)}, u32[]{:S(2)}, u32[]{:S(2)}) collective-permute-start(bf16[304,704]{1,0:T(8,128)(2,1)S(1)} %get-tuple-element.247), channel_id=1, source_target_pairs={{0,2},{1,3},{2,0},{3,1},{4,6},{5,7},{6,4},{7,5},{8,10},{9,11},{10,... | collective-permute-start | bytes 1284104 | tf_op jit(solution)/shard_map/ppermute | solution.py:291
  938.5 19.7 %collective-permute-start.93 = (bf16[304,704]{1,0:T(8,128)(2,1)}, bf16[304,704]{1,0:T(8,128)(2,1)}, u32[]{:S(2)}, u32[]{:S(2)}) collective-permute-start(bf16[304,704]{1,0:T(8,128)(2,1)} %fusion.51), channel_id=1, source_target_pairs={{0,24},{1,25},{2,26},{3,27},{4,28},{5,29},{6,30},{7,31},{8,0},{9,1... | collective-permute-start | bytes 1284104 | tf_op jit(solution)/shard_map/ppermute | solution.py:291
  983.9 20.2 %collective-permute-start.107 = (bf16[176,1408]{1,0:T(8,128)(2,1)}, bf16[176,1408]{1,0:T(8,128)(2,1)}, u32[]{:S(2)}, u32[]{:S(2)}) collective-permute-start(bf16[176,1408]{1,0:T(8,128)(2,1)} %get-tuple-element.259), channel_id=1, source_target_pairs={{0,4},{1,5},{2,6},{3,7},{4,0},{5,1},{6,2},{7,3},{8,12},{9,13},{10,... | collective-permute-start | bytes 1486856 | tf_op jit(solution)/shard_map/ppermute | solution.py:291
  984.7 20.4 %collective-permute-start.106 = (bf16[176,1408]{1,0:T(8,128)(2,1)}, bf16[176,1408]{1,0:T(8,128)(2,1)}, u32[]{:S(2)}, u32[]{:S(2)}) collective-permute-start(bf16[176,1408]{1,0:T(8,128)(2,1)} %fusion.36), channel_id=1, source_target_pairs={{0,24},{1,25},{2,26},{3,27},{4,28},{5,29},{6,30},{7,31},{8,0},{9,1... | collective-permute-start | bytes 1486856 | tf_op jit(solution)/shard_map/ppermute | solution.py:291
  1004.1 90.6 %collective-permute-start.78 = (bf16[256,1408]{1,0:T(8,128)(2,1)}, bf16[256,1408]{1,0:T(8,128)(2,1)}, u32[]{:S(2)}, u32[]{:S(2)}) collective-permute-start(bf16[256,1408]{1,0:T(8,128)(2,1)} %get-tuple-element.590), channel_id=1, source_target_pairs={{0,2},{1,3},{2,0},{3,1},{4,6},{5,7},{6,4},{7,5},{8,10},{9,11},{10,... | collective-permute-start | bytes 2162696 | tf_op jit(solution)/shard_map/ppermute | solution.py:291
  1005.1 91.7 %collective-permute-start.77 = (bf16[256,1408]{1,0:T(8,128)(2,1)}, bf16[256,1408]{1,0:T(8,128)(2,1)}, u32[]{:S(2)}, u32[]{:S(2)}) collective-permute-start(bf16[256,1408]{1,0:T(8,128)(2,1)} %get-tuple-element.591), channel_id=1, source_target_pairs={{0,2},{1,3},{2,0},{3,1},{4,6},{5,7},{6,4},{7,5},{8,10},{9,11},{10,... | collective-permute-start | bytes 2162696 | tf_op jit(solution)/shard_map/ppermute | solution.py:291
  1009.2 31.7 %collective-permute-start.112 = (bf16[176,1408]{1,0:T(8,128)(2,1)}, bf16[176,1408]{1,0:T(8,128)(2,1)S(1)}, u32[]{:S(2)}, u32[]{:S(2)}) collective-permute-start(bf16[176,1408]{1,0:T(8,128)(2,1)} %get-tuple-element.264), channel_id=1, source_target_pairs={{0,4},{1,5},{2,6},{3,7},{4,0},{5,1},{6,2},{7,3},{8,12},{9,13},{10,... | collective-permute-start | bytes 1486856 | tf_op jit(solution)/shard_map/ppermute | solution.py:291
  1011.6 25.3 %collective-permute-start.109 = (bf16[176,1408]{1,0:T(8,128)(2,1)}, bf16[176,1408]{1,0:T(8,128)(2,1)}, u32[]{:S(2)}, u32[]{:S(2)}) collective-permute-start(bf16[176,1408]{1,0:T(8,128)(2,1)} %copy.344), channel_id=1, source_target_pairs={{0,2},{1,3},{2,0},{3,1},{4,6},{5,7},{6,4},{7,5},{8,10},{9,11},{10,... | collective-permute-start | bytes 1486856 | tf_op jit(solution)/shard_map/ppermute | solution.py:291
  1015.7 21.8 %collective-permute-start.108 = (bf16[176,1408]{1,0:T(8,128)(2,1)}, bf16[176,1408]{1,0:T(8,128)(2,1)}, u32[]{:S(2)}, u32[]{:S(2)}) collective-permute-start(bf16[176,1408]{1,0:T(8,128)(2,1)} %add_convert_fusion.10), channel_id=1, source_target_pairs={{0,24},{1,25},{2,26},{3,27},{4,28},{5,29},{6,30},{7,31},{8,0},{9,1... | collective-permute-start | bytes 1486856 | tf_op jit(solution)/shard_map/ppermute | solution.py:291
  (249 other events, 2518.4 us)
